TPU v7x, 32 devices: a whole 2x2x4 slice. The times are simulated.
32 devices in a mesh: half: 2 (over core), dp: 2 (over x), expert: 8 (over z, y).
Axes of the slice: x: 2, y: 2, z: 4, core: 2. Of those that a mesh axis runs over, the one named last changes fastest.
Arguments:
- tokens: bfloat16 [2, 32, 128, 1024], P('half', ('dp', 'expert')), may hold values from -6 to 6
- cotangent: bfloat16 [2, 32, 128, 1024], P('half', ('dp', 'expert')), may hold values from -6 to 6
- lengths: int32 [2, 32], P(None, ('dp', 'expert')), may hold values from 64 to 128
- routes: int32 [2, 32, 128, 2], P('half', ('dp', 'expert')), may hold values from 0 to 7, all different within a row
- self_qkv: bfloat16 [2, 1024, 3072], P('half'), may hold values from -0.1875 to 0.1875
- self_out: bfloat16 [2, 1024, 1024], P('half'), may hold values from -1 to 1
- cross_weights: bfloat16 [2, 1024, 2048], P('half')
- router: bfloat16 [2, 1024, 8], P('half'), may hold values from -0.125 to 0.125
- gains: float32 [2, 3, 1024], P('half'), may hold values from 0.5 to 1.5
- bias_table: float32 [2, 512], P('half'), may hold values from -4 to 4
- expert_in: bfloat16 [2, 8, 2, 1024, 2816], P('half', 'expert'), may hold values from -0.1875 to 0.1875
- expert_out: bfloat16 [2, 8, 2816, 1024], P('half', 'expert'), may hold values from -0.21875 to 0.21875
Outputs:
- outputs: bfloat16 [2, 32, 128, 1024], P('half', ('dp', 'expert'))
- d_tokens: bfloat16 [2, 32, 128, 1024], P('half', ('dp', 'expert'))
- d_self_qkv: float32 [2, 1024, 3072], P('half', ('dp', 'expert'))
- d_self_out: float32 [2, 1024, 1024], P('half', ('dp', 'expert'))
- d_cross: float32 [2, 1024, 2048], P('half', ('dp', 'expert'))
- d_router: float32 [2, 1024, 8], P('half', ('dp', 'expert'))
- d_gains: float32 [2, 3, 1024], P('half', None, ('dp', 'expert'))
- d_bias_table: float32 [2, 512], P('half', ('dp', 'expert'))
- d_expert_in: float32 [2, 8, 2, 1024, 2816], P('half', 'expert', None, None, 'dp')
- d_expert_out: float32 [2, 8, 2816, 1024], P('half', 'expert', 'dp')
- counts: int32 [2, 2, 8], P('half', 'dp', 'expert')
Inputs may be any that keep to these rules, and one draw needn't show every extreme that they name: `routes`: the 2 experts of a token differ.
All inputs are finite; a program needn't handle non-finite values.
Results may differ from a plain program's by a relative error of at most 0.023.
Values may be sent and summed in bfloat16 or wider, within the bound.
A program may use at most 640 MiB of HBM per device.

v0:
```python
import jax
import jax.numpy as jnp
from jax import lax
from jax.sharding import PartitionSpec as P

H = 16
BUCKETS = 32


EPS = 1e-06
UPPER_PRECISION = lax.Precision.HIGHEST
ENC_STEPS = (12, 16, 23, 32, 46, 64, 91)
DEC_STEPS = (19, 21, 24, 27, 31, 35, 40, 46, 52, 59, 67, 77, 87, 99, 113)


def spread_2(value, axis, source):
    kept = jnp.where(lax.axis_index(axis) == source, value, 0).astype(value.dtype)
    return lax.psum(kept, axis)


def rms(values, gain):
    return values * lax.rsqrt(jnp.mean(values * values, axis=-1, keepdims=True) + EPS) * gain


def positions(length):
    query_pos = jnp.arange(length)[:, None]
    key_pos = jnp.arange(length)[None, :]
    apart = jnp.abs(key_pos - query_pos)
    coarse = 8 + sum(((apart >= step).astype(jnp.int32) for step in ENC_STEPS))
    forward_bucket = jnp.where(apart < 8, apart, coarse) + 16 * (key_pos > query_pos).astype(
        jnp.int32
    )
    behind = jnp.maximum(query_pos - key_pos, 0)
    coarse = 16 + sum(((behind >= step).astype(jnp.int32) for step in DEC_STEPS))
    causal_bucket = jnp.where(behind < 16, behind, coarse)
    return (forward_bucket, causal_bucket)


def geglu(mixed_heads):
    return jax.nn.gelu(mixed_heads[0]) * mixed_heads[1]


def gated(flag, piece, *operands):

    def skipped(*values):
        return jax.tree.map(jnp.zeros_like, piece(*values))

    return lax.cond(flag, piece, skipped, *operands)


def gate_values(normed_rows, weights, route_hot):
    router_logits = jnp.dot(
        normed_rows, weights, precision=UPPER_PRECISION, preferred_element_type=jnp.float32
    )
    probs = jax.nn.softmax(router_logits, axis=-1)
    picked = jnp.sum(probs[:, None, :] * route_hot, axis=-1)
    return picked / jnp.sum(picked, axis=-1, keepdims=True)


def attend(query_rows, key_rows, values, bias, allowed):
    scores = (
        jnp.einsum("qhd,khd->hqk", query_rows, key_rows, preferred_element_type=jnp.float32) * 0.125
        + bias
    )
    scores = jnp.where(allowed, scores, -1000000000.0)
    peak = jnp.max(scores, axis=-1, keepdims=True)
    spread = jnp.exp(scores - peak)
    total = jnp.sum(spread, axis=-1, keepdims=True)
    weights = (spread / total).astype(jnp.bfloat16)
    mixed_heads = jnp.einsum("hqk,khd->qhd", weights, values, preferred_element_type=jnp.float32)
    return (
        mixed_heads.reshape(query_rows.shape[0], -1).astype(jnp.bfloat16),
        (peak + jnp.log(total))[..., 0],
    )


def attend_back(query_rows, key_rows, values, bias, allowed, log_total, grad_mixed):
    grad_heads = grad_mixed.reshape(query_rows.shape)
    scores = (
        jnp.einsum("qhd,khd->hqk", query_rows, key_rows, preferred_element_type=jnp.float32) * 0.125
        + bias
    )
    scores = jnp.where(allowed, scores, -1000000000.0)
    probs = jnp.exp(scores - log_total[..., None])
    grad_probs = jnp.einsum("qhd,khd->hqk", grad_heads, values, preferred_element_type=jnp.float32)
    grad_values = jnp.einsum(
        "hqk,qhd->khd", probs.astype(jnp.bfloat16), grad_heads, preferred_element_type=jnp.float32
    )
    grad_scores = probs * (grad_probs - jnp.sum(grad_probs * probs, axis=-1, keepdims=True))
    grad_scores = grad_scores.astype(jnp.bfloat16)
    grad_queries = (
        jnp.einsum("hqk,khd->qhd", grad_scores, key_rows, preferred_element_type=jnp.float32)
        * 0.125
    )
    grad_keys = (
        jnp.einsum("hqk,qhd->khd", grad_scores, query_rows, preferred_element_type=jnp.float32)
        * 0.125
    )
    return (grad_queries, grad_keys, grad_values, grad_scores)


def body(
    tokens,
    cotangent,
    lengths,
    routes,
    self_qkv,
    self_out,
    cross_weights,
    router,
    gains,
    bias_table,
    expert_in,
    expert_out,
):
    micro = tokens.shape[1]
    length = tokens.shape[2]
    width = tokens.shape[3]
    heads = H
    head_size = width // heads
    experts = router.shape[2]
    top = routes.shape[3]
    capacity = (5 * top * length + 4 * experts - 1) // (4 * experts)
    half_index = lax.axis_index("half")
    decoder = half_index == 1
    encoder = jnp.logical_not(decoder)
    query_key_value_weight = self_qkv[0]
    output_weight = self_out[0]
    w_cross = cross_weights[0]
    router_weight = router[0].astype(jnp.float32)
    gain = gains[0]
    w_in = expert_in[0, 0]
    w_down = expert_out[0, 0]
    enc_bucket, dec_bucket = positions(length)
    bucket = jnp.where(decoder, dec_bucket, enc_bucket)
    onehot = (bucket[:, :, None] == jnp.arange(BUCKETS)[None, None, :]).astype(jnp.float32)
    bias = jnp.einsum(
        "qkb,bh->hqk", onehot, bias_table[0].reshape(BUCKETS, heads), precision=UPPER_PRECISION
    )
    onehot_low = onehot.astype(jnp.bfloat16)
    query_pos = jnp.arange(length)[:, None]
    key_pos = jnp.arange(length)[None, :]
    expert_ids = jnp.arange(experts)
    slot_ids = jnp.arange(experts * capacity)

    def self_forward(values, allowed):
        normed_low = rms(values, gain[0]).astype(jnp.bfloat16)
        projected_rows = jnp.dot(
            normed_low, query_key_value_weight, preferred_element_type=jnp.float32
        ).astype(jnp.bfloat16)
        split = projected_rows.reshape(length, 3, heads, head_size)
        attended, log_total = attend(split[:, 0], split[:, 1], split[:, 2], bias, allowed)
        branch_output = jnp.dot(attended, output_weight, preferred_element_type=jnp.float32)
        return (branch_output, (normed_low, projected_rows, attended, log_total))

    def self_backward(values, saved, allowed, grad_out):
        normed_low, projected_rows, attended, log_total = saved
        grad_branch = grad_out.astype(jnp.bfloat16)
        grad_wout = jnp.einsum(
            "lf,ld->fd", attended, grad_branch, preferred_element_type=jnp.float32
        )
        grad_attended = jnp.einsum(
            "ld,fd->lf", grad_branch, output_weight, preferred_element_type=jnp.float32
        ).astype(jnp.bfloat16)
        split = projected_rows.reshape(length, 3, heads, head_size)
        grad_queries, grad_keys, grad_values, grad_scores = attend_back(
            split[:, 0], split[:, 1], split[:, 2], bias, allowed, log_total, grad_attended
        )
        grad_table = jnp.einsum(
            "hqk,qkb->bh", grad_scores, onehot_low, preferred_element_type=jnp.float32
        )
        grad_projected = (
            jnp.stack([grad_queries, grad_keys, grad_values], axis=1)
            .reshape(length, 3 * width)
            .astype(jnp.bfloat16)
        )
        grad_wqkv = jnp.einsum(
            "ld,le->de", normed_low, grad_projected, preferred_element_type=jnp.float32
        )
        grad_normed = jnp.einsum(
            "le,de->ld", grad_projected, query_key_value_weight, preferred_element_type=jnp.float32
        )
        grad_input, grad_gain = jax.vjp(rms, values, gain[0])[1](grad_normed)
        return (grad_input, grad_wqkv, grad_wout, grad_table.reshape(-1), grad_gain)

    def cross_forward(values, memory_kv, allowed):
        normed_low = rms(values, gain[2]).astype(jnp.bfloat16)
        query_rows = jnp.dot(
            normed_low, w_cross[:, :width], preferred_element_type=jnp.float32
        ).astype(jnp.bfloat16)
        pairs = memory_kv.reshape(length, 2, heads, head_size)
        attended, log_total = attend(
            query_rows.reshape(length, heads, head_size), pairs[:, 0], pairs[:, 1], 0.0, allowed
        )
        branch_output = jnp.dot(attended, w_cross[:, width:], preferred_element_type=jnp.float32)
        return (branch_output, (normed_low, query_rows, attended, log_total))

    def cross_backward(values, memory_kv, saved, allowed, grad_out):
        normed_low, query_rows, attended, log_total = saved
        grad_branch = grad_out.astype(jnp.bfloat16)
        grad_wo = jnp.einsum("lf,ld->fd", attended, grad_branch, preferred_element_type=jnp.float32)
        grad_attended = jnp.einsum(
            "ld,fd->lf", grad_branch, w_cross[:, width:], preferred_element_type=jnp.float32
        ).astype(jnp.bfloat16)
        pairs = memory_kv.reshape(length, 2, heads, head_size)
        grad_queries, grad_keys, grad_values, unused = attend_back(
            query_rows.reshape(length, heads, head_size),
            pairs[:, 0],
            pairs[:, 1],
            0.0,
            allowed,
            log_total,
            grad_attended,
        )
        grad_queries = grad_queries.reshape(length, width).astype(jnp.bfloat16)
        grad_wq = jnp.einsum(
            "ld,lf->df", normed_low, grad_queries, preferred_element_type=jnp.float32
        )
        grad_normed = jnp.einsum(
            "lf,df->ld", grad_queries, w_cross[:, :width], preferred_element_type=jnp.float32
        )
        grad_input, grad_gain = jax.vjp(rms, values, gain[2])[1](grad_normed)
        grad_memory = (
            jnp.stack([grad_keys, grad_values], axis=1)
            .reshape(length, 2 * width)
            .astype(jnp.bfloat16)
        )
        return (grad_input, jnp.concatenate([grad_wq, grad_wo], axis=1), grad_gain, grad_memory)

    def memory_forward(values):
        normed_low = rms(values, gain[2]).astype(jnp.bfloat16)
        return (
            jnp.dot(normed_low, w_cross, preferred_element_type=jnp.float32).astype(jnp.bfloat16),
            normed_low,
        )

    def memory_backward(values, normed_low, grad_memory):
        grad_weights = jnp.einsum(
            "ld,le->de", normed_low, grad_memory, preferred_element_type=jnp.float32
        )
        grad_normed = jnp.einsum(
            "le,de->ld", grad_memory, w_cross, preferred_element_type=jnp.float32
        )
        grad_input, grad_gain = jax.vjp(rms, values, gain[2])[1](grad_normed)
        return (grad_input, grad_weights, grad_gain)

    def expert_apply(flat):
        mixed_heads = jnp.einsum("rd,gdf->grf", flat, w_in, preferred_element_type=jnp.float32)
        hidden = geglu(mixed_heads).astype(jnp.bfloat16)
        return jnp.dot(hidden, w_down, preferred_element_type=jnp.float32).astype(jnp.bfloat16)

    def expert_core(flat_in, flat_grad):
        mixed_heads = jnp.einsum("rd,gdf->grf", flat_in, w_in, preferred_element_type=jnp.float32)
        active, active_back = jax.vjp(geglu, mixed_heads)
        hidden = active.astype(jnp.bfloat16)
        grad_active = jnp.einsum("rd,fd->rf", flat_grad, w_down, preferred_element_type=jnp.float32)
        grad_mixed = active_back(grad_active)[0].astype(jnp.bfloat16)
        grad_rows = jnp.einsum(
            "grf,gdf->rd", grad_mixed, w_in, preferred_element_type=jnp.float32
        ).astype(jnp.bfloat16)
        return (grad_rows, grad_mixed, hidden)

    def expert_back(flat_in, flat_grad):
        grad_rows, grad_mixed, hidden = expert_core(flat_in, flat_grad)
        grad_in = jnp.einsum("rd,grf->gdf", flat_in, grad_mixed, preferred_element_type=jnp.float32)
        grad_down = jnp.einsum("rf,rd->fd", hidden, flat_grad, preferred_element_type=jnp.float32)
        return (grad_rows, grad_in, grad_down)

    memory_in = jnp.zeros((length, 2 * width), jnp.bfloat16)
    forward_state = []
    finals = []
    kept_total = jnp.zeros((experts,), jnp.float32)
    dropped_total = jnp.zeros((experts,), jnp.float32)
    for tick in range(micro + 1):
        mine = tick - half_index
        valid = (mine >= 0) & (mine < micro)
        index = jnp.clip(mine, 0, micro - 1)
        values = tokens[0][index].astype(jnp.float32)
        enc_size = lengths[0][index]
        dec_size = lengths[1][index]
        self_allowed = jnp.where(
            decoder,
            (key_pos < dec_size) & (key_pos <= query_pos),
            (key_pos < enc_size) & (query_pos >= 0),
        )
        cross_allowed = key_pos < enc_size
        branch_output, self_saved = gated(valid, self_forward, values, self_allowed)
        first = values + branch_output
        branch_output, cross_saved = gated(
            valid & decoder, cross_forward, first, memory_in, cross_allowed
        )
        second = first + branch_output
        moe_route_rows = routes[0][index]
        moe_normed_rows = rms(second, gain[1])
        moe_normed_low = moe_normed_rows.astype(jnp.bfloat16)
        moe_route_hot = (moe_route_rows[:, :, None] == expert_ids[None, None, :]).astype(
            jnp.float32
        )
        moe_gates = gate_values(moe_normed_rows, router_weight, moe_route_hot)
        order = jnp.transpose(moe_route_rows).reshape(-1)
        picked = (order[:, None] == expert_ids[None, :]).astype(jnp.int32)
        running = jnp.cumsum(picked, axis=0)
        place = jnp.sum(running * picked, axis=1) - 1
        kept = place < capacity
        target = jnp.where(kept, order * capacity + place, -1)
        route_dispatch = (
            target.reshape(top, length)[:, :, None] == slot_ids[None, None, :]
        ).astype(jnp.bfloat16)
        kept_count = jnp.sum(picked * kept[:, None].astype(jnp.int32), axis=0)
        moe_kept_count = kept_count
        dropped_count = jnp.sum(picked, axis=0) - kept_count
        send = jnp.einsum(
            "ktc,td->cd", route_dispatch, moe_normed_low, preferred_element_type=jnp.float32
        )
        send = send.astype(jnp.bfloat16).reshape(experts, capacity, width)
        arrived = lax.all_to_all(send, "expert", split_axis=0, concat_axis=0, tiled=True)
        outcome = gated(valid, expert_apply, arrived.reshape(-1, width)).reshape(arrived.shape)
        returned = lax.all_to_all(outcome, "expert", split_axis=0, concat_axis=0, tiled=True)
        moe_rows = jnp.einsum(
            "ktc,cd->ktd",
            route_dispatch,
            returned.reshape(experts * capacity, width),
            preferred_element_type=jnp.float32,
        )
        moe_mixed_heads = jnp.sum(jnp.transpose(moe_gates)[:, :, None] * moe_rows, axis=0)
        final, moe_saved, kept_count, dropped_count = (
            second + moe_mixed_heads,
            (moe_route_hot, route_dispatch, moe_gates, moe_rows, arrived),
            moe_kept_count,
            dropped_count,
        )
        kept_total = kept_total + jnp.where(valid, kept_count, 0).astype(jnp.float32)
        dropped_total = dropped_total + jnp.where(valid, dropped_count, 0).astype(jnp.float32)
        memory_out, memory_saved = gated(valid & encoder, memory_forward, final)
        forward_state.append(
            (
                index,
                valid,
                values,
                self_allowed,
                cross_allowed,
                memory_in,
                first,
                second,
                final,
                self_saved,
                cross_saved,
                moe_saved,
                memory_saved,
            )
        )
        finals.append(final)
        memory_in = spread_2(memory_out, "half", 0)
    outputs = jnp.stack(
        [jnp.where(decoder, finals[part + 1], finals[part]) for part in range(micro)]
    )
    grad_memory_in = jnp.zeros((length, 2 * width), jnp.bfloat16)
    input_grads = []
    list_qkv, list_out, list_cross, list_router = ([], [], [], [])
    list_self_gain, list_moe_gain, list_third_gain, list_table = ([], [], [], [])
    list_in, list_down = ([], [])
    for tick in range(micro + 1):
        (
            index,
            valid,
            values,
            self_allowed,
            cross_allowed,
            memory_in,
            first,
            second,
            final,
            self_saved,
            cross_saved,
            moe_saved,
            memory_saved,
        ) = forward_state[micro - tick]
        grad_final = cotangent[0][index].astype(jnp.float32) * valid.astype(jnp.float32)
        grad_from_memory, grad_memory_weights, grad_memory_gain = gated(
            valid & encoder, memory_backward, final, memory_saved, grad_memory_in
        )
        grad_final = grad_final + grad_from_memory
        route_hot, dispatch, gates, rows, received = moe_saved
        normed_rows = rms(second, gain[1])
        grad_gates = jnp.transpose(jnp.sum(grad_final[None] * rows, axis=-1))
        gate_back = jax.vjp(gate_values, normed_rows, router_weight, route_hot)[1]
        moe_grad_normed, grad_router, moe_unused = gate_back(grad_gates)
        weighted = jnp.transpose(gates)[:, :, None] * grad_final[None]
        grad_send = jnp.einsum(
            "ktc,ktd->cd",
            dispatch.astype(jnp.float32),
            weighted,
            precision=UPPER_PRECISION,
            preferred_element_type=jnp.float32,
        )
        grad_send = grad_send.astype(jnp.bfloat16).reshape(experts, capacity, width)
        moe_arrived = lax.all_to_all(grad_send, "expert", split_axis=0, concat_axis=0, tiled=True)
        moe_flat_in = received.reshape(-1, width)
        moe_flat_grad = moe_arrived.reshape(-1, width)
        moe_grad_rows, moe_grad_in, moe_grad_down = gated(
            valid, expert_back, moe_flat_in, moe_flat_grad
        )
        moe_returned = lax.all_to_all(
            moe_grad_rows.reshape(moe_arrived.shape),
            "expert",
            split_axis=0,
            concat_axis=0,
            tiled=True,
        )
        moe_grad_normed = moe_grad_normed + jnp.einsum(
            "ktc,cd->td",
            dispatch,
            moe_returned.reshape(experts * capacity, width),
            preferred_element_type=jnp.float32,
        )
        moe_grad_input, moe_grad_gain = jax.vjp(rms, second, gain[1])[1](moe_grad_normed)
        grad_second, grad_router, grad_moe_gain, grad_in, grad_down = (
            grad_final + moe_grad_input,
            grad_router,
            moe_grad_gain,
            moe_grad_in,
            moe_grad_down,
        )
        grad_cross_part, grad_cross_weights, grad_cross_gain, grad_memory = gated(
            valid & decoder,
            cross_backward,
            first,
            memory_in,
            cross_saved,
            cross_allowed,
            grad_second,
        )
        grad_memory_in = spread_2(grad_memory, "half", 1)
        grad_first = grad_second + grad_cross_part
        grad_self_part, grad_wqkv, grad_wout, grad_table, grad_self_gain = gated(
            valid, self_backward, values, self_saved, self_allowed, grad_first
        )
        input_grads.append(grad_first + grad_self_part)
        list_qkv.append(grad_wqkv)
        list_out.append(grad_wout)
        list_cross.append(grad_memory_weights + grad_cross_weights)
        list_router.append(grad_router)
        list_self_gain.append(grad_self_gain)
        list_moe_gain.append(grad_moe_gain)
        list_third_gain.append(grad_memory_gain + grad_cross_gain)
        list_table.append(grad_table)
        list_in.append(grad_in)
        list_down.append(grad_down)
    d_tokens = jnp.stack(
        [
            jnp.where(decoder, input_grads[micro - 1 - part], input_grads[micro - part])
            for part in range(micro)
        ]
    )
    grad_gains = jnp.stack([sum(list_self_gain), sum(list_moe_gain), sum(list_third_gain)])
    tallies = jnp.concatenate([kept_total, dropped_total])
    dense = (
        lax.psum_scatter(sum(list_qkv), ("dp", "expert"), scatter_dimension=0, tiled=True),
        lax.psum_scatter(sum(list_out), ("dp", "expert"), scatter_dimension=0, tiled=True),
        lax.psum_scatter(sum(list_cross), ("dp", "expert"), scatter_dimension=0, tiled=True),
        lax.psum_scatter(sum(list_router), ("dp", "expert"), scatter_dimension=0, tiled=True),
        lax.psum_scatter(grad_gains, ("dp", "expert"), scatter_dimension=1, tiled=True),
        lax.psum_scatter(sum(list_table), ("dp", "expert"), scatter_dimension=0, tiled=True),
        lax.psum_scatter(tallies, ("dp", "expert"), scatter_dimension=0, tiled=True),
    )
    expert_grads = (
        lax.psum_scatter(
            sum(list_in).astype(jnp.bfloat16), "dp", scatter_dimension=2, tiled=True
        ).astype(jnp.float32),
        lax.psum_scatter(
            sum(list_down).astype(jnp.bfloat16), "dp", scatter_dimension=0, tiled=True
        ).astype(jnp.float32),
    )
    counts = dense[6].astype(jnp.int32).reshape(1, 1, 1)
    return (
        outputs.astype(jnp.bfloat16)[None],
        d_tokens.astype(jnp.bfloat16)[None],
        dense[0][None],
        dense[1][None],
        dense[2][None],
        dense[3][None],
        dense[4][None],
        dense[5][None],
        expert_grads[0][None, None],
        expert_grads[1][None, None],
        counts,
    )


def solution(mesh):
    placed = (
        P("half", ("dp", "expert"), None, None),
        P("half", ("dp", "expert"), None, None),
        P(None, ("dp", "expert")),
        P("half", ("dp", "expert"), None, None),
        P("half", None, None),
        P("half", None, None),
        P("half", None, None),
        P("half", None, None),
        P("half", None, None),
        P("half", None),
        P("half", "expert", None, None, None),
        P("half", "expert", None, None),
    )
    return jax.shard_map(
        body,
        mesh=mesh,
        in_specs=placed,
        out_specs=(
            P("half", ("dp", "expert"), None, None),
            P("half", ("dp", "expert"), None, None),
            P("half", ("dp", "expert"), None),
            P("half", ("dp", "expert"), None),
            P("half", ("dp", "expert"), None),
            P("half", ("dp", "expert"), None),
            P("half", None, ("dp", "expert")),
            P("half", ("dp", "expert")),
            P("half", "expert", None, None, "dp"),
            P("half", "expert", "dp", None),
            P("half", "dp", "expert"),
        ),
        check_vma=False,
    )
```

profile of v0, /device:TPU:0, one launch (start us, length us, event | category | flops | bytes accessed | tf_op | source)
XLA Modules:
  0.0 1632.4 jit_solution(10855838999542439945)
XLA Ops:
  25.8 17.2 %conditional.24 = (f32[128,1024]{1,0:T(8,128)}, bf16[128,1024]{1,0:T(8,128)(2,1)S(1)}, bf16[128,3072]{1,0:T(8,128)(2,1)}, bf16[128,1024]{0,1:T(8,128)(2,1)}, f32[16,128]{1,0:T(8,128)S(1)}) conditional(s32[]{:T(128)} %convert_element_type.687, () %tuple.192, (f32[128,1024]{1,0:T(8,128)}, f32[3,1024]{1,0:T(4,128)S(1)}, bf16[1024,3072]{1,0:T(8,128)(2,1)}, ...), branch_computations={%region_0.1_spmd, %region_1.5_spmd} | conditional | flops 1144387712 | bytes 22640736 | solution.py:48
  43.7 17.6 %conditional.25 = (f32[128,1024]{1,0:T(8,128)}, bf16[128,1024]{1,0:T(8,128)(2,1)S(1)}, bf16[128,3072]{1,0:T(8,128)(2,1)}, bf16[128,1024]{0,1:T(8,128)(2,1)}, f32[16,128]{1,0:T(8,128)S(1)}) conditional(s32[]{:T(128)} %convert_element_type.714, () %tuple.196, (f32[128,1024]{1,0:T(8,128)}, f32[3,1024]{1,0:T(4,128)S(1)}, bf16[1024,3072]{1,0:T(8,128)(2,1)}, ...), branch_computations={%region_5.6_spmd, %region_6.10_spmd} | conditional | flops 1144387712 | bytes 22640736 | solution.py:48
  79.4 16.9 %all-to-all-done = bf16[8,40,1024]{2,1,0:T(8,128)(2,1)} async-done(((bf16[8,40,1024]{2,1,0:T(8,128)(2,1)}), bf16[8,40,1024]{2,1,0:T(8,128)(2,1)}, u32[]{:S(2)}, u32[]{:S(2)}) %all-to-all-start) | async-done | bytes 655392 | tf_op jit(solution)/shard_map/all_to_all | solution.py:316
  130.2 16.5 %all-reduce.14.cloned.1.call-done = bf16[128,2048]{1,0:T(8,128)(2,1)} async-done(((bf16[128,2048]{1,0:T(8,128)(2,1)}), bf16[128,2048]{1,0:T(8,128)(2,1)}) %all-reduce.14.cloned.1.call-update) | async-done | bytes 524304 | tf_op jit(solution)/shard_map/psum | solution.py:18
  188.0 15.7 all-to-all-done.3
  211.2 17.5 %all-reduce.16.cloned.1.call-done = bf16[128,2048]{1,0:T(8,128)(2,1)} async-done(((bf16[128,2048]{1,0:T(8,128)(2,1)}), bf16[128,2048]{1,0:T(8,128)(2,1)}) %all-reduce.16.cloned.1.call-update) | async-done | bytes 524304 | tf_op jit(solution)/shard_map/psum | solution.py:18
  297.8 16.5 %conditional.37 = (bf16[320,1024]{1,0:T(8,128)(2,1)}, f32[2816,1024]{1,0:T(8,128)}, f32[2,1024,2816]{2,1,0:T(8,128)}) conditional(s32[]{:T(128)} %convert_element_type.728, () %tuple.220, (bf16[2,1024,2816]{2,1,0:T(8,128)(2,1)}, bf16[320,1024]{1,0:T(8,128)(2,1)S(1)}, bf16[8,40,1024]{2,1,0:T(8,128)(2,1)S(1)}, bf16[2816,1024]{1,0:T(8,128)(2,1)}) %tuple.556), branch_computations={%region_86.87_spmd, %region_87.88_spmd} | conditional | flops 14800322560 | bytes 270926080 | solution.py:48
  337.7 100.4 %all-reduce.18.cloned.1.call-done = bf16[128,2048]{1,0:T(8,128)(2,1)} async-done(((bf16[128,2048]{1,0:T(8,128)(2,1)}), bf16[128,2048]{1,0:T(8,128)(2,1)}) %all-reduce.18.cloned.1.call-update) | async-done | bytes 524304 | tf_op jit(solution)/shard_map/psum | solution.py:18
  468.1 68.4 %conditional.40 = (bf16[320,1024]{1,0:T(8,128)(2,1)S(1)}, f32[2816,1024]{1,0:T(8,128)}, f32[2,1024,2816]{2,1,0:T(8,128)}) conditional(s32[]{:T(128)} %convert_element_type.687, () %tuple.224, (bf16[2,1024,2816]{2,1,0:T(8,128)(2,1)}, bf16[320,1024]{1,0:T(8,128)(2,1)}, bf16[8,40,1024]{2,1,0:T(8,128)(2,1)S(1)}, ...), branch_computations={%region_105.106_spmd, %region_106.107_spmd} | conditional | flops 14800322560 | bytes 268304608 | solution.py:48
  494.8 23.3 %copy.433 = f32[2,1024,2816]{2,1,0:T(8,128)} copy(f32[2,1024,2816]{1,2,0:T(8,128)} %convolution_bitcast_fusion.8) | data formatting | bytes 46137344 | tf_op jit(solution)/shard_map/cond | solution.py:48
  562.3 40.5 %all-reduce.20.cloned.1.call-done = bf16[128,2048]{1,0:T(8,128)(2,1)} async-done(((bf16[128,2048]{1,0:T(8,128)(2,1)}), bf16[128,2048]{1,0:T(8,128)(2,1)}) %all-reduce.20.cloned.1.call-update) | async-done | bytes 524304 | tf_op jit(solution)/shard_map/psum | solution.py:18
  638.4 74.0 %conditional.44 = (bf16[320,1024]{1,0:T(8,128)(2,1)}, f32[2816,1024]{1,0:T(8,128)}, f32[2,1024,2816]{2,1,0:T(8,128)}) conditional(s32[]{:T(128)} %convert_element_type.714, () %tuple.232, (bf16[2,1024,2816]{2,1,0:T(8,128)(2,1)}, bf16[320,1024]{1,0:T(8,128)(2,1)}, bf16[8,40,1024]{2,1,0:T(8,128)(2,1)}, bf16[2816,1024]{1,0:T(8,128)(2,1)}) %tuple.558), branch_computations={%region_130.131_spmd, %region_131.132_spmd} | conditional | flops 14800322560 | bytes 236847264 | solution.py:48
  666.6 23.4 %copy.441 = f32[2,1024,2816]{2,1,0:T(8,128)} copy(f32[2,1024,2816]{1,2,0:T(8,128)} %convolution_bitcast_fusion.14) | data formatting | bytes 46137344 | tf_op jit(solution)/shard_map/cond | solution.py:48
  722.2 47.6 %conditional.42 = (f32[128,1024]{1,0:T(8,128)}, f32[1024,1024]{1,0:T(8,128)}, f32[512]{0:T(512)S(1)}, f32[1024]{0:T(1024)S(1)}, f32[1024,3072]{1,0:T(8,128)}) conditional(s32[]{:T(128)} %convert_element_type.687, () %tuple.228, (pred[128,128]{0,1:T(8,128)(4,1)}, bf16[128,3072]{1,0:T(8,128)(2,1)}, f32[16,128,128]{2,0,1:T(8,128)S(1)}, ...), branch_computations={%region_114.115_spmd, %region_115.120_spmd} | conditional | flops 2338191104 | bytes 97856776 | solution.py:48
  788.5 46.0 %conditional.46 = (f32[128,1024]{1,0:T(8,128)}, f32[1024,1024]{1,0:T(8,128)}, f32[512]{0:T(512)S(1)}, f32[1024]{0:T(1024)S(1)}, f32[1024,3072]{1,0:T(8,128)}) conditional(s32[]{:T(128)} %convert_element_type.714, () %tuple.236, (pred[128,128]{0,1:T(8,128)(4,1)S(1)}, bf16[128,3072]{1,0:T(8,128)(2,1)}, f32[16,128,128]{2,0,1:T(8,128)S(1)}, ...), branch_computations={%region_139.140_spmd, %region_140.145_spmd} | conditional | flops 2338191104 | bytes 88419512 | solution.py:48
  850.7 26.3 %add_convert_fusion.9 = bf16[2,1024,2816]{2,1,0:T(8,128)(2,1)} fusion(f32[2,1024,2816]{2,1,0:T(8,128)} %get-tuple-element.1124, f32[2,1024,2816]{2,1,0:T(8,128)} %get-tuple-element.1117, f32[2,1024,2816]{2,1,0:T(8,128)} %get-tuple-element.1120), kind=kLoop, calls=%fused_computation.537 | loop fusion | flops 17301504 | bytes 80740352 | tf_op jit(solution)/shard_map/convert_element_type | solution.py:468
  877.0 29.0 %copy.422 = bf16[2,1024,2816]{1,0,2:T(2,128)(2,1)} copy(bf16[2,1024,2816]{2,1,0:T(8,128)(2,1)} %add_convert_fusion.9) | data formatting | bytes 23068672
  927.0 23.3 %add_add_fusion.10 = f32[1024,2048]{1,0:T(8,128)} fusion(f32[1024,2048]{1,0:T(8,128)} %get-tuple-element.582, f32[1024,2048]{1,0:T(8,128)} %get-tuple-element.1125, f32[1024,2048]{1,0:T(8,128)} %get-tuple-element.580, f32[1024,2048]{1,0:T(8,128)} %get-tuple-element.1122, f32[1024,2048]{1,0:T(8,128)} %get-tuple-element.1116, f32[1024,2048]{1,0:T(8,128)} %get-tuple-element.1119), kind=kLoop, calls=%fused_computation.540 | loop fusion | flops 10485760 | bytes 58720256 | tf_op jit(solution)/shard_map/add | solution.py:460
  950.3 19.7 %add_add_fusion.9 = f32[1024,3072]{1,0:T(8,128)} fusion(f32[1024,3072]{1,0:T(8,128)} %get-tuple-element.1126, f32[1024,3072]{1,0:T(8,128)} %get-tuple-element.1127, f32[1024,3072]{1,0:T(8,128)} %get-tuple-element.1123), kind=kLoop, calls=%fused_computation.538 | loop fusion | flops 6291456 | bytes 50331648 | tf_op jit(solution)/shard_map/add | solution.py:458
  974.7 42.7 %all-reduce.8 = (f32[512]{0:T(512)S(1)}, f32[16]{0:T(128)S(1)}) all-reduce(f32[512]{0:T(512)S(1)} %add_add_fusion.18, f32[16]{0:T(128)S(1)} %pad_maximum_fusion.11), channel_id=7, replica_groups=mesh['half'=2,'dp'=2,'expert'=8] {'dp','expert'}, use_global_device_ids=true, to_apply=%region_159.160.clone | all-reduce | flops 528 | bytes 4224
  1028.9 106.5 %reduce-scatter.26.cloned.1.call-done = bf16[1408,2048]{1,0:T(8,128)(2,1)} async-done(((bf16[2816,2048]{1,0:T(8,128)(2,1)}), bf16[1408,2048]{1,0:T(8,128)(2,1)}) %reduce-scatter.26.cloned.1.call-update) | async-done | bytes 5767184
  1168.8 65.1 %reduce-scatter.16.cloned.1.call-done = f32[64,1024]{1,0:T(8,128)} async-done(((f32[1024,1024]{1,0:T(8,128)}), f32[64,1024]{1,0:T(8,128)}) %reduce-scatter.16.cloned.1.call-update) | async-done | bytes 262160 | tf_op jit(solution)/shard_map/reduce_scatter | solution.py:459
  1233.9 179.6 %reduce-scatter.18.cloned.1.call-done = f32[64,2048]{1,0:T(8,128)} async-done(((f32[1024,2048]{1,0:T(8,128)}), f32[64,2048]{1,0:T(8,128)}) %reduce-scatter.18.cloned.1.call-update) | async-done | bytes 524304 | tf_op jit(solution)/shard_map/reduce_scatter | solution.py:460
  1413.5 210.9 %reduce-scatter.14.cloned.1.call-done = f32[64,3072]{1,0:T(8,128)} async-done(((f32[1024,3072]{1,0:T(8,128)}), f32[64,3072]{1,0:T(8,128)}) %reduce-scatter.14.cloned.1.call-update) | async-done | bytes 786448 | tf_op jit(solution)/shard_map/reduce_scatter | solution.py:458
  (713 shorter events, 733.4 us)
Async XLA Ops:
  69.9 141.2 %copy-start.149 = (s32[256]{0:T(256)}, s32[256]{0:T(256)S(1)}, u32[]{:S(2)}) copy-start(s32[256]{0:T(256)S(1)} %get-tuple-element.1227) | copy-start | bytes 3076
  72.1 24.1 %all-to-all-start = ((bf16[8,40,1024]{2,1,0:T(8,128)(2,1)}), bf16[8,40,1024]{2,1,0:T(8,128)(2,1)}, u32[]{:S(2)}, u32[]{:S(2)}) async-start(bf16[8,40,1024]{2,1,0:T(8,128)(2,1)} %bitcast.204), calls=%async_computation | async-start | bytes 1310720 | tf_op jit(solution)/shard_map/all_to_all | solution.py:316
  106.7 15.3 all-to-all-start.1
  110.4 36.4 %all-reduce.14.cloned.1.call-start = ((), (), s32[]{:S(2)}) async-start(), calls=%async_computation.19 | async-start | bytes 1048576 | tf_op jit(solution)/shard_map/psum | solution.py:18
  149.7 18.3 %all-to-all-start.2 = ((bf16[8,40,1024]{2,1,0:T(8,128)(2,1)}), bf16[8,40,1024]{2,1,0:T(8,128)(2,1)}, u32[]{:S(2)}, u32[]{:S(2)}) async-start(bf16[8,40,1024]{2,1,0:T(8,128)(2,1)} %bitcast.218), calls=%async_computation.2 | async-start | bytes 1310720 | tf_op jit(solution)/shard_map/all_to_all | solution.py:316
  178.4 25.3 %all-to-all-start.3 = ((bf16[8,40,1024]{2,1,0:T(8,128)(2,1)}), bf16[8,40,1024]{2,1,0:T(8,128)(2,1)S(1)}, u32[]{:S(2)}, u32[]{:S(2)}) async-start(bf16[8,40,1024]{2,1,0:T(8,128)(2,1)} %bitcast.220), calls=%async_computation.3 | async-start | bytes 1310720 | tf_op jit(solution)/shard_map/all_to_all | solution.py:318
  186.0 42.6 %all-reduce.16.cloned.1.call-start = ((), (), s32[]{:S(2)}) async-start(), calls=%async_computation.20 | async-start | bytes 1048576 | tf_op jit(solution)/shard_map/psum | solution.py:18
  232.3 18.2 %all-to-all-start.4 = ((bf16[8,40,1024]{2,1,0:T(8,128)(2,1)}), bf16[8,40,1024]{2,1,0:T(8,128)(2,1)S(1)}, u32[]{:S(2)}, u32[]{:S(2)}) async-start(bf16[8,40,1024]{2,1,0:T(8,128)(2,1)} %bitcast.236), calls=%async_computation.4 | async-start | bytes 1310720 | tf_op jit(solution)/shard_map/all_to_all | solution.py:316
  251.9 19.4 %all-to-all-start.5 = ((bf16[8,40,1024]{2,1,0:T(8,128)(2,1)}), bf16[8,40,1024]{2,1,0:T(8,128)(2,1)S(1)}, u32[]{:S(2)}, u32[]{:S(2)}) async-start(bf16[8,40,1024]{2,1,0:T(8,128)(2,1)} %bitcast.866), calls=%async_computation.5 | async-start | bytes 1310720 | tf_op jit(solution)/shard_map/all_to_all | solution.py:318
  282.5 15.4 all-to-all-start.6
  314.3 15.5 all-to-all-start.7
  318.2 120.0 %all-reduce.18.cloned.1.call-start = ((), (), s32[]{:S(2)}) async-start(), calls=%async_computation.21 | async-start | bytes 1048576 | tf_op jit(solution)/shard_map/psum | solution.py:18
  449.8 18.2 %all-to-all-start.8 = ((bf16[8,40,1024]{2,1,0:T(8,128)(2,1)}), bf16[8,40,1024]{2,1,0:T(8,128)(2,1)S(1)}, u32[]{:S(2)}, u32[]{:S(2)}) async-start(bf16[8,40,1024]{2,1,0:T(8,128)(2,1)} %bitcast.253), calls=%async_computation.8 | async-start | bytes 1310720 | tf_op jit(solution)/shard_map/all_to_all | solution.py:397
  537.3 17.2 %all-to-all-start.9 = ((bf16[8,40,1024]{2,1,0:T(8,128)(2,1)}), bf16[8,40,1024]{2,1,0:T(8,128)(2,1)S(1)}, u32[]{:S(2)}, u32[]{:S(2)}) async-start(bf16[8,40,1024]{2,1,0:T(8,128)(2,1)} %bitcast.864), calls=%async_computation.9 | async-start | bytes 1310720 | tf_op jit(solution)/shard_map/all_to_all | solution.py:403
  541.1 61.7 %all-reduce.20.cloned.1.call-start = ((), (), s32[]{:S(2)}) async-start(), calls=%async_computation.22 | async-start | bytes 1048576 | tf_op jit(solution)/shard_map/psum | solution.py:18
  617.9 19.9 %all-to-all-start.10 = ((bf16[8,40,1024]{2,1,0:T(8,128)(2,1)}), bf16[8,40,1024]{2,1,0:T(8,128)(2,1)}, u32[]{:S(2)}, u32[]{:S(2)}) async-start(bf16[8,40,1024]{2,1,0:T(8,128)(2,1)} %bitcast.861), calls=%async_computation.10 | async-start | bytes 1310720 | tf_op jit(solution)/shard_map/all_to_all | solution.py:397
  712.5 63.0 %all-to-all-start.11 = ((bf16[8,40,1024]{2,1,0:T(8,128)(2,1)}), bf16[8,40,1024]{2,1,0:T(8,128)(2,1)}, u32[]{:S(2)}, u32[]{:S(2)}) async-start(bf16[8,40,1024]{2,1,0:T(8,128)(2,1)} %bitcast.261), calls=%async_computation.11 | async-start | bytes 1310720 | tf_op jit(solution)/shard_map/all_to_all | solution.py:403
  718.5 254.8 %reduce-scatter.22.cloned.1.call-start = ((), (), s32[]{:S(2)}) async-start(), calls=%async_computation.27 | async-start | bytes 557056
  775.4 247.0 %reduce-scatter.24.cloned.1.call-start = ((), (), s32[]{:S(2)}) async-start(), calls=%async_computation.28 | async-start | bytes 557056
  835.6 188.2 %reduce-scatter.20.cloned.1.call-start = ((), (), s32[]{:S(2)}) async-start(), calls=%async_computation.26 | async-start | bytes 8650752 | tf_op jit(solution)/shard_map/reduce_scatter | solution.py:470
  850.7 284.7 %reduce-scatter.26.cloned.1.call-start = ((), (), s32[]{:S(2)}) async-start(), calls=%async_computation.29 | async-start | bytes 17301504
  918.0 315.9 %reduce-scatter.16.cloned.1.call-start = ((), (), s32[]{:S(2)}) async-start(), calls=%async_computation.24 | async-start | bytes 4456448 | tf_op jit(solution)/shard_map/reduce_scatter | solution.py:459
  926.9 486.6 %reduce-scatter.18.cloned.1.call-start = ((), (), s32[]{:S(2)}) async-start(), calls=%async_computation.25 | async-start | bytes 8912896 | tf_op jit(solution)/shard_map/reduce_scatter | solution.py:460
  950.2 674.2 %reduce-scatter.14.cloned.1.call-start = ((), (), s32[]{:S(2)}) async-start(), calls=%async_computation.23 | async-start | bytes 13369344 | tf_op jit(solution)/shard_map/reduce_scatter | solution.py:458
  (165 other events, 4130.0 us)
Sparse Core Ops, SparseCore 0:
  128.9 17.7 all-reduce.13
  209.9 18.6 all-reduce.15
  337.8 100.2 all-reduce.17
  562.4 40.3 all-reduce.19
  775.5 77.8 reduce-scatter.21
  855.7 72.8 reduce-scatter.23
  931.5 67.7 reduce-scatter.19
  1002.2 133.1 reduce-scatter.25
  1138.4 95.4 reduce-scatter.15
  1236.7 176.7 reduce-scatter.17
  1420.7 203.7 reduce-scatter.13
where the time goes:
time: 1650 us; the launch traced here: 1630 us
  waiting for transfers between devices  863 us (52%)
  local copies, waits for them, and re-layouts  242 us (15%)
  matrix products  228 us (14%)
  other arithmetic  162 us (10%)
  starting transfers between devices  67.4 us (4%)
  blocking collectives  42.7 us (3%)
  between operations  18.6 us (1%)
    reduce_scatter x1, waiting for transfers between devices, body(): lax.psum_scatter(sum(list_qkv), ('dp', 'expert'), scatter_dimension=0, ti...  211 us
    reduce_scatter x1, waiting for transfers between devices, body(): lax.psum_scatter(sum(list_cross), ('dp', 'expert'), scatter_dimension=0,...  180 us
    psum x4, waiting for transfers between devices, spread_2(): return lax.psum(kept, axis)  175 us
    unnamed x14, waiting for transfers between devices  107 us
    unnamed x283, local copies, waits for them, and re-layouts  84.9 us
    cond x4, local copies, waits for them, and re-layouts, gated(): return lax.cond(flag, piece, skipped, *operands)  72.1 us
    reduce_scatter x1, waiting for transfers between devices, body(): lax.psum_scatter(sum(list_out), ('dp', 'expert'), scatter_dimension=0, ti...  65.1 us
    another operation x55, local copies, waits for them, and re-layouts  63.8 us
  transfers between devices with their start and end apart: 23, of which 18 were waited for; matrix products, arithmetic and copies ran while one was open for 19% of the time, Pallas kernels for 0%

commit v1 on v0

v1 whole, which is shorter than its diff:
```python
import functools

import jax
import jax.numpy as jnp
import numpy as np
from jax import lax
from jax.experimental import pallas as pl
from jax.experimental.pallas import tpu as pltpu
from jax.sharding import PartitionSpec as P

H = 16
BUCKETS = 32
EPS = 1e-06
ENC_STEPS = (12, 16, 23, 32, 46, 64, 91)
DEC_STEPS = (19, 21, 24, 27, 31, 35, 40, 46, 52, 59, 67, 77, 87, 99, 113)
F32 = jnp.float32
BF16 = jnp.bfloat16
MESH = pl.DeviceIdType.MESH
NT = (((1,), (1,)), ((), ()))
TN = (((0,), (0,)), ((), ()))


def dot(a, b, dims=(((1,), (0,)), ((), ()))):
    return lax.dot_general(a, b, dims, preferred_element_type=F32)


def diagonal_buckets(diff):
    apart = np.abs(diff)
    coarse = 8 + sum((apart >= step).astype(np.int32) for step in ENC_STEPS)
    enc = np.where(apart < 8, apart, coarse) + 16 * (diff > 0)
    behind = np.maximum(-diff, 0)
    coarse = 16 + sum((behind >= step).astype(np.int32) for step in DEC_STEPS)
    dec = np.where(behind < 16, behind, coarse)
    return enc.astype(np.int32), dec.astype(np.int32)


def masked_scores(info, seq, bias_ref, query, key_rows, head, lane_mask, length):
    part = jnp.where(lane_mask, query, jnp.zeros_like(query))
    scores = dot(part, key_rows, NT) * 0.125
    if bias_ref is not None:
        row = jnp.broadcast_to(bias_ref[pl.ds(head, 1), :], (length, 2 * length))
        scores = scores + pltpu.roll(row, 0, 1, stride=1, stride_axis=0)[:, :length]
    row_id = lax.broadcasted_iota(jnp.int32, (length, length), 0)
    col_id = lax.broadcasted_iota(jnp.int32, (length, length), 1)
    reach = jnp.where(info[2] > 0, row_id, length)
    return jnp.where((col_id < info[seq]) & (col_id <= reach), scores, -1000000000.0)


def softmax_parts(scores):
    peak = jnp.max(scores, axis=-1, keepdims=True)
    spread = jnp.exp(scores - peak)
    return spread / jnp.sum(spread, axis=-1, keepdims=True)


def attend_kernel(has_bias, info, *refs):
    bias_ref, (q_ref, k_ref, v_ref, out_ref) = (refs[0], refs[1:]) if has_bias else (None, refs)
    length, width = q_ref.shape
    seq = pl.program_id(0)
    low = lax.broadcasted_iota(jnp.int32, (length, 128), 1) < 64

    @pl.loop(0, width // 128)
    def _(pair):
        cols = pl.ds(pl.multiple_of(pair * 128, 128), 128)
        q, k, v = q_ref[:, cols], k_ref[:, cols], v_ref[:, cols]
        mixed = []
        for side in range(2):
            mask = low if side == 0 else jnp.logical_not(low)
            scores = masked_scores(info, seq, bias_ref, q, k, 2 * pair + side, mask, length)
            mixed.append(dot(softmax_parts(scores).astype(BF16), v))
        out_ref[:, cols] = jnp.where(low, mixed[0], mixed[1]).astype(BF16)


def attend_back_kernel(has_bias, info, *refs):
    if has_bias:
        bias_ref, q_ref, k_ref, v_ref, g_ref, dq_ref, dkv_ref, diag_ref = refs
    else:
        bias_ref = diag_ref = None
        q_ref, k_ref, v_ref, g_ref, dq_ref, dkv_ref = refs
    length, width = q_ref.shape
    seq = pl.program_id(0)
    low = lax.broadcasted_iota(jnp.int32, (length, 128), 1) < 64
    if has_bias:
        row_id = lax.broadcasted_iota(jnp.int32, (length, length), 0)
        col_id = lax.broadcasted_iota(jnp.int32, (length, length), 1)
        flip = (row_id + col_id == length - 1).astype(F32).astype(BF16)

        @pl.when(seq == 0)
        def _():
            diag_ref[...] = jnp.zeros_like(diag_ref)

    @pl.loop(0, width // 128)
    def _(pair):
        cols = pl.ds(pl.multiple_of(pair * 128, 128), 128)
        q, k, v, g = q_ref[:, cols], k_ref[:, cols], v_ref[:, cols], g_ref[:, cols]
        dqs, dks, dvs = [], [], []
        for side in range(2):
            mask = low if side == 0 else jnp.logical_not(low)
            head = 2 * pair + side
            probs = softmax_parts(masked_scores(info, seq, bias_ref, q, k, head, mask, length))
            part = jnp.where(mask, g, jnp.zeros_like(g))
            dweights = dot(part, v, NT)
            dvs.append(dot(probs.astype(BF16), g, TN))
            dscores = probs * (dweights - jnp.sum(dweights * probs, axis=-1, keepdims=True))
            dlow = dscores.astype(BF16)
            dqs.append(dot(dlow, k))
            dks.append(dot(dlow, q, TN))
            if has_bias:
                upside = dot(flip, dlow)
                wide = jnp.concatenate([upside, jnp.zeros((length, length), F32)], axis=1)
                turned = pltpu.roll(wide, 0, 1, stride=1, stride_axis=0)
                diag_ref[pl.ds(head, 1), :] += jnp.sum(turned, axis=0, keepdims=True)
        dq_ref[:, cols] = (jnp.where(low, dqs[0], dqs[1]) * 0.125).astype(BF16)
        dkv_ref[:, cols] = (jnp.where(low, dks[0], dks[1]) * 0.125).astype(BF16)
        vcols = pl.ds(pl.multiple_of(width + pair * 128, 128), 128)
        dkv_ref[:, vcols] = jnp.where(low, dvs[0], dvs[1]).astype(BF16)


def attend(info, bias, q, kv, blocks, length, width):
    rows = q.shape[0]
    seqs = rows // length
    specs = [
        pl.BlockSpec((length, width), lambda s, b=b: (s, b)) for b in blocks
    ]
    lead = [] if bias is None else [pl.BlockSpec(bias.shape, lambda s: (0, 0))]
    args = [] if bias is None else [bias]
    return pl.pallas_call(
        functools.partial(attend_kernel, bias is not None),
        grid=(seqs,),
        in_specs=[pl.BlockSpec(memory_space=pltpu.SMEM)] + lead + specs,
        out_specs=pl.BlockSpec((length, width), lambda s: (s, 0)),
        out_shape=jax.ShapeDtypeStruct((rows, width), BF16),
        name="attend",
    )(info, *args, q, kv, kv)


def attend_back(info, bias, q, kv, blocks, grad, length, width):
    rows = q.shape[0]
    seqs = rows // length
    specs = [
        pl.BlockSpec((length, width), lambda s, b=b: (s, b)) for b in (*blocks, 0)
    ]
    lead = [] if bias is None else [pl.BlockSpec(bias.shape, lambda s: (0, 0))]
    args = [] if bias is None else [bias]
    out_specs = [
        pl.BlockSpec((length, width), lambda s: (s, 0)),
        pl.BlockSpec((length, 2 * width), lambda s: (s, 0)),
    ]
    out_shape = [
        jax.ShapeDtypeStruct((rows, width), BF16),
        jax.ShapeDtypeStruct((rows, 2 * width), BF16),
    ]
    if bias is not None:
        out_specs.append(pl.BlockSpec(bias.shape, lambda s: (0, 0)))
        out_shape.append(jax.ShapeDtypeStruct(bias.shape, F32))
    return pl.pallas_call(
        functools.partial(attend_back_kernel, bias is not None),
        grid=(seqs,),
        in_specs=[pl.BlockSpec(memory_space=pltpu.SMEM)] + lead + specs,
        out_specs=out_specs,
        out_shape=out_shape,
        name="attend_back",
    )(info, *args, q, kv, kv, grad)


def norm_parts(values, gain):
    scale = lax.rsqrt(jnp.mean(values * values, axis=-1, keepdims=True) + EPS)
    return values * scale * gain, scale


def norm_back(values, scale, gain, grad):
    unit = values * scale
    gain_grad = jnp.sum(grad * unit, axis=0)
    pushed = grad * gain
    back = scale * (pushed - unit * jnp.mean(pushed * unit, axis=-1, keepdims=True))
    return back, gain_grad


def gelu_parts(gate):
    c = 0.7978845608028654
    inner = c * (gate + 0.044715 * gate * gate * gate)
    t = jnp.tanh(inner)
    value = 0.5 * gate * (1.0 + t)
    slope = 0.5 * (1.0 + t) + 0.5 * gate * (1.0 - t * t) * c * (1.0 + 3.0 * 0.044715 * gate * gate)
    return value, slope


def moe_forward(send, w_in, w_down, turn, kept_from):
    experts, rows, width = send.shape
    arrived = lax.all_to_all(send, "expert", split_axis=0, concat_axis=0, tiled=True)
    flat = arrived.reshape(-1, width)
    value, _ = gelu_parts(dot(flat, w_in[0]))
    hidden = (value * dot(flat, w_in[1])).astype(BF16)
    result = dot(hidden, w_down).astype(BF16).reshape(send.shape)
    back = lax.all_to_all(result, "expert", split_axis=0, concat_axis=0, tiled=True)
    if kept_from is None:
        return back, arrived
    mine = lax.axis_index("half") == turn
    return jnp.where(mine, back, kept_from[0]), jnp.where(mine, arrived, kept_from[1])


def moe_backward(grad_send, received, w_in, w_down, turn, kept_from):
    width = grad_send.shape[2]
    arrived = lax.all_to_all(grad_send, "expert", split_axis=0, concat_axis=0, tiled=True)
    flat_grad = arrived.reshape(-1, width)
    flat = received.reshape(-1, width)
    up = dot(flat, w_in[1])
    value, slope = gelu_parts(dot(flat, w_in[0]))
    hidden = (value * up).astype(BF16)
    dhidden = dot(flat_grad, w_down, NT)
    dgate = (dhidden * up * slope).astype(BF16)
    dup = (dhidden * value).astype(BF16)
    drows = (dot(dgate, w_in[0], NT) + dot(dup, w_in[1], NT)).astype(BF16)
    back = lax.all_to_all(
        drows.reshape(arrived.shape), "expert", split_axis=0, concat_axis=0, tiled=True
    )
    out = (back, dgate, dup, hidden, flat_grad)
    if kept_from is None:
        return out
    mine = lax.axis_index("half") == turn
    return tuple(jnp.where(mine, a, b) for a, b in zip(out, kept_from))


def body(
    tokens,
    cotangent,
    lengths,
    routes,
    self_qkv,
    self_out,
    cross_weights,
    router,
    gains,
    bias_table,
    expert_in,
    expert_out,
):
    _, seqs, length, width = tokens.shape
    heads = H
    experts = router.shape[2]
    top = routes.shape[3]
    capacity = (5 * top * length + 4 * experts - 1) // (4 * experts)
    block_rows = -(-seqs * capacity // 16) * 16
    rows = seqs * length
    slots = experts * block_rows
    half_index = lax.axis_index("half")
    decoder = half_index == 1
    wqkv, wout, wcross, wrouter, gain = (
        self_qkv[0],
        self_out[0],
        cross_weights[0],
        router[0],
        gains[0],
    )
    w_in, w_down = expert_in[0, 0], expert_out[0, 0]

    column = np.arange(2 * length)
    hot, hot_back = (
        (
            jnp.where(decoder, *reversed(diagonal_buckets(diff)))[:, None]
            == jnp.arange(BUCKETS)[None, :]
        ).astype(F32)
        for diff in (np.where(column < length, column, column - 2 * length), column - length + 1)
    )
    bias = lax.dot_general(
        bias_table[0].reshape(BUCKETS, heads),
        hot,
        (((0,), (1,)), ((), ())),
        precision=lax.Precision.HIGHEST,
        preferred_element_type=F32,
    )
    own_lengths = jnp.where(decoder, lengths[1], lengths[0])
    self_info = jnp.concatenate([own_lengths, half_index[None]]).astype(jnp.int32)
    cross_info = jnp.concatenate([lengths[0], jnp.zeros((1,), jnp.int32)]).astype(jnp.int32)

    order = jnp.transpose(routes[0], (0, 2, 1)).reshape(seqs, top * length)
    expert_ids = jnp.arange(experts, dtype=jnp.int32)
    picked = (order[:, :, None] == expert_ids).astype(BF16)
    earlier = np.tril(np.ones((top * length, top * length), np.float32), -1).astype(BF16)
    before = jnp.einsum("pq,sqe->spe", earlier, picked, preferred_element_type=F32)
    place = jnp.sum(before * picked.astype(F32), axis=2).astype(jnp.int32)
    kept = place < capacity
    base = order * block_rows + jnp.arange(seqs, dtype=jnp.int32)[:, None] * capacity
    target = jnp.where(kept, base + place, -1).reshape(seqs, top, length)
    target = jnp.transpose(target, (1, 0, 2)).reshape(top, rows)
    slot_ids = jnp.arange(slots, dtype=jnp.int32)
    spots = (target[:, :, None] == slot_ids).astype(BF16)
    both = jnp.sum(spots.astype(F32), axis=0).astype(BF16)
    stacked = spots.reshape(top * rows, slots)
    kept_hot = picked.astype(F32) * kept[:, :, None].astype(F32)
    kept_count = jnp.sum(kept_hot, axis=(0, 1))
    all_count = jnp.sum(picked.astype(F32), axis=(0, 1))
    tallies = jnp.concatenate([kept_count, all_count - kept_count])
    route_hot = (routes[0].reshape(rows, top, 1) == expert_ids).astype(F32)

    def route(values):
        normed, scale = norm_parts(values, gain[1])
        low = normed.astype(BF16)
        rest = (normed - low.astype(F32)).astype(BF16)
        logits = dot(low, wrouter) + dot(rest, wrouter)
        probs = jax.nn.softmax(logits, axis=-1)
        chosen = jnp.sum(probs[:, None, :] * route_hot, axis=-1)
        total = jnp.sum(chosen, axis=-1, keepdims=True)
        gates = chosen / total
        send = dot(both, low, TN).astype(BF16).reshape(experts, block_rows, width)
        return dict(scale=scale, low=low, probs=probs, gates=gates, total=total, send=send)

    def fetch(returned):
        flat = returned.reshape(slots, width)
        return dot(stacked, flat).reshape(top, rows, width)

    def combine(values, gates, results):
        return values + jnp.sum(jnp.transpose(gates)[:, :, None] * results, axis=0)

    values = tokens[0].reshape(rows, width).astype(F32)
    normed, scale0 = norm_parts(values, gain[0])
    low0 = normed.astype(BF16)
    qkv = dot(low0, wqkv).astype(BF16)
    mixed0 = attend(self_info, bias, qkv, qkv, (0, 1, 2), length, width)
    first = values + dot(mixed0, wout)

    state = route(first)
    returned, received = moe_forward(state["send"], w_in, w_down, 0, None)
    final_enc = combine(first, state["gates"], fetch(returned))
    normed, scale_m = norm_parts(final_enc, gain[2])
    low_m = normed.astype(BF16)
    memory = dot(low_m, wcross).astype(BF16)
    names = ("half", "dp", "expert")
    forward_pairs, back_pairs = half_pairs(lax.axis_size("dp") * lax.axis_size("expert"))
    memory = lax.ppermute(memory, names, forward_pairs)

    normed, scale_c = norm_parts(first, gain[2])
    low_c = normed.astype(BF16)
    query = dot(low_c, wcross[:, :width]).astype(BF16)
    mixed_c = attend(cross_info, None, query, memory, (0, 0, 1), length, width)
    second = jnp.where(decoder, first + dot(mixed_c, wcross[:, width:]), first)

    state = route(second)
    returned, received = moe_forward(state["send"], w_in, w_down, 1, (returned, received))
    results = fetch(returned)
    final = combine(second, state["gates"], results)
    outputs = final.astype(BF16)

    def moe_gradient(grad):
        dgates = jnp.transpose(jnp.sum(grad[None] * results, axis=-1))
        spread = (jnp.transpose(state["gates"])[:, :, None] * grad[None]).astype(BF16)
        send = dot(stacked, spread.reshape(top * rows, width), TN)
        return dgates, send.astype(BF16).reshape(experts, block_rows, width)

    def moe_input_gradient(grad, dgates, back):
        gates, total, probs = state["gates"], state["total"], state["probs"]
        dchosen = (dgates - jnp.sum(dgates * gates, axis=-1, keepdims=True)) / total
        dprobs = jnp.sum(dchosen[:, :, None] * route_hot, axis=1)
        dlogits = probs * (dprobs - jnp.sum(dprobs * probs, axis=-1, keepdims=True))
        dnormed = dot(both, back.reshape(slots, width)) + lax.dot_general(
            dlogits, wrouter.astype(F32), NT, preferred_element_type=F32
        )
        dvalues, dgain = norm_back(second, state["scale"], gain[1], dnormed)
        normed = second * state["scale"] * gain[1]
        drouter = lax.dot_general(
            normed, dlogits, TN, precision=lax.Precision.HIGHEST, preferred_element_type=F32
        )
        return grad + dvalues, dgain, drouter

    grad_dec = cotangent[0].reshape(rows, width).astype(F32)
    dgates, grad_send = moe_gradient(grad_dec)
    kept_from = moe_backward(grad_send, received, w_in, w_down, 1, None)
    grad_second, _, _ = moe_input_gradient(grad_dec, dgates, kept_from[0])

    dbranch_c = grad_second.astype(BF16)
    dmixed_c = dot(dbranch_c, wcross[:, width:], NT).astype(BF16)
    dquery, dmemory = attend_back(
        cross_info, None, query, memory, (0, 0, 1), dmixed_c, length, width
    )
    dmemory = lax.ppermute(dmemory, names, back_pairs)
    dnormed = dot(dquery, wcross[:, :width], NT)
    dvalues, dgain_c = norm_back(first, scale_c, gain[2], dnormed)
    grad_first_dec = grad_second + dvalues

    dnormed = dot(dmemory, wcross, NT)
    dvalues, dgain_m = norm_back(final_enc, scale_m, gain[2], dnormed)
    grad = jnp.where(decoder, grad_dec, grad_dec + dvalues)
    dgates, grad_send = moe_gradient(grad)
    back, dgate, dup, hidden, flat_grad = moe_backward(
        grad_send, received, w_in, w_down, 0, kept_from
    )
    grad_second, dgain_moe, drouter = moe_input_gradient(grad, dgates, back)
    grad_first = jnp.where(decoder, grad_first_dec, grad_second)

    dbranch = grad_first.astype(BF16)
    dmixed = dot(dbranch, wout, NT).astype(BF16)
    dq, dkv, diag = attend_back(self_info, bias, qkv, qkv, (0, 1, 2), dmixed, length, width)
    dnormed = dot(dq, wqkv[:, :width], NT) + dot(dkv, wqkv[:, width:], NT)
    dvalues, dgain_self = norm_back(values, scale0, gain[0], dnormed)
    d_tokens = (grad_first + dvalues).astype(BF16)
    dtable = lax.dot_general(
        hot_back, diag, (((0,), (1,)), ((), ())), precision=lax.Precision.HIGHEST,
        preferred_element_type=F32,
    ).reshape(-1)

    left = jnp.where(decoder, low_c, low_m)
    right_enc = dot(left, jnp.where(decoder, jnp.concatenate([dquery, dquery], 1), dmemory), TN)
    dcross_out = dot(mixed_c, dbranch_c, TN)
    dcross = jnp.where(
        decoder, jnp.concatenate([right_enc[:, :width], dcross_out], axis=1), right_enc
    )
    dqkv = jnp.concatenate([dot(low0, dq, TN), dot(low0, dkv, TN)], axis=1)
    dout = dot(mixed0, dbranch, TN)
    flat = received.reshape(-1, width)
    din = jnp.stack([dot(flat, dgate, TN), dot(flat, dup, TN)])
    ddown = dot(hidden, flat_grad, TN)
    dgains = jnp.stack([dgain_self, dgain_moe, jnp.where(decoder, dgain_c, dgain_m)])

    axes = ("dp", "expert")

    def scattered(array, dim, over=axes):
        return lax.psum_scatter(array, over, scatter_dimension=dim, tiled=True).astype(F32)

    counts = scattered(tallies, 0).astype(jnp.int32).reshape(1, 1, 1)
    return (
        outputs.reshape(1, seqs, length, width),
        d_tokens.reshape(1, seqs, length, width),
        scattered(dqkv.astype(BF16), 0)[None],
        scattered(dout.astype(BF16), 0)[None],
        scattered(dcross.astype(BF16), 0)[None],
        scattered(drouter, 0)[None],
        scattered(dgains, 1)[None],
        scattered(dtable, 0)[None],
        scattered(din.astype(BF16), 2, "dp")[None, None],
        scattered(ddown.astype(BF16), 0, "dp")[None, None],
        counts,
    )


def half_pairs(count):
    return (
        [(i, count + i) for i in range(count)],
        [(count + i, i) for i in range(count)],
    )


def solution(mesh):
    placed = (
        P("half", ("dp", "expert"), None, None),
        P("half", ("dp", "expert"), None, None),
        P(None, ("dp", "expert")),
        P("half", ("dp", "expert"), None, None),
        P("half", None, None),
        P("half", None, None),
        P("half", None, None),
        P("half", None, None),
        P("half", None, None),
        P("half", None),
        P("half", "expert", None, None, None),
        P("half", "expert", None, None),
    )
    return jax.shard_map(
        body,
        mesh=mesh,
        in_specs=placed,
        out_specs=(
            P("half", ("dp", "expert"), None, None),
            P("half", ("dp", "expert"), None, None),
            P("half", ("dp", "expert"), None),
            P("half", ("dp", "expert"), None),
            P("half", ("dp", "expert"), None),
            P("half", ("dp", "expert"), None),
            P("half", None, ("dp", "expert")),
            P("half", ("dp", "expert")),
            P("half", "expert", None, None, "dp"),
            P("half", "expert", "dp", None),
            P("half", "dp", "expert"),
        ),
        check_vma=False,
    )
```

time: 1650 us -> 1220 us (0.74)
  waiting for transfers between devices: 863 us -> 595 us
  local copies, waits for them, and re-layouts: 242 us -> 89.6 us
  other arithmetic: 162 us -> 55.6 us
  blocking collectives: 42.7 us -> 149 us
  Pallas kernels: 0 us -> 66.4 us
  starting transfers between devices: 67.4 us -> 27.1 us
    psum x4 -> x0, waiting for transfers between devices: 175 us -> none  [spread_2(): return lax.psum(kept, axis)]
    reduce_scatter x4, waiting for transfers between devices: 456 us -> 340 us  [scattered(): lax.psum_scatter(array, over, scatter_dimension=dim, tiled=True).astype(F32)]
    all_to_all x0 -> x3, blocking collectives: none -> 109 us  [the longest x2 73.8 us: moe_forward(): lax.all_to_all(send, 'expert', split_axis=0, concat_axis=0, tiled=True)]
    cond x66 -> x0, local copies, waits for them, and re-layouts: 79.8 us -> none  [the longest x4 72.1 us: gated(): return lax.cond(flag, piece, skipped, *operands)]
    pallas_call x0 -> x4, Pallas kernels: none -> 66.4 us  [the longest x2 38 us: attend_back(): pl.pallas_call(functools.partial(attend_back_kernel, bias is not None), g...]
    add x21 -> x1, other arithmetic: 64 us -> 0.31 us  [moe_input_gradient(): return (grad + dvalues, dgain, drouter)]
    another operation x55 -> x1, local copies, waits for them, and re-layouts: 63.8 us -> 3.94 us
    all_to_all x12 -> x5, starting transfers between devices: 66.8 us -> 22 us  [the longest x2 8.71 us: moe_backward(): lax.all_to_all(drows.reshape(arrived.shape), 'expert', split_axis=0, conc...]
  transfers between devices with their start and end apart: 23 -> 14, of which waited for: 18 -> 11; matrix products, arithmetic and copies ran while one was open for 19% -> 13% of each run, Pallas kernels for 0% -> 2%
where the time goes in v1:
time: 1220 us; the launch traced here: 1210 us
  waiting for transfers between devices  595 us (49%)
  matrix products  213 us (17%)
  blocking collectives  149 us (12%)
  local copies, waits for them, and re-layouts  89.6 us (7%)
  Pallas kernels  66.4 us (5%)
  other arithmetic  55.6 us (5%)
  starting transfers between devices  27.1 us (2%)
  between operations  17.8 us (1%)
    reduce_scatter x4, waiting for transfers between devices, scattered(): lax.psum_scatter(array, over, scatter_dimension=dim, tiled=True).astype(F32)  340 us
    dot_general x43, matrix products, dot(): return lax.dot_general(a, b, dims, preferred_element_type=F32)  206 us
    unnamed x10, waiting for transfers between devices  133 us
    unnamed x142, local copies, waits for them, and re-layouts  82.6 us
    all_to_all x2, blocking collectives, moe_forward(): lax.all_to_all(send, 'expert', split_axis=0, concat_axis=0, tiled=True)  73.8 us
    all_to_all x2, waiting for transfers between devices, moe_forward(): lax.all_to_all(result, 'expert', split_axis=0, concat_axis=0, tiled=True)  57.7 us
    all_to_all x2, waiting for transfers between devices, moe_backward(): lax.all_to_all(drows.reshape(arrived.shape), 'expert', split_axis=0, conc...  46.7 us
    unnamed x1, blocking collectives  40 us
  transfers between devices with their start and end apart: 14, of which 11 were waited for; matrix products, arithmetic and copies ran while one was open for 13% of the time, Pallas kernels for 2%

profile of v1, /device:TPU:0, one launch (start us, length us, event | category | flops | bytes accessed | tf_op | source)
XLA Modules:
  0.0 1213.6 jit_solution(12637075029245442883)
XLA Ops:
  24.5 14.3 %attend.2 = bf16[256,1024]{1,0:T(8,128)(2,1)} custom-call(s32[3]{0:T(128)} %pad_add_fusion.info, f32[16,256]{1,0:T(8,128)} %convolution_bitcast_fusion.1.refs_0_, bf16[256,3072]{1,0:T(8,128)(2,1)} %convolution_convert_fusion.1.refs_1_.refs_2_.refs_3_, bf16[256,3072]{1,0:T(8,128)(2,1)} %convolution_convert_fusion.1.refs_1_.refs_2_.refs_3_, ...), custom_call_target="tpu_custom_call" | custom-call | tf_op jit(solution)/shard_map/attend/pallas_call | solution.py:126
  41.4 38.9 %all_to_all.40 = bf16[8,80,1024]{2,1,0:T(8,128)(2,1)S(1)} all-to-all(bf16[8,80,1024]{2,1,0:T(8,128)(2,1)S(1)} %bitcast.280), channel_id=1, replica_groups=mesh['half'=2,'dp'=2,'expert'=8] {'expert'}, dimensions={0} | all-to-all | bytes 2621440 | tf_op jit(solution)/shard_map/all_to_all | solution.py:189
  89.9 15.7 %fusion.84 = bf16[640,1024]{1,0:T(8,128)(2,1)} fusion(bf16[1,1,2816,1024]{3,2,1,0:T(8,128)(2,1)} %param.28, f32[640,2816]{1,0:T(8,128)} %fusion.34, bf16[640,1024]{1,0:T(8,128)(2,1)} %bitcast.276, bf16[1,1,2,1024,2816]{4,3,2,1,0:T(8,128)(2,1)} %param.27), kind=kOutput, calls=%fused_computation.111 | convolution fusion | flops 7400652800 | bytes 21364736 | tf_op jit(solution)/shard_map/dot_general | solution.py:24
  110.8 30.0 %all-to-all-done.1 = bf16[8,80,1024]{2,1,0:T(8,128)(2,1)} async-done(((bf16[8,80,1024]{2,1,0:T(8,128)(2,1)}), bf16[8,80,1024]{2,1,0:T(8,128)(2,1)}, u32[]{:S(2)}, u32[]{:S(2)}) %all-to-all-start.1) | async-done | bytes 1310752 | tf_op jit(solution)/shard_map/all_to_all | solution.py:194
  149.6 14.2 %attend.3 = bf16[256,1024]{1,0:T(8,128)(2,1)} custom-call(s32[3]{0:T(128)} %pad_add_fusion.1.info, bf16[256,1024]{1,0:T(8,128)(2,1)} %fusion.110.refs_0_, bf16[256,2048]{1,0:T(8,128)(2,1)} %collective-permute-done.refs_1_.refs_2_, bf16[256,2048]{1,0:T(8,128)(2,1)} %collective-permute-done.refs_1_.refs_2_), custom_call_target="tpu_custom_call" | custom-call | tf_op jit(solution)/shard_map/attend/pallas_call | solution.py:126
  167.2 34.9 %all_to_all.41 = bf16[8,80,1024]{2,1,0:T(8,128)(2,1)S(1)} all-to-all(bf16[8,80,1024]{2,1,0:T(8,128)(2,1)S(1)} %bitcast.281), channel_id=1, replica_groups=mesh['half'=2,'dp'=2,'expert'=8] {'expert'}, dimensions={0} | all-to-all | bytes 2621440 | tf_op jit(solution)/shard_map/all_to_all | solution.py:189
  211.7 15.7 %fusion.87 = bf16[640,1024]{1,0:T(8,128)(2,1)} fusion(bf16[1,1,2816,1024]{3,2,1,0:T(8,128)(2,1)} %param.28, f32[640,2816]{1,0:T(8,128)} %fusion.32, bf16[640,1024]{1,0:T(8,128)(2,1)} %bitcast.278, bf16[1,1,2,1024,2816]{4,3,2,1,0:T(8,128)(2,1)} %param.27), kind=kOutput, calls=%fused_computation.112 | convolution fusion | flops 7400652800 | bytes 21364736 | tf_op jit(solution)/shard_map/dot_general | solution.py:24
  234.5 27.8 %all-to-all-done.3 = bf16[8,80,1024]{2,1,0:T(8,128)(2,1)} async-done(((bf16[8,80,1024]{2,1,0:T(8,128)(2,1)}), bf16[8,80,1024]{2,1,0:T(8,128)(2,1)}, u32[]{:S(2)}, u32[]{:S(2)}) %all-to-all-start.3) | async-done | bytes 1310752 | tf_op jit(solution)/shard_map/all_to_all | solution.py:194
  290.2 14.3 %all-to-all-done.4 = bf16[8,80,1024]{2,1,0:T(8,128)(2,1)} async-done(((bf16[8,80,1024]{2,1,0:T(8,128)(2,1)}), bf16[8,80,1024]{2,1,0:T(8,128)(2,1)}, u32[]{:S(2)}, u32[]{:S(2)}) %all-to-all-start.4) | async-done | bytes 1310752 | tf_op jit(solution)/shard_map/all_to_all | solution.py:203
  339.3 30.3 %all-to-all-done.5 = bf16[8,80,1024]{2,1,0:T(8,128)(2,1)} async-done(((bf16[8,80,1024]{2,1,0:T(8,128)(2,1)}), bf16[8,80,1024]{2,1,0:T(8,128)(2,1)}, u32[]{:S(2)}, u32[]{:S(2)}) %all-to-all-start.5) | async-done | bytes 1310752 | tf_op jit(solution)/shard_map/all_to_all | solution.py:213
  375.7 18.2 %attend_back.2 = (bf16[256,1024]{1,0:T(8,128)(2,1)}, bf16[256,2048]{1,0:T(8,128)(2,1)}) custom-call(s32[3]{0:T(128)} %pad_add_fusion.1.info, bf16[256,1024]{1,0:T(8,128)(2,1)} %fusion.110.refs_0_, bf16[256,2048]{1,0:T(8,128)(2,1)} %collective-permute-done.refs_1_.refs_2_, bf16[256,2048]{1,0:T(8,128)(2,1)} %collective-permute-done.refs_1_.refs_2_, ...), custom_call_target="tpu_custom_call" | custom-call | tf_op jit(solution)/shard_map/attend_back/pallas_call | solution.py:155
  408.4 34.9 %all_to_all.42 = bf16[8,80,1024]{2,1,0:T(8,128)(2,1)S(1)} all-to-all(bf16[8,80,1024]{2,1,0:T(8,128)(2,1)S(1)} %bitcast.295), channel_id=1, replica_groups=mesh['half'=2,'dp'=2,'expert'=8] {'expert'}, dimensions={0} | all-to-all | bytes 2621440 | tf_op jit(solution)/shard_map/all_to_all | solution.py:203
  443.4 15.6 %multiply_convert_fusion.2 = (bf16[640,2816]{1,0:T(8,128)(2,1)}, bf16[640,2816]{1,0:T(8,128)(2,1)}) fusion(f32[640,2816]{1,0:T(8,128)} %fusion.30, f32[640,2816]{1,0:T(8,128)} %fusion.40, bf16[640,1024]{1,0:T(8,128)(2,1)S(1)} %bitcast.288, bf16[1,1,2816,1024]{3,2,1,0:T(8,128)(2,1)} %param.28), kind=kOutput, calls=%fused_computation.26 | convolution fusion | flops 3732439040 | bytes 28704768 | tf_op jit(solution)/shard_map/dot_general | solution.py:24
  489.8 16.4 %all-to-all-done.7 = bf16[8,80,1024]{2,1,0:T(8,128)(2,1)} async-done(((bf16[8,80,1024]{2,1,0:T(8,128)(2,1)}), bf16[8,80,1024]{2,1,0:T(8,128)(2,1)}, u32[]{:S(2)}, u32[]{:S(2)}) %all-to-all-start.7) | async-done | bytes 1310752 | tf_op jit(solution)/shard_map/all_to_all | solution.py:213
  513.0 19.8 %attend_back.3 = (bf16[256,1024]{1,0:T(8,128)(2,1)}, bf16[256,2048]{1,0:T(8,128)(2,1)}, f32[16,256]{1,0:T(8,128)}) custom-call(s32[3]{0:T(128)} %pad_add_fusion.info, f32[16,256]{1,0:T(8,128)} %convolution_bitcast_fusion.1.refs_0_, bf16[256,3072]{1,0:T(8,128)(2,1)} %convolution_convert_fusion.1.refs_1_.refs_2_.refs_3_, ...), custom_call_target="tpu_custom_call" | custom-call | tf_op jit(solution)/shard_map/attend_back/pallas_call | solution.py:155
  552.2 14.0 %convolution_convert_fusion = bf16[2816,1024]{1,0:T(8,128)(2,1)} fusion(f32[640,2816]{1,0:T(8,128)} %fusion.30, bf16[640,1024]{1,0:T(8,128)(2,1)} %bitcast.289, bf16[640,1024]{1,0:T(8,128)(2,1)} %bitcast.43, pred[]{:T(512)S(6)} %eq.126, f32[640,2816]{1,0:T(8,128)} %fusion.40), kind=kOutput, calls=%fused_computation.62 | convolution fusion | flops 3712548864 | bytes 22806528 | tf_op jit(solution)/shard_map/dot_general | solution.py:24
  597.2 29.0 %copy.61 = bf16[2,1024,2816]{1,0,2:T(2,128)(2,1)} copy(bf16[2,1024,2816]{2,1,0:T(8,128)(2,1)} %pad_maximum_fusion) | data formatting | bytes 23068672
  642.2 40.0 %all-reduce.2 = (f32[512]{0:T(512)S(1)}, f32[16]{0:T(128)S(1)}) all-reduce(f32[512]{0:T(512)S(1)} %reshape.298, f32[16]{0:T(128)S(1)} %pad_maximum_fusion.3), channel_id=7, replica_groups=mesh['half'=2,'dp'=2,'expert'=8] {'dp','expert'}, use_global_device_ids=true, to_apply=%region_38.39.clone | all-reduce | flops 528 | bytes 4224
  688.5 43.8 %reduce-scatter.18.cloned.1.call-done = bf16[64,2048]{1,0:T(8,128)(2,1)} async-done(((bf16[1024,2048]{1,0:T(8,128)(2,1)}), bf16[64,2048]{1,0:T(8,128)(2,1)}) %reduce-scatter.18.cloned.1.call-update) | async-done | bytes 262160 | tf_op jit(solution)/shard_map/reduce_scatter | solution.py:416
  734.1 79.5 %reduce-scatter.16.cloned.1.call-done = bf16[64,1024]{1,0:T(8,128)(2,1)} async-done(((bf16[1024,1024]{1,0:T(8,128)(2,1)}), bf16[64,1024]{1,0:T(8,128)(2,1)}) %reduce-scatter.16.cloned.1.call-update) | async-done | bytes 131088 | tf_op jit(solution)/shard_map/reduce_scatter | solution.py:416
  815.2 69.4 %reduce-scatter.20.cloned.1.call-done = bf16[1408,1024]{1,0:T(8,128)(2,1)} async-done(((bf16[2816,1024]{1,0:T(8,128)(2,1)}), bf16[1408,1024]{1,0:T(8,128)(2,1)}) %reduce-scatter.20.cloned.1.call-update) | async-done | bytes 2883600 | tf_op jit(solution)/shard_map/reduce_scatter | solution.py:416
  889.7 147.1 %reduce-scatter.14.cloned.1.call-done = bf16[64,3072]{1,0:T(8,128)(2,1)} async-done(((bf16[1024,3072]{1,0:T(8,128)(2,1)}), bf16[64,3072]{1,0:T(8,128)(2,1)}) %reduce-scatter.14.cloned.1.call-update) | async-done | bytes 393232 | tf_op jit(solution)/shard_map/reduce_scatter | solution.py:416
  1038.7 133.4 %reduce-scatter.26.cloned.1.call-done = bf16[1408,2048]{1,0:T(8,128)(2,1)} async-done(((bf16[2816,2048]{1,0:T(8,128)(2,1)}), bf16[1408,2048]{1,0:T(8,128)(2,1)}) %reduce-scatter.26.cloned.1.call-update) | async-done | bytes 5767184
  1182.5 15.1 %copy.62 = bf16[2,1024,1408]{2,1,0:T(8,128)(2,1)} copy(bf16[2,1024,1408]{1,0,2:T(2,128)(2,1)} %bitcast.272) | data formatting | bytes 11534336
  (279 shorter events, 283.7 us)
Async XLA Ops:
  7.2 31.6 %copy-start = (bf16[1,1024,1024]{2,1,0:T(8,128)(2,1)S(1)}, bf16[1,1024,1024]{2,1,0:T(8,128)(2,1)}, u32[]{:S(2)}) copy-start(bf16[1,1024,1024]{2,1,0:T(8,128)(2,1)} %param.22) | copy-start | bytes 6291460
  11.7 12.8 %copy-start.32 = (f32[1,1,1024]{2,0,1:T(1,128)}, f32[1,1,1024]{2,0,1:T(1,128)S(1)}, u32[]{:S(2)}) copy-start(f32[1,1,1024]{2,0,1:T(1,128)S(1)} %get-tuple-element.73) | copy-start | bytes 12292
  40.8 107.2 %copy-start.1 = (f32[256,1024]{1,0:T(8,128)}, f32[256,1024]{1,0:T(8,128)S(1)}, u32[]{:S(2)}) copy-start(f32[256,1024]{1,0:T(8,128)S(1)} %get-tuple-element.80) | copy-start | bytes 3145732
  89.9 20.1 %copy-start.28 = (bf16[1,1024,8]{1,2,0:T(8,128)(2,1)S(1)}, bf16[1,1024,8]{1,2,0:T(8,128)(2,1)}, u32[]{:S(2)}) copy-start(bf16[1,1024,8]{1,2,0:T(8,128)(2,1)} %param.24) | copy-start | bytes 49156
  105.6 35.1 %all-to-all-start.1 = ((bf16[8,80,1024]{2,1,0:T(8,128)(2,1)}), bf16[8,80,1024]{2,1,0:T(8,128)(2,1)}, u32[]{:S(2)}, u32[]{:S(2)}) async-start(bf16[8,80,1024]{2,1,0:T(8,128)(2,1)} %bitcast.291), calls=%async_computation.1 | async-start | bytes 2621440 | tf_op jit(solution)/shard_map/all_to_all | solution.py:194
  144.9 4.6 collective-permute-start
  227.4 34.9 %all-to-all-start.3 = ((bf16[8,80,1024]{2,1,0:T(8,128)(2,1)}), bf16[8,80,1024]{2,1,0:T(8,128)(2,1)}, u32[]{:S(2)}, u32[]{:S(2)}) async-start(bf16[8,80,1024]{2,1,0:T(8,128)(2,1)} %bitcast.292), calls=%async_computation.3 | async-start | bytes 2621440 | tf_op jit(solution)/shard_map/all_to_all | solution.py:194
  268.9 35.6 %all-to-all-start.4 = ((bf16[8,80,1024]{2,1,0:T(8,128)(2,1)}), bf16[8,80,1024]{2,1,0:T(8,128)(2,1)}, u32[]{:S(2)}, u32[]{:S(2)}) async-start(bf16[8,80,1024]{2,1,0:T(8,128)(2,1)} %bitcast.294), calls=%async_computation.4 | async-start | bytes 2621440 | tf_op jit(solution)/shard_map/all_to_all | solution.py:203
  326.6 12.1 copy-start.45
  334.2 35.4 %all-to-all-start.5 = ((bf16[8,80,1024]{2,1,0:T(8,128)(2,1)}), bf16[8,80,1024]{2,1,0:T(8,128)(2,1)}, u32[]{:S(2)}, u32[]{:S(2)}) async-start(bf16[8,80,1024]{2,1,0:T(8,128)(2,1)} %bitcast.293), calls=%async_computation.5 | async-start | bytes 2621440 | tf_op jit(solution)/shard_map/all_to_all | solution.py:213
  393.9 5.0 collective-permute-start.1
  407.5 51.5 %slice-start.3 = ((s8[11534336]{0:T(1024)(128)(4,1)}), s8[3145728]{0:T(1024)(128)(4,1)S(1)}, s32[]{:S(2)}) async-start(s8[11534336]{0:T(1024)(128)(4,1)} %bitcast.336), calls=%async_computation.25 | async-start | bytes 6291456
  443.4 15.6 %copy-start.25 = (bf16[8,80,1024]{2,1,0:T(8,128)(2,1)}, bf16[8,80,1024]{2,1,0:T(8,128)(2,1)S(1)}, u32[]{:S(2)}) copy-start(bf16[8,80,1024]{2,1,0:T(8,128)(2,1)S(1)} %all_to_all.42) | copy-start | bytes 3932164
  443.4 15.6 %slice-start.4 = ((s8[11534336]{0:T(1024)(128)(4,1)}), s8[4194304]{0:T(1024)(128)(4,1)S(1)}, s32[]{:S(2)}) async-start(s8[11534336]{0:T(1024)(128)(4,1)} %bitcast.336), calls=%async_computation.26 | async-start | bytes 8388608
  443.4 15.6 %slice-start.5 = ((s8[11534336]{0:T(1024)(128)(4,1)}), s8[4194304]{0:T(1024)(128)(4,1)S(1)}, s32[]{:S(2)}) async-start(s8[11534336]{0:T(1024)(128)(4,1)} %bitcast.336), calls=%async_computation.27 | async-start | bytes 8388608
  470.1 36.1 %all-to-all-start.7 = ((bf16[8,80,1024]{2,1,0:T(8,128)(2,1)}), bf16[8,80,1024]{2,1,0:T(8,128)(2,1)}, u32[]{:S(2)}, u32[]{:S(2)}) async-start(bf16[8,80,1024]{2,1,0:T(8,128)(2,1)} %bitcast.290), calls=%async_computation.7 | async-start | bytes 2621440 | tf_op jit(solution)/shard_map/all_to_all | solution.py:213
  474.4 166.0 %reduce-scatter.22.cloned.1.call-start = ((), (), s32[]{:S(2)}) async-start(), calls=%async_computation.19 | async-start | bytes 557056
  482.3 204.8 %reduce-scatter.24.cloned.1.call-start = ((), (), s32[]{:S(2)}) async-start(), calls=%async_computation.20 | async-start | bytes 557056
  489.8 19.2 %copy-start.42 = (f32[256]{0:T(256)S(1)}, f32[256]{0:T(256)}, u32[]{:S(2)}) copy-start(f32[256]{0:T(256)} %get-tuple-element.95) | copy-start | bytes 3076
  541.6 190.7 %reduce-scatter.18.cloned.1.call-start = ((), (), s32[]{:S(2)}) async-start(), calls=%async_computation.17 | async-start | bytes 4456448 | tf_op jit(solution)/shard_map/reduce_scatter | solution.py:416
  547.3 266.3 %reduce-scatter.16.cloned.1.call-start = ((), (), s32[]{:S(2)}) async-start(), calls=%async_computation.16 | async-start | bytes 2228224 | tf_op jit(solution)/shard_map/reduce_scatter | solution.py:416
  551.7 332.9 %reduce-scatter.20.cloned.1.call-start = ((), (), s32[]{:S(2)}) async-start(), calls=%async_computation.18 | async-start | bytes 8650752 | tf_op jit(solution)/shard_map/reduce_scatter | solution.py:416
  566.2 470.6 %reduce-scatter.14.cloned.1.call-start = ((), (), s32[]{:S(2)}) async-start(), calls=%async_computation.15 | async-start | bytes 6684672 | tf_op jit(solution)/shard_map/reduce_scatter | solution.py:416
  579.6 592.4 %reduce-scatter.26.cloned.1.call-start = ((), (), s32[]{:S(2)}) async-start(), calls=%async_computation.21 | async-start | bytes 17301504
  (55 other events, 256.9 us)
Sparse Core Ops, SparseCore 0:
  482.4 78.2 reduce-scatter.21
  563.0 73.5 reduce-scatter.23
  638.9 93.3 reduce-scatter.17
  734.4 79.1 reduce-scatter.15
  816.3 68.2 reduce-scatter.19
  890.5 146.1 reduce-scatter.13
  1039.7 132.2 reduce-scatter.25

commit v2 on v1

--- a/solution.py
+++ b/solution.py
@@ -198,17 +198,20 @@
     return jnp.where(mine, back, kept_from[0]), jnp.where(mine, arrived, kept_from[1])
 
 
+def expert_parts(flat, flat_grad, w_in, w_down):
+    up = dot(flat, w_in[1])
+    value, slope = gelu_parts(dot(flat, w_in[0]))
+    hidden = (value * up).astype(BF16)
+    dhidden = dot(flat_grad, w_down, NT)
+    return (dhidden * up * slope).astype(BF16), (dhidden * value).astype(BF16), hidden
+
+
 def moe_backward(grad_send, received, w_in, w_down, turn, kept_from):
     width = grad_send.shape[2]
     arrived = lax.all_to_all(grad_send, "expert", split_axis=0, concat_axis=0, tiled=True)
     flat_grad = arrived.reshape(-1, width)
     flat = received.reshape(-1, width)
-    up = dot(flat, w_in[1])
-    value, slope = gelu_parts(dot(flat, w_in[0]))
-    hidden = (value * up).astype(BF16)
-    dhidden = dot(flat_grad, w_down, NT)
-    dgate = (dhidden * up * slope).astype(BF16)
-    dup = (dhidden * value).astype(BF16)
+    dgate, dup, hidden = expert_parts(flat, flat_grad, w_in, w_down)
     drows = (dot(dgate, w_in[0], NT) + dot(dup, w_in[1], NT)).astype(BF16)
     back = lax.all_to_all(
         drows.reshape(arrived.shape), "expert", split_axis=0, concat_axis=0, tiled=True
@@ -218,6 +221,184 @@
         return out
     mine = lax.axis_index("half") == turn
     return tuple(jnp.where(mine, a, b) for a, b in zip(out, kept_from))
+
+
+def flipped(value, bit):
+    step = 1 << bit
+    return value + step * (1 - 2 * (value // step % 2))
+
+
+def greet(partners):
+    barrier = pltpu.get_barrier_semaphore()
+    for partner in partners:
+        pl.semaphore_signal(barrier, inc=1, device_id=partner, device_id_type=MESH)
+    pl.semaphore_wait(barrier, len(partners))
+
+
+def dense_kernel(starts, stages, ahead, *refs):
+    xt_ref, dy_ref, small_ref, out_ref, small_out = refs[:5]
+    xp, dyp, small_in = refs[5:8]
+    sums = refs[8 : 8 + stages]
+    parts = refs[8 + stages : 8 + 2 * stages]
+    sx, rx, sy, ry, ss, rs, sk, rk = refs[8 + 2 * stages :]
+    chunks = dy_ref.shape[0]
+    half_rows = xp.shape[1]
+    dp, me = lax.axis_index("dp"), lax.axis_index("expert")
+    peer = {"dp": 1 - dp}
+    partners = [{"expert": flipped(me, k)} for k in range(stages)]
+    bits = [me // (1 << k) % 2 for k in range(stages)]
+    greet([peer] + partners)
+
+    def send(src, dst, out_sem, in_sem, device):
+        return pltpu.make_async_remote_copy(
+            src_ref=src,
+            dst_ref=dst,
+            send_sem=out_sem,
+            recv_sem=in_sem,
+            device_id=device,
+            device_id_type=MESH,
+        )
+
+    def send_x(g):
+        rows = pl.ds(pl.multiple_of((1 - dp) * half_rows, half_rows), half_rows)
+        return send(xt_ref.at[g, rows], xp.at[g], sx.at[g], rx.at[g], peer)
+
+    def send_dy(c):
+        return send(dy_ref.at[c], dyp.at[c], sy.at[c], ry.at[c], peer)
+
+    def send_small(step):
+        src = small_ref if step == 0 else small_out.at[step - 1]
+        device = peer if step == 0 else partners[step - 1]
+        return send(src, small_in.at[step], ss.at[step], rs.at[step], device)
+
+    def send_part(k, c):
+        return send(
+            sums[k].at[c, :, 1 - bits[k]], parts[k].at[c], sk.at[k, c], rk.at[k, c], partners[k]
+        )
+
+    send_small(0).start()
+    for g in range(len(starts)):
+        send_x(g).start()
+        if g == 0:
+            for c in range(ahead):
+                send_dy(c).start()
+
+    def step(i, carry):
+        @pl.when(i < chunks)
+        def _():
+            @pl.when(i + ahead < chunks)
+            def _():
+                send_dy(i + ahead).start()
+
+            group = jnp.int32(0)
+            for g, first in enumerate(starts):
+                if g:
+                    group = group + (i >= first).astype(jnp.int32)
+
+                @pl.when(i == first)
+                def _(g=g):
+                    send_x(g).wait_recv()
+
+            send_dy(i).wait_recv()
+            rows = pl.ds(pl.multiple_of(dp * half_rows, half_rows), half_rows)
+            total = dot(xt_ref[group, rows], dy_ref[i]) + dot(xp[group], dyp[i])
+            sums[0][i] = total.astype(BF16).reshape(sums[0].shape[1:])
+            send_part(0, i).start()
+
+        for k in range(stages):
+            c = i - 1 - k
+
+            @pl.when((c >= 0) & (c < chunks))
+            def _(k=k, c=c):
+                send_part(k, c).wait_recv()
+                total = sums[k][c, :, bits[k]].astype(F32) + parts[k][c].astype(F32)
+                if k + 1 < stages:
+                    sums[k + 1][c] = total.astype(BF16).reshape(sums[k + 1].shape[1:])
+                    send_part(k + 1, c).start()
+                else:
+                    out_ref[c] = total[0]
+
+        for j in range(stages + 1):
+
+            @pl.when(i == j)
+            def _(j=j):
+                send_small(j).wait_recv()
+                own = small_ref[...] if j == 0 else small_out[j - 1]
+                small_out[j] = own + small_in[j]
+                if j < stages:
+                    send_small(j + 1).start()
+
+        return carry
+
+    lax.fori_loop(0, chunks + stages, step, 0)
+
+    def finish(c, carry):
+        send_dy(c).wait_send()
+        for k in range(stages):
+            send_part(k, c).wait_send()
+        return carry
+
+    lax.fori_loop(0, chunks, finish, 0)
+    for g in range(len(starts)):
+        send_x(g).wait_send()
+    for j in range(stages + 1):
+        send_small(j).wait_send()
+
+
+def dense_gradients(pairs, small, experts):
+    chunk = 512
+    rows, width = pairs[0][0].shape
+    xt = jnp.stack([jnp.transpose(x) for x, _ in pairs])
+    dy = jnp.concatenate([y for _, y in pairs], axis=1)
+    chunks = dy.shape[1] // chunk
+    dy = jnp.transpose(dy.reshape(rows, chunks, chunk), (1, 0, 2))
+    starts, at = [], 0
+    for _, y in pairs:
+        starts.append(at)
+        at += y.shape[1] // chunk
+    stages = experts.bit_length() - 1
+    own = width // (2 * experts)
+    vmem = pl.BlockSpec(memory_space=pltpu.VMEM)
+    dma = pltpu.SemaphoreType.DMA
+    scratch = [
+        pltpu.VMEM((len(pairs), width // 2, rows), BF16),
+        pltpu.VMEM(dy.shape, BF16),
+        pltpu.VMEM((stages + 1, *small.shape), F32),
+    ]
+    scratch += [
+        pltpu.VMEM((chunks, experts >> (k + 1), 2, own, chunk), BF16) for k in range(stages)
+    ]
+    scratch += [pltpu.VMEM((chunks, experts >> (k + 1), own, chunk), BF16) for k in range(stages)]
+    scratch += [
+        dma((len(pairs),)),
+        dma((len(pairs),)),
+        dma((chunks,)),
+        dma((chunks,)),
+        dma((stages + 1,)),
+        dma((stages + 1,)),
+        dma((stages, chunks)),
+        dma((stages, chunks)),
+    ]
+    out, sums = pl.pallas_call(
+        functools.partial(dense_kernel, tuple(starts), stages, 4),
+        in_specs=[vmem] * 3,
+        out_specs=[vmem] * 2,
+        out_shape=[
+            jax.ShapeDtypeStruct((chunks, own, chunk), F32),
+            jax.ShapeDtypeStruct((stages + 1, *small.shape), F32),
+        ],
+        scratch_shapes=scratch,
+        compiler_params=pltpu.CompilerParams(
+            collective_id=0, has_side_effects=True, vmem_limit_bytes=56 << 20
+        ),
+        name="dense_gradients",
+    )(xt, dy, small)
+    results = []
+    for (_, y), first in zip(pairs, starts):
+        count = y.shape[1] // chunk
+        part = jnp.transpose(out[first : first + count], (1, 0, 2))
+        results.append(part.reshape(own, count * chunk))
+    return results, sums[stages]
 
 
 def body(
@@ -398,36 +579,65 @@
     ).reshape(-1)
 
     left = jnp.where(decoder, low_c, low_m)
-    right_enc = dot(left, jnp.where(decoder, jnp.concatenate([dquery, dquery], 1), dmemory), TN)
-    dcross_out = dot(mixed_c, dbranch_c, TN)
-    dcross = jnp.where(
-        decoder, jnp.concatenate([right_enc[:, :width], dcross_out], axis=1), right_enc
-    )
-    dqkv = jnp.concatenate([dot(low0, dq, TN), dot(low0, dkv, TN)], axis=1)
-    dout = dot(mixed0, dbranch, TN)
-    flat = received.reshape(-1, width)
-    din = jnp.stack([dot(flat, dgate, TN), dot(flat, dup, TN)])
-    ddown = dot(hidden, flat_grad, TN)
-    dgains = jnp.stack([dgain_self, dgain_moe, jnp.where(decoder, dgain_c, dgain_m)])
-
-    axes = ("dp", "expert")
-
-    def scattered(array, dim, over=axes):
-        return lax.psum_scatter(array, over, scatter_dimension=dim, tiled=True).astype(F32)
-
-    counts = scattered(tallies, 0).astype(jnp.int32).reshape(1, 1, 1)
+    right = jnp.where(decoder, dquery, dmemory[:, :width])
+    left_out = jnp.where(decoder, mixed_c, low_m)
+    right_out = jnp.where(decoder, dbranch_c, dmemory[:, width:])
+    pairs = [
+        (low0, jnp.concatenate([dq, dkv], axis=1)),
+        (mixed0, dbranch),
+        (left, right),
+        (left_out, right_out),
+    ]
+    extra = jnp.concatenate([dtable, tallies, jnp.zeros((width - dtable.shape[0] - tallies.shape[0],), F32)])
+    small = jnp.concatenate(
+        [
+            jnp.transpose(drouter),
+            dgain_self[None],
+            dgain_moe[None],
+            jnp.where(decoder, dgain_c, dgain_m)[None],
+            extra[None],
+        ]
+    )
+    small = jnp.pad(small, ((0, -small.shape[0] % 8), (0, 0)))
+    (dqkv, dout, dcross_a, dcross_b), small = dense_gradients(pairs, small, experts)
+    dp_index = lax.axis_index("dp")
+    place = dp_index * experts + lax.axis_index("expert")
+    own = width // (2 * experts)
+    mine = lax.dynamic_slice_in_dim(small[: experts + 3], place * own, own, 1)
+    tail = small[experts + 3]
+    own_table = dtable.shape[0] // (2 * experts)
+    d_table = lax.dynamic_slice_in_dim(tail, place * own_table, own_table)
+    counts = lax.dynamic_slice_in_dim(tail, dtable.shape[0] + place, 1).astype(jnp.int32)
+
+    swap = [(0, 1), (1, 0)]
+    ff = w_down.shape[0]
+    span = ff // 2
+    rows_own = received.reshape(-1, width)
+    rows_peer = lax.ppermute(rows_own, "dp", swap)
+    grad_peer = lax.ppermute(flat_grad, "dp", swap)
+    in_half = lax.dynamic_slice_in_dim(w_in, dp_index * span, span, 2)
+    down_half = lax.dynamic_slice_in_dim(w_down, dp_index * span, span, 0)
+    peer_parts = expert_parts(rows_peer, grad_peer, in_half, down_half)
+    own_parts = [
+        lax.dynamic_slice_in_dim(a, dp_index * span, span, 1) for a in (dgate, dup, hidden)
+    ]
+    dgate, dup, hidden = [jnp.concatenate(p) for p in zip(own_parts, peer_parts)]
+    all_rows = jnp.concatenate([rows_own, rows_peer])
+    all_grad = jnp.concatenate([flat_grad, grad_peer])
+    din = jnp.stack([dot(all_rows, dgate, TN), dot(all_rows, dup, TN)])
+    ddown = dot(hidden, all_grad, TN)
     return (
         outputs.reshape(1, seqs, length, width),
         d_tokens.reshape(1, seqs, length, width),
-        scattered(dqkv.astype(BF16), 0)[None],
-        scattered(dout.astype(BF16), 0)[None],
-        scattered(dcross.astype(BF16), 0)[None],
-        scattered(drouter, 0)[None],
-        scattered(dgains, 1)[None],
-        scattered(dtable, 0)[None],
-        scattered(din.astype(BF16), 2, "dp")[None, None],
-        scattered(ddown.astype(BF16), 0, "dp")[None, None],
-        counts,
+        dqkv[None],
+        dout[None],
+        jnp.concatenate([dcross_a, dcross_b], axis=1)[None],
+        jnp.transpose(mine[:experts])[None],
+        mine[experts:][None],
+        d_table[None],
+        din[None, None],
+        ddown[None, None],
+        counts.reshape(1, 1, 1),
     )
 
 

time: 1220 us -> 760 us (0.62)
  waiting for transfers between devices: 595 us -> 115 us
  Pallas kernels: 66.4 us -> 180 us
  blocking collectives: 149 us -> 73.2 us
  local copies, waits for them, and re-layouts: 89.6 us -> 69 us
  between operations: 17.8 us -> 1.93 us
    reduce_scatter x4 -> x0, waiting for transfers between devices: 340 us -> none  [scattered(): lax.psum_scatter(array, over, scatter_dimension=dim, tiled=True).astype(F32)]
    unnamed x10 -> x0, waiting for transfers between devices: 133 us -> none
    pallas_call x0 -> x1, Pallas kernels: none -> 114 us  [dense_gradients(): pl.pallas_call(functools.partial(dense_kernel, tuple(starts), stages, 4),...]
    unnamed x142 -> x148, local copies, waits for them, and re-layouts: 82.6 us -> 20.3 us
    unnamed x1 -> x0, blocking collectives: 40 us -> none
    all_to_all x1 -> x0, blocking collectives: 34.9 us -> none  [moe_backward(): lax.all_to_all(grad_send, 'expert', split_axis=0, concat_axis=0, tiled=True)]
    all_to_all x2, waiting for transfers between devices: 46.7 us -> 26.8 us  [moe_backward(): lax.all_to_all(drows.reshape(arrived.shape), 'expert', split_axis=0, conc...]
    ppermute x0 -> x2, waiting for transfers between devices: none -> 19.5 us  [the longest x1 9.92 us: body(): rows_peer = lax.ppermute(rows_own, 'dp', swap)]
  transfers between devices with their start and end apart: 14 -> 10, of which waited for: 11 -> 6; matrix products, arithmetic and copies ran while one was open for 13% -> 17% of each run, Pallas kernels for 2% -> 0%
where the time goes in v2:
time: 760 us; the launch traced here: 753 us
  matrix products  218 us (29%)
  Pallas kernels  180 us (24%)
  waiting for transfers between devices  115 us (15%)
  blocking collectives  73.2 us (10%)
  local copies, waits for them, and re-layouts  69 us (9%)
  other arithmetic  61.8 us (8%)
  starting transfers between devices  33.5 us (4%)
    dot_general x41, matrix products, dot(): return lax.dot_general(a, b, dims, preferred_element_type=F32)  212 us
    pallas_call x1, Pallas kernels, dense_gradients(): pl.pallas_call(functools.partial(dense_kernel, tuple(starts), stages, 4),...  114 us
    all_to_all x2, blocking collectives, moe_forward(): lax.all_to_all(send, 'expert', split_axis=0, concat_axis=0, tiled=True)  73.2 us
    all_to_all x2, waiting for transfers between devices, moe_forward(): lax.all_to_all(result, 'expert', split_axis=0, concat_axis=0, tiled=True)  54.6 us
    pallas_call x2, Pallas kernels, attend_back(): pl.pallas_call(functools.partial(attend_back_kernel, bias is not None), g...  38.2 us
    pallas_call x2, Pallas kernels, attend(): pl.pallas_call(functools.partial(attend_kernel, bias is not None), grid=(...  28.4 us
    all_to_all x2, waiting for transfers between devices, moe_backward(): lax.all_to_all(drows.reshape(arrived.shape), 'expert', split_axis=0, conc...  26.8 us
    unnamed x148, local copies, waits for them, and re-layouts  20.3 us
  transfers between devices with their start and end apart: 10, of which 6 were waited for; matrix products, arithmetic and copies ran while one was open for 17% of the time, Pallas kernels for 0%

profile of v2, /device:TPU:0, one launch (start us, length us, event | category | flops | bytes accessed | tf_op | source)
XLA Modules:
  0.0 753.1 jit_solution(10199735896461008468)
XLA Ops:
  17.5 14.3 %attend.2 = bf16[256,1024]{1,0:T(8,128)(2,1)} custom-call(s32[3]{0:T(128)} %pad_add_fusion.info, f32[16,256]{1,0:T(8,128)} %convolution_bitcast_fusion.4.refs_0_, bf16[256,3072]{1,0:T(8,128)(2,1)} %convolution_convert_fusion.refs_1_.refs_2_.refs_3_, bf16[256,3072]{1,0:T(8,128)(2,1)} %convolution_convert_fusion.refs_1_.refs_2_.refs_3_, ...), custom_call_target="tpu_custom_call" | custom-call | tf_op jit(solution)/shard_map/attend/pallas_call | solution.py:126
  35.4 38.6 %all_to_all.40 = bf16[8,80,1024]{2,1,0:T(8,128)(2,1)S(1)} all-to-all(bf16[8,80,1024]{2,1,0:T(8,128)(2,1)S(1)} %bitcast.293), channel_id=1, replica_groups=mesh['half'=2,'dp'=2,'expert'=8] {'expert'}, dimensions={0} | all-to-all | bytes 2621440 | tf_op jit(solution)/shard_map/all_to_all | solution.py:189
  75.1 8.5 %fusion.33 = f32[640,2816]{1,0:T(8,128)} fusion(bf16[640,1024]{1,0:T(8,128)(2,1)S(1)} %bitcast.288, bf16[1,1,2,1024,2816]{4,3,2,1,0:T(8,128)(2,1)} %param.27), kind=kOutput, calls=%fused_computation.43 | convolution fusion | flops 3690987520 | bytes 14286848 | tf_op jit(solution)/shard_map/dot_general | solution.py:24
  83.6 15.5 %fusion.104 = bf16[640,1024]{1,0:T(8,128)(2,1)} fusion(bf16[1,1,2816,1024]{3,2,1,0:T(8,128)(2,1)} %param.28, f32[640,2816]{1,0:T(8,128)} %fusion.33, bf16[640,1024]{1,0:T(8,128)(2,1)} %bitcast.289, bf16[1,1,2,1024,2816]{4,3,2,1,0:T(8,128)(2,1)} %param.27), kind=kOutput, calls=%fused_computation.135 | convolution fusion | flops 7400652800 | bytes 21364736 | tf_op jit(solution)/shard_map/dot_general | solution.py:24
  104.2 30.0 %all-to-all-done.1 = bf16[8,80,1024]{2,1,0:T(8,128)(2,1)} async-done(((bf16[8,80,1024]{2,1,0:T(8,128)(2,1)}), bf16[8,80,1024]{2,1,0:T(8,128)(2,1)}, u32[]{:S(2)}, u32[]{:S(2)}) %all-to-all-start.1) | async-done | bytes 1310752 | tf_op jit(solution)/shard_map/all_to_all | solution.py:194
  150.0 14.2 %attend.3 = bf16[256,1024]{1,0:T(8,128)(2,1)} custom-call(s32[3]{0:T(128)} %pad_add_fusion.1.info, bf16[256,1024]{1,0:T(8,128)(2,1)} %fusion.128.refs_0_, bf16[256,2048]{1,0:T(8,128)(2,1)} %collective-permute-done.refs_1_.refs_2_, bf16[256,2048]{1,0:T(8,128)(2,1)} %collective-permute-done.refs_1_.refs_2_), custom_call_target="tpu_custom_call" | custom-call | tf_op jit(solution)/shard_map/attend/pallas_call | solution.py:126
  168.5 34.6 %all_to_all.41 = bf16[8,80,1024]{2,1,0:T(8,128)(2,1)S(1)} all-to-all(bf16[8,80,1024]{2,1,0:T(8,128)(2,1)S(1)} %bitcast.294), channel_id=1, replica_groups=mesh['half'=2,'dp'=2,'expert'=8] {'expert'}, dimensions={0} | all-to-all | bytes 2621440 | tf_op jit(solution)/shard_map/all_to_all | solution.py:189
  204.1 8.5 %fusion.31 = f32[640,2816]{1,0:T(8,128)} fusion(bf16[640,1024]{1,0:T(8,128)(2,1)S(1)} %bitcast.290, bf16[1,1,2,1024,2816]{4,3,2,1,0:T(8,128)(2,1)} %param.27), kind=kOutput, calls=%fused_computation.41 | convolution fusion | flops 3690987520 | bytes 14286848 | tf_op jit(solution)/shard_map/dot_general | solution.py:24
  212.6 15.5 %fusion.107 = bf16[640,1024]{1,0:T(8,128)(2,1)} fusion(bf16[1,1,2816,1024]{3,2,1,0:T(8,128)(2,1)} %param.28, f32[640,2816]{1,0:T(8,128)} %fusion.31, bf16[640,1024]{1,0:T(8,128)(2,1)} %bitcast.291, bf16[1,1,2,1024,2816]{4,3,2,1,0:T(8,128)(2,1)} %param.27), kind=kOutput, calls=%fused_computation.136 | convolution fusion | flops 7400652800 | bytes 21364736 | tf_op jit(solution)/shard_map/dot_general | solution.py:24
  238.5 24.6 %all-to-all-done.3 = bf16[8,80,1024]{2,1,0:T(8,128)(2,1)} async-done(((bf16[8,80,1024]{2,1,0:T(8,128)(2,1)}), bf16[8,80,1024]{2,1,0:T(8,128)(2,1)}, u32[]{:S(2)}, u32[]{:S(2)}) %all-to-all-start.3) | async-done | bytes 1310752 | tf_op jit(solution)/shard_map/all_to_all | solution.py:194
  275.6 9.0 %fusion.29 = f32[640,2816]{1,0:T(8,128)} fusion(bf16[640,1024]{1,0:T(8,128)(2,1)S(1)} %bitcast.299, bf16[1,1,2,1024,2816]{4,3,2,1,0:T(8,128)(2,1)} %param.27), kind=kOutput, calls=%fused_computation.39 | convolution fusion | flops 3690987520 | bytes 14286848 | tf_op jit(solution)/shard_map/dot_general | solution.py:24
  290.6 14.3 %all-to-all-done.4 = bf16[8,80,1024]{2,1,0:T(8,128)(2,1)} async-done(((bf16[8,80,1024]{2,1,0:T(8,128)(2,1)}), bf16[8,80,1024]{2,1,0:T(8,128)(2,1)}, u32[]{:S(2)}, u32[]{:S(2)}) %all-to-all-start.4) | async-done | bytes 1310752 | tf_op jit(solution)/shard_map/all_to_all | solution.py:211
  304.9 13.8 %multiply_convert_fusion.3 = (bf16[640,2816]{1,0:T(8,128)(2,1)S(1)}, bf16[640,2816]{1,0:T(8,128)(2,1)S(1)}) fusion(f32[640,2816]{1,0:T(8,128)} %fusion.29, f32[640,2816]{1,0:T(8,128)} %fusion.39, bf16[640,1024]{1,0:T(8,128)(2,1)} %bitcast.43, bf16[1,1,2816,1024]{3,2,1,0:T(8,128)(2,1)} %param.28), kind=kOutput, calls=%fused_computation.25 | convolution fusion | flops 3732439040 | bytes 28704768 | tf_op jit(solution)/shard_map/dot_general | solution.py:24
  318.7 8.1 %fusion.27 = f32[640,1024]{1,0:T(8,128)S(1)} fusion(bf16[640,2816]{1,0:T(8,128)(2,1)S(1)} %get-tuple-element.96, bf16[1,1,2,1024,2816]{4,3,2,1,0:T(8,128)(2,1)} %param.27), kind=kOutput, calls=%fused_computation.37 | convolution fusion | flops 3690987520 | bytes 11993088 | tf_op jit(solution)/shard_map/dot_general | solution.py:24
  343.1 26.8 %all-to-all-done.5 = bf16[8,80,1024]{2,1,0:T(8,128)(2,1)} async-done(((bf16[8,80,1024]{2,1,0:T(8,128)(2,1)}), bf16[8,80,1024]{2,1,0:T(8,128)(2,1)}, u32[]{:S(2)}, u32[]{:S(2)}) %all-to-all-start.5) | async-done | bytes 1310752 | tf_op jit(solution)/shard_map/all_to_all | solution.py:216
  376.8 18.1 %attend_back.2 = (bf16[256,1024]{1,0:T(8,128)(2,1)}, bf16[256,2048]{1,0:T(8,128)(2,1)}) custom-call(s32[3]{0:T(128)} %pad_add_fusion.1.info, bf16[256,1024]{1,0:T(8,128)(2,1)} %fusion.128.refs_0_, bf16[256,2048]{1,0:T(8,128)(2,1)} %collective-permute-done.refs_1_.refs_2_, bf16[256,2048]{1,0:T(8,128)(2,1)} %collective-permute-done.refs_1_.refs_2_, ...), custom_call_target="tpu_custom_call" | custom-call | tf_op jit(solution)/shard_map/attend_back/pallas_call | solution.py:155
  426.2 9.9 %collective-permute-done.2 = bf16[640,1024]{1,0:T(8,128)(2,1)} collective-permute-done((bf16[640,1024]{1,0:T(8,128)(2,1)}, bf16[640,1024]{1,0:T(8,128)(2,1)}, u32[]{:S(2)}, u32[]{:S(2)}) %collective-permute-start.2) | collective-permute-done | bytes 1310752 | tf_op jit(solution)/shard_map/ppermute | solution.py:616
  460.0 15.7 %multiply_convert_fusion.1 = (bf16[640,2816]{1,0:T(8,128)(2,1)S(1)}, bf16[640,2816]{1,0:T(8,128)(2,1)S(1)}, f32[640,2816]{1,0:T(8,128)}) fusion(f32[640,2816]{1,0:T(8,128)} %fusion.29, f32[640,2816]{1,0:T(8,128)} %fusion.39, bf16[640,1024]{1,0:T(8,128)(2,1)} %bitcast.50, bf16[1,1,2816,1024]{3,2,1,0:T(8,128)(2,1)} %param.28), kind=kOutput, calls=%fused_computation.23 | convolution fusion | flops 3732439040 | bytes 35913728 | tf_op jit(solution)/shard_map/dot_general | solution.py:24
  475.7 8.1 %fusion.25 = f32[640,1024]{1,0:T(8,128)S(1)} fusion(bf16[640,2816]{1,0:T(8,128)(2,1)S(1)} %get-tuple-element.94, bf16[1,1,2,1024,2816]{4,3,2,1,0:T(8,128)(2,1)} %param.27), kind=kOutput, calls=%fused_computation.35 | convolution fusion | flops 3690987520 | bytes 11993088 | tf_op jit(solution)/shard_map/dot_general | solution.py:24
  508.9 9.5 %collective-permute-done.3 = bf16[640,1024]{1,0:T(8,128)(2,1)} collective-permute-done((bf16[640,1024]{1,0:T(8,128)(2,1)}, bf16[640,1024]{1,0:T(8,128)(2,1)}, u32[]{:S(2)}, u32[]{:S(2)}) %collective-permute-start.3) | collective-permute-done | bytes 1310752 | tf_op jit(solution)/shard_map/ppermute | solution.py:617
  542.5 8.2 %convolution_bitcast_fusion = f32[1,1,1408,1024]{3,2,1,0:T(8,128)} fusion(bf16[640,1408]{1,0:T(8,128)(2,1)S(1)} %get-tuple-element.98, bf16[640,1408]{1,0:T(8,128)(2,1)S(1)} %fusion.58, bf16[640,1024]{1,0:T(8,128)(2,1)} %collective-permute-done.3, bf16[640,1024]{1,0:T(8,128)(2,1)} %broadcast_select_fusion), kind=kOutput, calls=%fused_computation.57 | convolution fusion | flops 3703439360 | bytes 11993088 | tf_op jit(solution)/shard_map/dot_general | solution.py:24
  550.7 8.5 %maximum_bitcast_fusion = f32[1,1,2,1024,1408]{4,3,2,1,0:T(8,128)} fusion(f32[1,1024,1408]{2,1,0:T(8,128)S(1)} %convolution_bitcast_fusion.1, f32[1,1024,1408]{2,1,0:T(8,128)} %convolution_bitcast_fusion.2), kind=kLoop, calls=%fused_computation | loop fusion | flops 2883584 | bytes 23068672 | tf_op jit(solution)/shard_map/broadcast_in_dim | solution.py:638
  568.4 20.1 %attend_back.3 = (bf16[256,1024]{1,0:T(8,128)(2,1)}, bf16[256,2048]{1,0:T(8,128)(2,1)}, f32[16,256]{1,0:T(8,128)}) custom-call(s32[3]{0:T(128)} %pad_add_fusion.info, f32[16,256]{1,0:T(8,128)} %convolution_bitcast_fusion.4.refs_0_, bf16[256,3072]{1,0:T(8,128)(2,1)} %convolution_convert_fusion.refs_1_.refs_2_.refs_3_, ...), custom_call_target="tpu_custom_call" | custom-call | tf_op jit(solution)/shard_map/attend_back/pallas_call | solution.py:155
  617.6 113.6 %dense_gradients.1 = (f32[12,64,512]{2,1,0:T(8,128)}, f32[4,16,1024]{2,1,0:T(8,128)}) custom-call(bf16[4,1024,256]{2,1,0:T(8,128)(2,1)} %pad_maximum_fusion.1.refs_0_, bf16[12,256,512]{2,1,0:T(8,128)(2,1)} %bitcast.286, f32[16,1024]{1,0:T(8,128)} %pad.4.refs_2_), custom_call_target="tpu_custom_call" | custom-call | tf_op jit(solution)/shard_map/dense_gradients/pallas_call | solution.py:382
  (296 shorter events, 263.0 us)
Async XLA Ops:
  0.6 31.1 %copy-start = (bf16[1,1024,1024]{2,1,0:T(8,128)(2,1)S(1)}, bf16[1,1024,1024]{2,1,0:T(8,128)(2,1)}, u32[]{:S(2)}) copy-start(bf16[1,1024,1024]{2,1,0:T(8,128)(2,1)} %param.22) | copy-start | bytes 6291460
  7.0 10.6 %copy-start.42 = (f32[1,1,1024]{2,0,1:T(1,128)}, f32[1,1,1024]{2,0,1:T(1,128)S(1)}, u32[]{:S(2)}) copy-start(f32[1,1,1024]{2,0,1:T(1,128)S(1)} %get-tuple-element.109) | copy-start | bytes 12292
  34.2 375.8 %copy-start.40 = (f32[256]{0:T(256)}, f32[256]{0:T(256)S(1)}, u32[]{:S(2)}) copy-start(f32[256]{0:T(256)S(1)} %add_rsqrt_fusion.2) | copy-start | bytes 3076
  83.6 19.8 %copy-start.34 = (bf16[1,1024,8]{1,2,0:T(8,128)(2,1)S(1)}, bf16[1,1024,8]{1,2,0:T(8,128)(2,1)}, u32[]{:S(2)}) copy-start(bf16[1,1024,8]{1,2,0:T(8,128)(2,1)} %param.24) | copy-start | bytes 49156
  99.2 35.0 %all-to-all-start.1 = ((bf16[8,80,1024]{2,1,0:T(8,128)(2,1)}), bf16[8,80,1024]{2,1,0:T(8,128)(2,1)}, u32[]{:S(2)}, u32[]{:S(2)}) async-start(bf16[8,80,1024]{2,1,0:T(8,128)(2,1)} %bitcast.306), calls=%async_computation.1 | async-start | bytes 2621440 | tf_op jit(solution)/shard_map/all_to_all | solution.py:194
  145.1 4.9 collective-permute-start
  166.9 207.1 %copy-start.37 = (f32[256]{0:T(256)}, f32[256]{0:T(256)S(1)}, u32[]{:S(2)}) copy-start(f32[256]{0:T(256)S(1)} %add_rsqrt_fusion) | copy-start | bytes 3076
  228.2 34.9 %all-to-all-start.3 = ((bf16[8,80,1024]{2,1,0:T(8,128)(2,1)}), bf16[8,80,1024]{2,1,0:T(8,128)(2,1)}, u32[]{:S(2)}, u32[]{:S(2)}) async-start(bf16[8,80,1024]{2,1,0:T(8,128)(2,1)} %bitcast.307), calls=%async_computation.3 | async-start | bytes 2621440 | tf_op jit(solution)/shard_map/all_to_all | solution.py:194
  237.9 29.2 %copy-start.45 = (f32[256]{0:T(256)}, f32[256]{0:T(256)S(1)}, u32[]{:S(2)}) copy-start(f32[256]{0:T(256)S(1)} %fusion.180) | copy-start | bytes 3076
  238.5 102.7 %copy-start.47 = (f32[256]{0:T(256)}, f32[256]{0:T(256)S(1)}, u32[]{:S(2)}) copy-start(f32[256]{0:T(256)S(1)} %get-tuple-element.79) | copy-start | bytes 3076
  269.7 35.2 %all-to-all-start.4 = ((bf16[8,80,1024]{2,1,0:T(8,128)(2,1)}), bf16[8,80,1024]{2,1,0:T(8,128)(2,1)}, u32[]{:S(2)}, u32[]{:S(2)}) async-start(bf16[8,80,1024]{2,1,0:T(8,128)(2,1)} %bitcast.309), calls=%async_computation.4 | async-start | bytes 2621440 | tf_op jit(solution)/shard_map/all_to_all | solution.py:211
  274.0 10.7 %slice-start = ((s8[11534336]{0:T(1024)(128)(4,1)}), s8[4194304]{0:T(1024)(128)(4,1)S(1)}, s32[]{:S(2)}) async-start(s8[11534336]{0:T(1024)(128)(4,1)} %bitcast.353), calls=%async_computation.8 | async-start | bytes 8388608
  334.5 35.4 %all-to-all-start.5 = ((bf16[8,80,1024]{2,1,0:T(8,128)(2,1)}), bf16[8,80,1024]{2,1,0:T(8,128)(2,1)}, u32[]{:S(2)}, u32[]{:S(2)}) async-start(bf16[8,80,1024]{2,1,0:T(8,128)(2,1)} %bitcast.308), calls=%async_computation.5 | async-start | bytes 2621440 | tf_op jit(solution)/shard_map/all_to_all | solution.py:216
  376.8 24.4 %copy-start.57 = (s32[256]{0:T(256)S(1)}, s32[256]{0:T(256)}, u32[]{:S(2)}) copy-start(s32[256]{0:T(256)} %constant.100.clone) | copy-start | bytes 3076
  397.2 8.8 %collective-permute-start.1 = (bf16[256,2048]{0,1:T(8,128)(2,1)}, bf16[256,2048]{0,1:T(8,128)(2,1)}, u32[]{:S(2)}, u32[]{:S(2)}) collective-permute-start(bf16[256,2048]{0,1:T(8,128)(2,1)} %copy.146), channel_id=1, source_target_pairs={{16,0},{17,1},{18,2},{19,3},{20,4},{21,5},{22,6},{23,7},{24,8},{25... | collective-permute-start | bytes 3145736 | tf_op jit(solution)/shard_map/ppermute | solution.py:555
  404.5 31.6 %collective-permute-start.2 = (bf16[640,1024]{1,0:T(8,128)(2,1)}, bf16[640,1024]{1,0:T(8,128)(2,1)}, u32[]{:S(2)}, u32[]{:S(2)}) collective-permute-start(bf16[640,1024]{1,0:T(8,128)(2,1)} %bitcast.301), channel_id=1, source_target_pairs={{0,8},{8,0},{1,9},{9,1},{2,10},{10,2},{3,11},{11,3},{4,12},{12,4},... | collective-permute-start | bytes 3932168 | tf_op jit(solution)/shard_map/ppermute | solution.py:616
  419.6 40.4 %all-to-all-start.6 = ((bf16[8,80,1024]{2,1,0:T(8,128)(2,1)}), bf16[8,80,1024]{2,1,0:T(8,128)(2,1)}, u32[]{:S(2)}, u32[]{:S(2)}) async-start(bf16[8,80,1024]{2,1,0:T(8,128)(2,1)} %bitcast.304), calls=%async_computation.6 | async-start | bytes 2621440 | tf_op jit(solution)/shard_map/all_to_all | solution.py:211
  447.8 9.4 %copy-start.46 = (f32[256]{0:T(256)S(1)}, f32[256]{0:T(256)}, u32[]{:S(2)}) copy-start(f32[256]{0:T(256)} %copy-done.45) | copy-start | bytes 3076
  475.7 12.5 %copy-start.32 = (bf16[640,2816]{1,0:T(8,128)(2,1)}, bf16[640,2816]{1,0:T(8,128)(2,1)S(1)}, u32[]{:S(2)}) copy-start(bf16[640,2816]{1,0:T(8,128)(2,1)S(1)} %get-tuple-element.93) | copy-start | bytes 10813444
  486.7 31.6 %collective-permute-start.3 = (bf16[640,1024]{1,0:T(8,128)(2,1)}, bf16[640,1024]{1,0:T(8,128)(2,1)}, u32[]{:S(2)}, u32[]{:S(2)}) collective-permute-start(bf16[640,1024]{1,0:T(8,128)(2,1)} %broadcast_select_fusion), channel_id=1, source_target_pairs={{0,8},{8,0},{1,9},{9,1},{2,10},{10,2},{3,11},{11,3},{4,12},{12,4},... | collective-permute-start | bytes 3932168 | tf_op jit(solution)/shard_map/ppermute | solution.py:617
  495.9 63.4 %all-to-all-start.7 = ((bf16[8,80,1024]{2,1,0:T(8,128)(2,1)}), bf16[8,80,1024]{2,1,0:T(8,128)(2,1)}, u32[]{:S(2)}, u32[]{:S(2)}) async-start(bf16[8,80,1024]{2,1,0:T(8,128)(2,1)} %bitcast.305), calls=%async_computation.7 | async-start | bytes 2621440 | tf_op jit(solution)/shard_map/all_to_all | solution.py:216
  500.4 18.0 %slice-start.3 = ((s8[5767168]{0:T(1024)(128)(4,1)}), s8[4194304]{0:T(1024)(128)(4,1)S(1)}, s32[]{:S(2)}) async-start(s8[5767168]{0:T(1024)(128)(4,1)} %bitcast.355), calls=%async_computation.11 | async-start | bytes 8388608
  505.6 12.8 %slice-start.4 = ((s8[5767168]{0:T(1024)(128)(4,1)}), s8[1572864]{0:T(1024)(128)(4,1)S(1)}, s32[]{:S(2)}) async-start(s8[5767168]{0:T(1024)(128)(4,1)} %bitcast.355), calls=%async_computation.12 | async-start | bytes 3145728
  508.8 13.1 %copy-start.63 = (f32[640,1408]{1,0:T(8,128)S(1)}, f32[640,1408]{1,0:T(8,128)}, u32[]{:S(2)}) copy-start(f32[640,1408]{1,0:T(8,128)} %fusion.78) | copy-start | bytes 10813444
  (55 other events, 241.1 us)

commit v3 on v2

--- a/solution.py
+++ b/solution.py
@@ -198,34 +198,16 @@
     return jnp.where(mine, back, kept_from[0]), jnp.where(mine, arrived, kept_from[1])
 
 
-def expert_parts(flat, flat_grad, w_in, w_down):
-    up = dot(flat, w_in[1])
-    value, slope = gelu_parts(dot(flat, w_in[0]))
-    hidden = (value * up).astype(BF16)
-    dhidden = dot(flat_grad, w_down, NT)
-    return (dhidden * up * slope).astype(BF16), (dhidden * value).astype(BF16), hidden
-
-
-def moe_backward(grad_send, received, w_in, w_down, turn, kept_from):
-    width = grad_send.shape[2]
-    arrived = lax.all_to_all(grad_send, "expert", split_axis=0, concat_axis=0, tiled=True)
-    flat_grad = arrived.reshape(-1, width)
-    flat = received.reshape(-1, width)
-    dgate, dup, hidden = expert_parts(flat, flat_grad, w_in, w_down)
-    drows = (dot(dgate, w_in[0], NT) + dot(dup, w_in[1], NT)).astype(BF16)
-    back = lax.all_to_all(
-        drows.reshape(arrived.shape), "expert", split_axis=0, concat_axis=0, tiled=True
-    )
-    out = (back, dgate, dup, hidden, flat_grad)
-    if kept_from is None:
-        return out
-    mine = lax.axis_index("half") == turn
-    return tuple(jnp.where(mine, a, b) for a, b in zip(out, kept_from))
-
-
 def flipped(value, bit):
     step = 1 << bit
     return value + step * (1 - 2 * (value // step % 2))
+
+
+def crossed(value, other):
+    for bit in range(other.bit_length()):
+        if other >> bit & 1:
+            value = flipped(value, bit)
+    return value
 
 
 def greet(partners):
@@ -233,6 +215,329 @@
     for partner in partners:
         pl.semaphore_signal(barrier, inc=1, device_id=partner, device_id_type=MESH)
     pl.semaphore_wait(barrier, len(partners))
+
+
+def remote(src, dst, out_sem, in_sem, device):
+    return pltpu.make_async_remote_copy(
+        src_ref=src,
+        dst_ref=dst,
+        send_sem=out_sem,
+        recv_sem=in_sem,
+        device_id=device,
+        device_id_type=MESH,
+    )
+
+
+def tile_loop(count, step, body):
+    @pl.loop(0, count // step)
+    def _(i):
+        body(pl.multiple_of(i * step, step), step)
+
+    if count % step:
+        body(count // step * step, count % step)
+
+
+def far_first(experts, group):
+    return [*range(group, experts), *range(1, group)]
+
+
+def expert_forward_kernel(turn, group, has_prev, *refs):
+    send_ref, w_in, w_down = refs[:3]
+    refs = refs[3 + 2 * has_prev :]
+    back_out, rows_out, wg, wu, wd, rows, back, made, hidden = refs[:9]
+    wsem, s1, r1, s2, r2, osem = refs[9:]
+    experts, block, width = send_ref.shape
+    ff = wd.shape[0]
+
+    @pl.when(lax.axis_index("half") == turn)
+    def _():
+        me = lax.axis_index("expert")
+        greet([{"expert": crossed(me, k)} for k in range(1, experts)])
+
+        def there(k):
+            partner = crossed(me, k)
+            return remote(send_ref.at[partner], rows.at[me], s1.at[k], r1.at[k], {"expert": partner})
+
+        def home(k):
+            partner = crossed(me, k)
+            return remote(made.at[partner], back.at[me], s2.at[k], r2.at[k], {"expert": partner})
+
+        for k in far_first(experts, group):
+            there(k).start()
+        loads = [
+            pltpu.make_async_copy(src, dst, wsem.at[i])
+            for i, (src, dst) in enumerate(((w_in.at[0], wg), (w_in.at[1], wu), (w_down, wd)))
+        ]
+        for load in loads:
+            load.start()
+        rows[me] = send_ref[me]
+        for part in range(experts // group):
+            for k in range(part * group, part * group + group):
+                if k:
+                    there(k).wait_recv()
+            base = crossed(me // group, part) * group
+            if part == 0:
+                loads[0].wait()
+                loads[1].wait()
+
+            def up_tile(start, size, base=base):
+                x = rows[pl.ds(base, group)].reshape(group * block, width)
+                cols = pl.ds(start, size)
+                value, _ = gelu_parts(dot(x, wg[:, cols]))
+                hidden[:, cols] = (value * dot(x, wu[:, cols])).astype(BF16)
+
+            tile_loop(ff, 256, up_tile)
+            if part == 0:
+                loads[2].wait()
+
+            def down_tile(start, size, base=base):
+                cols = pl.ds(start, size)
+                y = dot(hidden[...], wd[:, cols]).astype(BF16)
+                made[pl.ds(base, group), :, cols] = y.reshape(group, block, size)
+
+            tile_loop(width, 256, down_tile)
+            for k in range(part * group, part * group + group):
+                if k:
+                    home(k).start()
+        rows_copy = pltpu.make_async_copy(rows, rows_out, osem.at[0])
+        rows_copy.start()
+        back[me] = made[me]
+        for k in range(1, experts):
+            home(k).wait_recv()
+        back_copy = pltpu.make_async_copy(back, back_out, osem.at[1])
+        back_copy.start()
+        for k in range(1, experts):
+            there(k).wait_send()
+            home(k).wait_send()
+        rows_copy.wait()
+        back_copy.wait()
+
+
+def expert_backward_kernel(turn, group, has_prev, *refs):
+    send_ref, own_rows, w_in, w_down = refs[:4]
+    refs = refs[4 + 5 * has_prev :]
+    back_out, mixed_out, hidden_out, rows_out, grad_out = refs[:5]
+    wg, wu, wd, grads, back, made, rows_peer, grads_peer = refs[5:13]
+    hidden, dgate, dup = refs[13:16]
+    wsem, s1, r1, s2, r2, sx, rx, osem = refs[16:]
+    experts, block, width = send_ref.shape
+    ff = wd.shape[0]
+    span = ff // 2
+    total = experts * block
+    parts = experts // group
+
+    @pl.when(lax.axis_index("half") == turn)
+    def _():
+        me, dp = lax.axis_index("expert"), lax.axis_index("dp")
+        peer = {"dp": 1 - dp}
+        greet([{"expert": crossed(me, k)} for k in range(1, experts)] + [peer])
+
+        def there(k):
+            partner = crossed(me, k)
+            return remote(send_ref.at[partner], grads.at[me], s1.at[k], r1.at[k], {"expert": partner})
+
+        def home(k):
+            partner = crossed(me, k)
+            return remote(made.at[partner], back.at[me], s2.at[k], r2.at[k], {"expert": partner})
+
+        def base_of(part):
+            return crossed(me // group, part) * group
+
+        rows_over = remote(own_rows, rows_peer, sx.at[parts], rx.at[parts], peer)
+
+        def grads_over(part):
+            blocks = pl.ds(base_of(part), group)
+            return remote(grads.at[blocks], grads_peer.at[blocks], sx.at[part], rx.at[part], peer)
+
+        for k in far_first(experts, group):
+            there(k).start()
+        loads = [
+            pltpu.make_async_copy(src, dst, wsem.at[i])
+            for i, (src, dst) in enumerate(((w_in.at[0], wg), (w_in.at[1], wu), (w_down, wd)))
+        ]
+        for load in loads:
+            load.start()
+        rows_over.start()
+        grads[me] = send_ref[me]
+        loads[0].wait()
+        loads[1].wait()
+
+        def up_tile(start, size):
+            x = own_rows[...].reshape(total, width)
+            cols = pl.ds(start, size)
+            value, slope = gelu_parts(dot(x, wg[:, cols]))
+            up = dot(x, wu[:, cols])
+            hidden[:, cols] = (value * up).astype(BF16)
+            dup[:, cols] = value.astype(BF16)
+            dgate[:, cols] = (up * slope).astype(BF16)
+
+        tile_loop(ff, 256, up_tile)
+        loads[2].wait()
+        for part in range(parts):
+            for k in range(part * group, part * group + group):
+                if k:
+                    there(k).wait_recv()
+            grads_over(part).start()
+            base = base_of(part)
+            span_rows = pl.ds(pl.multiple_of(base * block, group * block), group * block)
+
+            def hidden_tile(start, size, base=base, span_rows=span_rows):
+                dy = grads[pl.ds(base, group)].reshape(group * block, width)
+                cols = pl.ds(start, size)
+                dhidden = dot(dy, wd[cols, :], NT)
+                dgate[span_rows, cols] = (dhidden * dgate[span_rows, cols].astype(F32)).astype(BF16)
+                dup[span_rows, cols] = (dhidden * dup[span_rows, cols].astype(F32)).astype(BF16)
+
+            tile_loop(ff, 256, hidden_tile)
+
+            def rows_tile(start, size, base=base, span_rows=span_rows):
+                cols = pl.ds(start, size)
+                dr = dot(dgate[span_rows, :], wg[cols, :], NT) + dot(dup[span_rows, :], wu[cols, :], NT)
+                made[pl.ds(base, group), :, cols] = dr.astype(BF16).reshape(group, block, size)
+
+            tile_loop(width, 256, rows_tile)
+            for k in range(part * group, part * group + group):
+                if k:
+                    home(k).start()
+        back[me] = made[me]
+        half_cols = pl.ds(pl.multiple_of(dp * span, 128), span)
+        outs = [
+            (dgate.at[:, half_cols], mixed_out.at[0, 0]),
+            (dup.at[:, half_cols], mixed_out.at[1, 0]),
+            (hidden.at[:, half_cols], hidden_out.at[0]),
+            (own_rows, rows_out.at[0]),
+            (grads, grad_out.at[0]),
+        ]
+        outs = [pltpu.make_async_copy(src, dst, osem.at[i]) for i, (src, dst) in enumerate(outs)]
+        for out in outs:
+            out.start()
+
+        rows_over.wait_recv()
+        for part in range(parts):
+            grads_over(part).wait_recv()
+
+        def peer_tile(start, size):
+            x = rows_peer[...].reshape(total, width)
+            dy = grads_peer[...].reshape(total, width)
+            here = pl.ds(pl.multiple_of((1 - dp) * span + start, 128), size)
+            cols = pl.ds(pl.multiple_of(dp * span + start, 128), size)
+            value, slope = gelu_parts(dot(x, wg[:, cols]))
+            up = dot(x, wu[:, cols])
+            dhidden = dot(dy, wd[cols, :], NT)
+            hidden[:, here] = (value * up).astype(BF16)
+            dgate[:, here] = (dhidden * up * slope).astype(BF16)
+            dup[:, here] = (dhidden * value).astype(BF16)
+
+        tile_loop(span, 256, peer_tile)
+        other_cols = pl.ds(pl.multiple_of((1 - dp) * span, 128), span)
+        peers = [
+            (dgate.at[:, other_cols], mixed_out.at[0, 1]),
+            (dup.at[:, other_cols], mixed_out.at[1, 1]),
+            (hidden.at[:, other_cols], hidden_out.at[1]),
+            (rows_peer, rows_out.at[1]),
+            (grads_peer, grad_out.at[1]),
+        ]
+        peers = [pltpu.make_async_copy(src, dst, osem.at[5 + i]) for i, (src, dst) in enumerate(peers)]
+        for out in peers:
+            out.start()
+        for k in range(1, experts):
+            home(k).wait_recv()
+        back_copy = pltpu.make_async_copy(back, back_out, osem.at[10])
+        back_copy.start()
+        for k in range(1, experts):
+            there(k).wait_send()
+            home(k).wait_send()
+        rows_over.wait_send()
+        for part in range(parts):
+            grads_over(part).wait_send()
+        for out in [*outs, *peers, back_copy]:
+            out.wait()
+
+
+def group_of(experts, block):
+    group = 1
+    while group * 2 * block <= 320 and group * 2 <= experts:
+        group *= 2
+    return group
+
+
+def expert_call(kernel, turn, inputs, weights, prev, out_shape, scratch, name):
+    experts, block, _ = inputs[0].shape
+    vmem, hbm = pl.BlockSpec(memory_space=pltpu.VMEM), pl.BlockSpec(memory_space=pl.ANY)
+    prev = list(prev or [])
+    first = len(inputs) + len(weights)
+    return pl.pallas_call(
+        functools.partial(kernel, turn, group_of(experts, block), bool(prev)),
+        in_specs=[vmem] * len(inputs) + [hbm] * (len(weights) + len(prev)),
+        out_specs=[hbm] * len(out_shape),
+        out_shape=out_shape,
+        input_output_aliases={first + i: i for i in range(len(prev))},
+        scratch_shapes=scratch,
+        compiler_params=pltpu.CompilerParams(
+            collective_id=1 + turn + 2 * (len(inputs) - 1),
+            has_side_effects=True,
+            vmem_limit_bytes=60 << 20,
+        ),
+        name=name,
+    )(*inputs, *weights, *prev)
+
+
+def moe_forward(send, w_in, w_down, turn, prev):
+    experts, block, width = send.shape
+    ff = w_down.shape[0]
+    group = group_of(experts, block)
+    dma = pltpu.SemaphoreType.DMA
+    scratch = [
+        pltpu.VMEM((width, ff), BF16),
+        pltpu.VMEM((width, ff), BF16),
+        pltpu.VMEM((ff, width), BF16),
+        *[pltpu.VMEM(send.shape, BF16)] * 3,
+        pltpu.VMEM((group * block, ff), BF16),
+        dma((3,)),
+        *[dma((experts,))] * 4,
+        dma((2,)),
+    ]
+    out_shape = [jax.ShapeDtypeStruct(send.shape, BF16)] * 2
+    return expert_call(
+        expert_forward_kernel, turn, [send], [w_in, w_down], prev, out_shape, scratch, "moe_forward"
+    )
+
+
+def moe_backward(grad_send, received, w_in, w_down, turn, prev):
+    experts, block, width = grad_send.shape
+    ff = w_down.shape[0]
+    total = experts * block
+    parts = experts // group_of(experts, block)
+    dma = pltpu.SemaphoreType.DMA
+    scratch = [
+        pltpu.VMEM((width, ff), BF16),
+        pltpu.VMEM((width, ff), BF16),
+        pltpu.VMEM((ff, width), BF16),
+        *[pltpu.VMEM(grad_send.shape, BF16)] * 5,
+        *[pltpu.VMEM((total, ff), BF16)] * 3,
+        dma((3,)),
+        *[dma((experts,))] * 4,
+        dma((parts + 1,)),
+        dma((parts + 1,)),
+        dma((11,)),
+    ]
+    out_shape = [
+        jax.ShapeDtypeStruct(grad_send.shape, BF16),
+        jax.ShapeDtypeStruct((2, 2, total, ff // 2), BF16),
+        jax.ShapeDtypeStruct((2, total, ff // 2), BF16),
+        jax.ShapeDtypeStruct((2, *grad_send.shape), BF16),
+        jax.ShapeDtypeStruct((2, *grad_send.shape), BF16),
+    ]
+    return expert_call(
+        expert_backward_kernel,
+        turn,
+        [grad_send, received],
+        [w_in, w_down],
+        prev,
+        out_shape,
+        scratch,
+        "moe_backward",
+    )
 
 
 def dense_kernel(starts, stages, ahead, *refs):
@@ -249,30 +554,20 @@
     bits = [me // (1 << k) % 2 for k in range(stages)]
     greet([peer] + partners)
 
-    def send(src, dst, out_sem, in_sem, device):
-        return pltpu.make_async_remote_copy(
-            src_ref=src,
-            dst_ref=dst,
-            send_sem=out_sem,
-            recv_sem=in_sem,
-            device_id=device,
-            device_id_type=MESH,
-        )
-
     def send_x(g):
         rows = pl.ds(pl.multiple_of((1 - dp) * half_rows, half_rows), half_rows)
-        return send(xt_ref.at[g, rows], xp.at[g], sx.at[g], rx.at[g], peer)
+        return remote(xt_ref.at[g, rows], xp.at[g], sx.at[g], rx.at[g], peer)
 
     def send_dy(c):
-        return send(dy_ref.at[c], dyp.at[c], sy.at[c], ry.at[c], peer)
+        return remote(dy_ref.at[c], dyp.at[c], sy.at[c], ry.at[c], peer)
 
     def send_small(step):
         src = small_ref if step == 0 else small_out.at[step - 1]
         device = peer if step == 0 else partners[step - 1]
-        return send(src, small_in.at[step], ss.at[step], rs.at[step], device)
+        return remote(src, small_in.at[step], ss.at[step], rs.at[step], device)
 
     def send_part(k, c):
-        return send(
+        return remote(
             sums[k].at[c, :, 1 - bits[k]], parts[k].at[c], sk.at[k, c], rk.at[k, c], partners[k]
         )
 
@@ -561,7 +856,7 @@
     dvalues, dgain_m = norm_back(final_enc, scale_m, gain[2], dnormed)
     grad = jnp.where(decoder, grad_dec, grad_dec + dvalues)
     dgates, grad_send = moe_gradient(grad)
-    back, dgate, dup, hidden, flat_grad = moe_backward(
+    back, mixed_grads, hidden, all_rows, all_grad = moe_backward(
         grad_send, received, w_in, w_down, 0, kept_from
     )
     grad_second, dgain_moe, drouter = moe_input_gradient(grad, dgates, back)
@@ -600,8 +895,7 @@
     )
     small = jnp.pad(small, ((0, -small.shape[0] % 8), (0, 0)))
     (dqkv, dout, dcross_a, dcross_b), small = dense_gradients(pairs, small, experts)
-    dp_index = lax.axis_index("dp")
-    place = dp_index * experts + lax.axis_index("expert")
+    place = lax.axis_index("dp") * experts + lax.axis_index("expert")
     own = width // (2 * experts)
     mine = lax.dynamic_slice_in_dim(small[: experts + 3], place * own, own, 1)
     tail = small[experts + 3]
@@ -609,23 +903,12 @@
     d_table = lax.dynamic_slice_in_dim(tail, place * own_table, own_table)
     counts = lax.dynamic_slice_in_dim(tail, dtable.shape[0] + place, 1).astype(jnp.int32)
 
-    swap = [(0, 1), (1, 0)]
-    ff = w_down.shape[0]
-    span = ff // 2
-    rows_own = received.reshape(-1, width)
-    rows_peer = lax.ppermute(rows_own, "dp", swap)
-    grad_peer = lax.ppermute(flat_grad, "dp", swap)
-    in_half = lax.dynamic_slice_in_dim(w_in, dp_index * span, span, 2)
-    down_half = lax.dynamic_slice_in_dim(w_down, dp_index * span, span, 0)
-    peer_parts = expert_parts(rows_peer, grad_peer, in_half, down_half)
-    own_parts = [
-        lax.dynamic_slice_in_dim(a, dp_index * span, span, 1) for a in (dgate, dup, hidden)
-    ]
-    dgate, dup, hidden = [jnp.concatenate(p) for p in zip(own_parts, peer_parts)]
-    all_rows = jnp.concatenate([rows_own, rows_peer])
-    all_grad = jnp.concatenate([flat_grad, grad_peer])
-    din = jnp.stack([dot(all_rows, dgate, TN), dot(all_rows, dup, TN)])
-    ddown = dot(hidden, all_grad, TN)
+    flat = all_rows.reshape(-1, width)
+    ff_half = hidden.shape[-1]
+    din = jnp.einsum(
+        "rd,grf->gdf", flat, mixed_grads.reshape(2, -1, ff_half), preferred_element_type=F32
+    )
+    ddown = dot(hidden.reshape(-1, ff_half), all_grad.reshape(-1, width), TN)
     return (
         outputs.reshape(1, seqs, length, width),
         d_tokens.reshape(1, seqs, length, width),

time: 760 us -> 534 us (0.70)
  matrix products: 218 us -> 83.9 us
  blocking collectives: 73.2 us -> 0 us
  Pallas kernels: 180 us -> 251 us
  other arithmetic: 61.8 us -> 27 us
  waiting for transfers between devices: 115 us -> 83 us
  starting transfers between devices: 33.5 us -> 4.02 us
    dot_general x41 -> x24, matrix products: 212 us -> 64.3 us  [dot(): return lax.dot_general(a, b, dims, preferred_element_type=F32)]
    pallas_call x0 -> x4, Pallas kernels: none -> 108 us  [expert_call(): pl.pallas_call(functools.partial(kernel, turn, group_of(experts, block),...]
    all_to_all x6 -> x0, waiting for transfers between devices: 95.7 us -> none  [the longest x2 54.6 us: moe_forward(): lax.all_to_all(result, 'expert', split_axis=0, concat_axis=0, tiled=True)]
    ppermute x1, waiting for transfers between devices: 0.01 us -> 83 us  [body(): dmemory = lax.ppermute(dmemory, names, back_pairs)]
    all_to_all x2 -> x0, blocking collectives: 73.2 us -> none  [moe_forward(): lax.all_to_all(send, 'expert', split_axis=0, concat_axis=0, tiled=True)]
    pallas_call x1, Pallas kernels: 114 us -> 76.7 us  [dense_gradients(): pl.pallas_call(functools.partial(dense_kernel, tuple(starts), stages, 4),...]
    all_to_all x6 -> x0, starting transfers between devices: 26.6 us -> none  [the longest x2 8.94 us: moe_backward(): lax.all_to_all(grad_send, 'expert', split_axis=0, concat_axis=0, tiled=True)]
    ppermute x2 -> x0, waiting for transfers between devices: 19.5 us -> none  [the longest x1 9.92 us: body(): rows_peer = lax.ppermute(rows_own, 'dp', swap)]
  transfers between devices with their start and end apart: 10 -> 2, of which waited for: 6 -> 1; matrix products, arithmetic and copies ran while one was open for 17% -> 3% of each run, Pallas kernels for 0% -> 0%
where the time goes in v3:
time: 534 us; the launch traced here: 525 us
  Pallas kernels  251 us (47%)
  matrix products  83.9 us (16%)
  waiting for transfers between devices  83 us (16%)
  local copies, waits for them, and re-layouts  74 us (14%)
  other arithmetic  27 us (5%)
    pallas_call x4, Pallas kernels, expert_call(): pl.pallas_call(functools.partial(kernel, turn, group_of(experts, block),...  108 us
    ppermute x1, waiting for transfers between devices, body(): dmemory = lax.ppermute(dmemory, names, back_pairs)  83 us
    pallas_call x1, Pallas kernels, dense_gradients(): pl.pallas_call(functools.partial(dense_kernel, tuple(starts), stages, 4),...  76.7 us
    dot_general x24, matrix products, dot(): return lax.dot_general(a, b, dims, preferred_element_type=F32)  64.3 us
    pallas_call x2, Pallas kernels, attend_back(): pl.pallas_call(functools.partial(attend_back_kernel, bias is not None), g...  37.9 us
    unnamed x129, local copies, waits for them, and re-layouts  30.2 us
    pallas_call x2, Pallas kernels, attend(): pl.pallas_call(functools.partial(attend_kernel, bias is not None), grid=(...  28.4 us
    dot_general x1, matrix products, body(): jnp.einsum('rd,grf->gdf', flat, mixed_grads.reshape(2, -1, ff_half), pref...  13.3 us
  transfers between devices with their start and end apart: 2, of which 1 were waited for; matrix products, arithmetic and copies ran while one was open for 3% of the time, Pallas kernels for 0%

profile of v3, /device:TPU:0, one launch (start us, length us, event | category | flops | bytes accessed | tf_op | source)
XLA Modules:
  0.0 525.3 jit_solution(15847379365704352550)
XLA Ops:
  12.7 5.7 %convolution_convert_fusion.refs_1_.refs_2_.refs_3_ = bf16[256,3072]{1,0:T(8,128)(2,1)} fusion(bf16[256,1024]{1,0:T(8,128)(2,1)S(1)} %bitcast.241, bf16[1,1024,3072]{2,1,0:T(8,128)(2,1)} %param.21), kind=kOutput, calls=%fused_computation.4 | convolution fusion | flops 1611399168 | bytes 8388608 | tf_op jit(solution)/shard_map/dot_general | solution.py:24
  18.4 14.3 %attend.2 = bf16[256,1024]{1,0:T(8,128)(2,1)} custom-call(s32[3]{0:T(128)} %pad_add_fusion.info, f32[16,256]{1,0:T(8,128)} %convolution_bitcast_fusion.3.refs_0_, bf16[256,3072]{1,0:T(8,128)(2,1)} %convolution_convert_fusion.refs_1_.refs_2_.refs_3_, bf16[256,3072]{1,0:T(8,128)(2,1)} %convolution_convert_fusion.refs_1_.refs_2_.refs_3_, ...), custom_call_target="tpu_custom_call" | custom-call | tf_op jit(solution)/shard_map/attend/pallas_call | solution.py:126
  37.5 47.1 %moe_forward.2 = (bf16[8,80,1024]{2,1,0:T(8,128)(2,1)}, bf16[8,80,1024]{2,1,0:T(8,128)(2,1)}) custom-call(bf16[8,80,1024]{2,1,0:T(8,128)(2,1)} %bitcast.220, bf16[2,1024,2816]{2,1,0:T(8,128)(2,1)} %bitcast.207, bf16[2816,1024]{1,0:T(8,128)(2,1)} %bitcast.211), custom_call_target="tpu_custom_call" | custom-call | tf_op jit(solution)/shard_map/moe_forward/pallas_call | solution.py:469
  84.6 3.4 multiply_reduce_fusion.3
  104.0 3.2 fusion.30.refs_0_
  107.2 14.2 %attend.3 = bf16[256,1024]{1,0:T(8,128)(2,1)} custom-call(s32[3]{0:T(128)} %pad_add_fusion.1.info, bf16[256,1024]{1,0:T(8,128)(2,1)} %fusion.30.refs_0_, bf16[256,2048]{1,0:T(8,128)(2,1)} %collective-permute-done.refs_1_.refs_2_, bf16[256,2048]{1,0:T(8,128)(2,1)} %collective-permute-done.refs_1_.refs_2_), custom_call_target="tpu_custom_call" | custom-call | tf_op jit(solution)/shard_map/attend/pallas_call | solution.py:126
  121.4 2.7 multiply_reduce_fusion.13
  128.3 4.1 multiply_reduce_fusion.1
  134.5 2.7 moe_backward.2
  144.6 18.1 %attend_back.2 = (bf16[256,1024]{1,0:T(8,128)(2,1)}, bf16[256,2048]{1,0:T(8,128)(2,1)}) custom-call(s32[3]{0:T(128)} %pad_add_fusion.1.info, bf16[256,1024]{1,0:T(8,128)(2,1)} %fusion.30.refs_0_, bf16[256,2048]{1,0:T(8,128)(2,1)} %collective-permute-done.refs_1_.refs_2_, bf16[256,2048]{1,0:T(8,128)(2,1)} %collective-permute-done.refs_1_.refs_2_, ...), custom_call_target="tpu_custom_call" | custom-call | tf_op jit(solution)/shard_map/attend_back/pallas_call | solution.py:155
  175.2 83.0 %collective-permute-done.1 = bf16[256,2048]{0,1:T(8,128)(2,1)} collective-permute-done((bf16[256,2048]{0,1:T(8,128)(2,1)}, bf16[256,2048]{0,1:T(8,128)(2,1)}, u32[]{:S(2)}, u32[]{:S(2)}) %collective-permute-start.1) | collective-permute-done | bytes 1048608 | tf_op jit(solution)/shard_map/ppermute | solution.py:850
  258.2 3.7 fusion.92
  269.0 3.4 bitcast_convert_fusion
  278.7 56.8 %moe_backward.3 = (bf16[8,80,1024]{2,1,0:T(8,128)(2,1)}, bf16[2,2,640,1408]{3,2,1,0:T(8,128)(2,1)}, bf16[2,640,1408]{2,1,0:T(8,128)(2,1)}, bf16[2,8,80,1024]{3,2,1,0:T(8,128)(2,1)}, bf16[2,8,80,1024]{3,2,1,0:T(8,128)(2,1)}) custom-call(bf16[8,80,1024]{2,1,0:T(8,128)(2,1)} %bitcast.231, ...), custom_call_target="tpu_custom_call", output_to_operand_aliasing={{0}: (4, {}), {1}: (5, {}), {2}: (6, {}), {3}: (7, {}), {4}... | custom-call | tf_op jit(solution)/shard_map/moe_backward/pallas_call | solution.py:469
  343.7 2.6 fusion.36.refs_4_
  349.0 19.8 %attend_back.3 = (bf16[256,1024]{1,0:T(8,128)(2,1)}, bf16[256,2048]{1,0:T(8,128)(2,1)}, f32[16,256]{1,0:T(8,128)}) custom-call(s32[3]{0:T(128)} %pad_add_fusion.info, f32[16,256]{1,0:T(8,128)} %convolution_bitcast_fusion.3.refs_0_, bf16[256,3072]{1,0:T(8,128)(2,1)} %convolution_convert_fusion.refs_1_.refs_2_.refs_3_, ...), custom_call_target="tpu_custom_call" | custom-call | tf_op jit(solution)/shard_map/attend_back/pallas_call | solution.py:155
  371.8 3.9 fusion
  384.9 4.6 copy.172
  389.5 4.7 copy.173
  394.2 2.8 pad_maximum_fusion.refs_0_
  397.0 76.7 %dense_gradients.1 = (f32[12,64,512]{2,1,0:T(8,128)}, f32[4,16,1024]{2,1,0:T(8,128)}) custom-call(bf16[4,1024,256]{2,1,0:T(8,128)(2,1)} %pad_maximum_fusion.refs_0_, bf16[12,256,512]{2,1,0:T(8,128)(2,1)} %bitcast.216, f32[16,1024]{1,0:T(8,128)} %pad.4.refs_2_), custom_call_target="tpu_custom_call" | custom-call | tf_op jit(solution)/shard_map/dense_gradients/pallas_call | solution.py:677
  483.6 13.3 %convolution_bitcast_fusion = f32[1,1,2,1024,1408]{3,4,2,1,0:T(8,128)} fusion(bf16[2,1280,1408]{2,1,0:T(8,128)(2,1)} %bitcast.219, bf16[1280,1024,1]{1,0,2:T(8,128)(2,1)} %bitcast.226), kind=kOutput, calls=%fused_computation | convolution fusion | flops 7381975040 | bytes 21364736 | tf_op jit(solution)/shard_map/rd,grf->gdf/dot_general | solution.py:908
  496.9 12.2 %copy.185 = f32[1,1,2,1024,1408]{4,3,2,1,0:T(8,128)} copy(f32[1,1,2,1024,1408]{3,4,2,1,0:T(8,128)} %convolution_bitcast_fusion) | data formatting | bytes 23068672
  515.4 9.4 %convolution_bitcast_fusion.1 = f32[1,1,1408,1024]{3,2,1,0:T(8,128)} fusion(bf16[1280,1408]{1,0:T(8,128)(2,1)} %bitcast.225, bf16[1280,1024]{1,0:T(8,128)(2,1)} %bitcast.227), kind=kOutput, calls=%fused_computation.1 | convolution fusion | flops 3690987520 | bytes 11993088 | tf_op jit(solution)/shard_map/dot_general | solution.py:24
  (238 shorter events, 110.9 us)
Async XLA Ops:
  0.6 32.0 %copy-start = (bf16[1,1024,1024]{2,1,0:T(8,128)(2,1)S(1)}, bf16[1,1024,1024]{2,1,0:T(8,128)(2,1)}, u32[]{:S(2)}) copy-start(bf16[1,1024,1024]{2,1,0:T(8,128)(2,1)} %param.22) | copy-start | bytes 6291460
  0.7 10.4 %copy-start.54 = (s32[256]{0:T(256)S(1)}, s32[256]{0:T(256)}, u32[]{:S(2)}) copy-start(s32[256]{0:T(256)} %constant.80.clone) | copy-start | bytes 3076
  0.7 10.4 %copy-start.55 = (s32[256]{0:T(256)S(1)}, s32[256]{0:T(256)}, u32[]{:S(2)}) copy-start(s32[256]{0:T(256)} %constant.79.clone) | copy-start | bytes 3076
  0.7 10.4 %copy-start.56 = (s32[256]{0:T(256)S(1)}, s32[256]{0:T(256)}, u32[]{:S(2)}) copy-start(s32[256]{0:T(256)} %constant.78.clone) | copy-start | bytes 3076
  0.7 10.4 %copy-start.57 = (s32[256]{0:T(256)S(1)}, s32[256]{0:T(256)}, u32[]{:S(2)}) copy-start(s32[256]{0:T(256)} %constant.77.clone) | copy-start | bytes 3076
  0.7 11.8 %copy-start.15 = (bf16[1,2,128,1024]{3,2,1,0:T(8,128)(2,1)S(1)}, bf16[1,2,128,1024]{3,2,1,0:T(8,128)(2,1)}, u32[]{:S(2)}) copy-start(bf16[1,2,128,1024]{3,2,1,0:T(8,128)(2,1)} %param.17) | copy-start | bytes 1572868
  0.7 9.7 %copy-start.52 = (s32[2,2]{1,0:T(2,128)S(1)}, s32[2,2]{1,0:T(2,128)}, u32[]{:S(2)}) copy-start(s32[2,2]{1,0:T(2,128)} %param.19) | copy-start | bytes 52
  5.3 13.2 %copy-start.38 = (f32[1,1,1024]{2,0,1:T(1,128)}, f32[1,1,1024]{2,0,1:T(1,128)S(1)}, u32[]{:S(2)}) copy-start(f32[1,1,1024]{2,0,1:T(1,128)S(1)} %get-tuple-element.129) | copy-start | bytes 12292
  96.5 10.7 %collective-permute-start = (bf16[256,2048]{1,0:T(8,128)(2,1)}, bf16[256,2048]{1,0:T(8,128)(2,1)}, u32[]{:S(2)}, u32[]{:S(2)}) collective-permute-start(bf16[256,2048]{1,0:T(8,128)(2,1)} %convolution_convert_fusion.1), channel_id=1, source_target_pairs={{0,16},{1,17},{2,18},{3,19},{4,20},{5,21},{6,22},{7,23},{8,24},{9,... | collective-permute-start | bytes 3145736 | tf_op jit(solution)/shard_map/ppermute | solution.py:805
  126.5 5.9 %copy-start.40 = (f32[256]{0:T(256)}, f32[256]{0:T(256)S(1)}, u32[]{:S(2)}) copy-start(f32[256]{0:T(256)S(1)} %fusion.82) | copy-start | bytes 3076
  126.6 5.8 %copy-start.42 = (f32[256]{0:T(256)}, f32[256]{0:T(256)S(1)}, u32[]{:S(2)}) copy-start(f32[256]{0:T(256)S(1)} %get-tuple-element.107) | copy-start | bytes 3076
  165.0 93.2 %collective-permute-start.1 = (bf16[256,2048]{0,1:T(8,128)(2,1)}, bf16[256,2048]{0,1:T(8,128)(2,1)}, u32[]{:S(2)}, u32[]{:S(2)}) collective-permute-start(bf16[256,2048]{0,1:T(8,128)(2,1)} %copy.159), channel_id=1, source_target_pairs={{16,0},{17,1},{18,2},{19,3},{20,4},{21,5},{22,6},{23,7},{24,8},{25... | collective-permute-start | bytes 3145736 | tf_op jit(solution)/shard_map/ppermute | solution.py:850
  168.7 93.3 %copy-start.50 = (f32[8]{0:T(128)}, f32[8]{0:T(128)S(1)}, u32[]{:S(2)}) copy-start(f32[8]{0:T(128)S(1)} %get-tuple-element.111) | copy-start | bytes 100
  175.2 86.8 %copy-start.8 = (f32[256,1024]{0,1:T(8,128)S(1)}, f32[256,1024]{0,1:T(8,128)}, u32[]{:S(2)}) copy-start(f32[256,1024]{0,1:T(8,128)} %copy-done.7) | copy-start | bytes 3145732
  175.2 86.8 %copy-start.32 = (bf16[1,1024,2048]{2,1,0:T(8,128)(2,1)S(1)}, bf16[1,1024,2048]{2,1,0:T(8,128)(2,1)}, u32[]{:S(2)}) copy-start(bf16[1,1024,2048]{2,1,0:T(8,128)(2,1)} %param.23) | copy-start | bytes 12582916
  175.2 86.8 %copy-start.36 = (bf16[256,1024]{1,0:T(8,128)(2,1)S(1)}, bf16[256,1024]{1,0:T(8,128)(2,1)}, u32[]{:S(2)}) copy-start(bf16[256,1024]{1,0:T(8,128)(2,1)} %get-tuple-element.37) | copy-start | bytes 1572868
  175.2 86.8 %copy-start.45 = (f32[256]{0:T(256)S(1)}, f32[256]{0:T(256)}, u32[]{:S(2)}) copy-start(f32[256]{0:T(256)} %copy-done.44) | copy-start | bytes 3076
  341.5 4.8 copy-start.13
  349.0 19.8 %copy-start.53 = (s32[256]{0:T(256)S(1)}, s32[256]{0:T(256)}, u32[]{:S(2)}) copy-start(s32[256]{0:T(256)} %get-tuple-element.149) | copy-start | bytes 3076
  389.5 4.7 copy-start.27
  475.4 5.1 copy-start.19
  496.9 14.7 %copy-start.34 = (f32[2,8,8,512]{3,2,1,0:T(8,128)S(1)}, f32[2,8,8,512]{3,2,1,0:T(8,128)}, u32[]{:S(2)}) copy-start(f32[2,8,8,512]{3,2,1,0:T(8,128)} %get-tuple-element.121) | copy-start | bytes 786436
  496.9 14.7 %copy-start.33 = (f32[2,8,8,512]{3,2,1,0:T(8,128)S(1)}, f32[2,8,8,512]{3,2,1,0:T(8,128)}, u32[]{:S(2)}) copy-start(f32[2,8,8,512]{3,2,1,0:T(8,128)} %get-tuple-element.122) | copy-start | bytes 786436
  515.4 9.4 %copy-start.1 = (bf16[1,1024,1024]{2,1,0:T(8,128)(2,1)S(1)}, bf16[1,1024,1024]{2,1,0:T(8,128)(2,1)}, u32[]{:S(2)}) copy-start(bf16[1,1024,1024]{2,1,0:T(8,128)(2,1)} %param.22) | copy-start | bytes 6291460
  (37 other events, 97.8 us)

commit v4 on v3

--- a/solution.py
+++ b/solution.py
@@ -58,7 +58,7 @@
     seq = pl.program_id(0)
     low = lax.broadcasted_iota(jnp.int32, (length, 128), 1) < 64
 
-    @pl.loop(0, width // 128)
+    @pl.loop(0, width // 128, unroll=True)
     def _(pair):
         cols = pl.ds(pl.multiple_of(pair * 128, 128), 128)
         q, k, v = q_ref[:, cols], k_ref[:, cols], v_ref[:, cols]
@@ -72,10 +72,12 @@
 
 def attend_back_kernel(has_bias, info, *refs):
     if has_bias:
-        bias_ref, q_ref, k_ref, v_ref, g_ref, dq_ref, dkv_ref, diag_ref = refs
+        bias_ref, q_ref, k_ref, v_ref, g_ref, dq_ref, diag_ref = refs
+        dkv_ref, shift = dq_ref, q_ref.shape[1]
     else:
         bias_ref = diag_ref = None
         q_ref, k_ref, v_ref, g_ref, dq_ref, dkv_ref = refs
+        shift = 0
     length, width = q_ref.shape
     seq = pl.program_id(0)
     low = lax.broadcasted_iota(jnp.int32, (length, 128), 1) < 64
@@ -88,7 +90,7 @@
         def _():
             diag_ref[...] = jnp.zeros_like(diag_ref)
 
-    @pl.loop(0, width // 128)
+    @pl.loop(0, width // 128, unroll=True)
     def _(pair):
         cols = pl.ds(pl.multiple_of(pair * 128, 128), 128)
         q, k, v, g = q_ref[:, cols], k_ref[:, cols], v_ref[:, cols], g_ref[:, cols]
@@ -110,8 +112,9 @@
                 turned = pltpu.roll(wide, 0, 1, stride=1, stride_axis=0)
                 diag_ref[pl.ds(head, 1), :] += jnp.sum(turned, axis=0, keepdims=True)
         dq_ref[:, cols] = (jnp.where(low, dqs[0], dqs[1]) * 0.125).astype(BF16)
-        dkv_ref[:, cols] = (jnp.where(low, dks[0], dks[1]) * 0.125).astype(BF16)
-        vcols = pl.ds(pl.multiple_of(width + pair * 128, 128), 128)
+        kcols = pl.ds(pl.multiple_of(shift + pair * 128, 128), 128)
+        dkv_ref[:, kcols] = (jnp.where(low, dks[0], dks[1]) * 0.125).astype(BF16)
+        vcols = pl.ds(pl.multiple_of(shift + width + pair * 128, 128), 128)
         dkv_ref[:, vcols] = jnp.where(low, dvs[0], dvs[1]).astype(BF16)
 
 
@@ -141,14 +144,9 @@
     ]
     lead = [] if bias is None else [pl.BlockSpec(bias.shape, lambda s: (0, 0))]
     args = [] if bias is None else [bias]
-    out_specs = [
-        pl.BlockSpec((length, width), lambda s: (s, 0)),
-        pl.BlockSpec((length, 2 * width), lambda s: (s, 0)),
-    ]
-    out_shape = [
-        jax.ShapeDtypeStruct((rows, width), BF16),
-        jax.ShapeDtypeStruct((rows, 2 * width), BF16),
-    ]
+    widths = (width, 2 * width) if bias is None else (3 * width,)
+    out_specs = [pl.BlockSpec((length, w), lambda s: (s, 0)) for w in widths]
+    out_shape = [jax.ShapeDtypeStruct((rows, w), BF16) for w in widths]
     if bias is not None:
         out_specs.append(pl.BlockSpec(bias.shape, lambda s: (0, 0)))
         out_shape.append(jax.ShapeDtypeStruct(bias.shape, F32))
@@ -286,7 +284,7 @@
                 value, _ = gelu_parts(dot(x, wg[:, cols]))
                 hidden[:, cols] = (value * dot(x, wu[:, cols])).astype(BF16)
 
-            tile_loop(ff, 256, up_tile)
+            tile_loop(ff, 512, up_tile)
             if part == 0:
                 loads[2].wait()
 
@@ -295,7 +293,7 @@
                 y = dot(hidden[...], wd[:, cols]).astype(BF16)
                 made[pl.ds(base, group), :, cols] = y.reshape(group, block, size)
 
-            tile_loop(width, 256, down_tile)
+            tile_loop(width, 512, down_tile)
             for k in range(part * group, part * group + group):
                 if k:
                     home(k).start()
@@ -371,7 +369,7 @@
             dup[:, cols] = value.astype(BF16)
             dgate[:, cols] = (up * slope).astype(BF16)
 
-        tile_loop(ff, 256, up_tile)
+        tile_loop(ff, 512, up_tile)
         loads[2].wait()
         for part in range(parts):
             for k in range(part * group, part * group + group):
@@ -388,14 +386,14 @@
                 dgate[span_rows, cols] = (dhidden * dgate[span_rows, cols].astype(F32)).astype(BF16)
                 dup[span_rows, cols] = (dhidden * dup[span_rows, cols].astype(F32)).astype(BF16)
 
-            tile_loop(ff, 256, hidden_tile)
+            tile_loop(ff, 512, hidden_tile)
 
             def rows_tile(start, size, base=base, span_rows=span_rows):
                 cols = pl.ds(start, size)
                 dr = dot(dgate[span_rows, :], wg[cols, :], NT) + dot(dup[span_rows, :], wu[cols, :], NT)
                 made[pl.ds(base, group), :, cols] = dr.astype(BF16).reshape(group, block, size)
 
-            tile_loop(width, 256, rows_tile)
+            tile_loop(width, 512, rows_tile)
             for k in range(part * group, part * group + group):
                 if k:
                     home(k).start()
@@ -428,7 +426,7 @@
             dgate[:, here] = (dhidden * up * slope).astype(BF16)
             dup[:, here] = (dhidden * value).astype(BF16)
 
-        tile_loop(span, 256, peer_tile)
+        tile_loop(span, 512, peer_tile)
         other_cols = pl.ds(pl.multiple_of((1 - dp) * span, 128), span)
         peers = [
             (dgate.at[:, other_cols], mixed_out.at[0, 1]),
@@ -540,78 +538,88 @@
     )
 
 
-def dense_kernel(starts, stages, ahead, *refs):
-    xt_ref, dy_ref, small_ref, out_ref, small_out = refs[:5]
-    xp, dyp, small_in = refs[5:8]
-    sums = refs[8 : 8 + stages]
-    parts = refs[8 + stages : 8 + 2 * stages]
-    sx, rx, sy, ry, ss, rs, sk, rk = refs[8 + 2 * stages :]
-    chunks = dy_ref.shape[0]
-    half_rows = xp.shape[1]
+def dense_kernel(stages, chunk, *refs):
+    xt_ref, own_refs, peer_refs, small_ref, out_ref, small_out, small_in = (
+        refs[0], refs[1:4], refs[4:7], refs[7], refs[8], refs[9], refs[10],
+    )
+    sums = refs[11 : 11 + stages]
+    parts = refs[11 + stages : 11 + 2 * stages]
+    ss, rs, sk, rk = refs[11 + 2 * stages :]
+    counts = [ref.shape[1] // chunk for ref in own_refs]
+    starts = [sum(counts[:i]) for i in range(3)]
+    chunks = sum(counts)
+    per_cross = counts[2] // 2
+    half = xt_ref.shape[2] // 2
     dp, me = lax.axis_index("dp"), lax.axis_index("expert")
     peer = {"dp": 1 - dp}
-    partners = [{"expert": flipped(me, k)} for k in range(stages)]
+    partners = [flipped(me, k) for k in range(stages)]
     bits = [me // (1 << k) % 2 for k in range(stages)]
-    greet([peer] + partners)
-
-    def send_x(g):
-        rows = pl.ds(pl.multiple_of((1 - dp) * half_rows, half_rows), half_rows)
-        return remote(xt_ref.at[g, rows], xp.at[g], sx.at[g], rx.at[g], peer)
-
-    def send_dy(c):
-        return remote(dy_ref.at[c], dyp.at[c], sy.at[c], ry.at[c], peer)
+    greet([peer] + [{"expert": p} for p in partners])
 
     def send_small(step):
         src = small_ref if step == 0 else small_out.at[step - 1]
-        device = peer if step == 0 else partners[step - 1]
+        device = peer if step == 0 else {"expert": partners[step - 1]}
         return remote(src, small_in.at[step], ss.at[step], rs.at[step], device)
 
+    def picked(k, c, values):
+        if k > 1:
+            return values[k]
+        odd = lax.rem(c, 2)
+        return values[k] + odd * (values[1 - k] - values[k])
+
+    def send_first(c, odd):
+        src = sums[0].at[c, :, 1 - bits[1]] if odd else sums[0].at[c, :, :, 1 - bits[0]]
+        return remote(src, parts[0].at[c], sk.at[0, c], rk.at[0, c], {"expert": partners[odd]})
+
     def send_part(k, c):
-        return remote(
-            sums[k].at[c, :, 1 - bits[k]], parts[k].at[c], sk.at[k, c], rk.at[k, c], partners[k]
-        )
+        src = sums[k].at[c, :, 1 - picked(k, c, bits)]
+        return remote(src, parts[k].at[c], sk.at[k, c], rk.at[k, c], {"expert": picked(k, c, partners)})
+
+    def by_parity(c, body):
+        for odd in range(2):
+
+            @pl.when(lax.rem(c, 2) == odd)
+            def _(odd=odd):
+                body(odd)
 
     send_small(0).start()
-    for g in range(len(starts)):
-        send_x(g).start()
-        if g == 0:
-            for c in range(ahead):
-                send_dy(c).start()
 
     def step(i, carry):
-        @pl.when(i < chunks)
-        def _():
-            @pl.when(i + ahead < chunks)
-            def _():
-                send_dy(i + ahead).start()
-
-            group = jnp.int32(0)
-            for g, first in enumerate(starts):
-                if g:
-                    group = group + (i >= first).astype(jnp.int32)
-
-                @pl.when(i == first)
-                def _(g=g):
-                    send_x(g).wait_recv()
-
-            send_dy(i).wait_recv()
-            rows = pl.ds(pl.multiple_of(dp * half_rows, half_rows), half_rows)
-            total = dot(xt_ref[group, rows], dy_ref[i]) + dot(xp[group], dyp[i])
-            sums[0][i] = total.astype(BF16).reshape(sums[0].shape[1:])
-            send_part(0, i).start()
+        for g in range(3):
+
+            @pl.when((i >= starts[g]) & (i < starts[g] + counts[g]))
+            def _(g=g):
+                c = i - starts[g]
+                cols = pl.ds(pl.multiple_of(c * chunk, chunk), chunk)
+                which = g if g < 2 else 2 + c // per_cross
+                total = dot(xt_ref[which, :, :half], own_refs[g][:, cols])
+                total += dot(xt_ref[which, :, half:], peer_refs[g][:, cols])
+                sums[0][i] = total.astype(BF16).reshape(sums[0].shape[1:])
+                by_parity(i, lambda odd: send_first(i, odd).start())
 
         for k in range(stages):
             c = i - 1 - k
 
             @pl.when((c >= 0) & (c < chunks))
             def _(k=k, c=c):
-                send_part(k, c).wait_recv()
-                total = sums[k][c, :, bits[k]].astype(F32) + parts[k][c].astype(F32)
-                if k + 1 < stages:
-                    sums[k + 1][c] = total.astype(BF16).reshape(sums[k + 1].shape[1:])
-                    send_part(k + 1, c).start()
+                def add(mine):
+                    total = mine.astype(F32) + parts[k][c].astype(F32)
+                    if k + 1 < stages:
+                        sums[k + 1][c] = total.astype(BF16).reshape(sums[k + 1].shape[1:])
+                        send_part(k + 1, c).start()
+                    else:
+                        out_ref[c] = total.reshape(out_ref.shape[1:])
+
+                if k == 0:
+
+                    def first(odd):
+                        send_first(c, odd).wait_recv()
+                        add(sums[0][c, :, bits[1]] if odd else sums[0][c, :, :, bits[0]])
+
+                    by_parity(c, first)
                 else:
-                    out_ref[c] = total[0]
+                    send_part(k, c).wait_recv()
+                    add(sums[k][c, :, picked(k, c, bits)])
 
         for j in range(stages + 1):
 
@@ -628,58 +636,48 @@
     lax.fori_loop(0, chunks + stages, step, 0)
 
     def finish(c, carry):
-        send_dy(c).wait_send()
-        for k in range(stages):
+        by_parity(c, lambda odd: send_first(c, odd).wait_send())
+        for k in range(1, stages):
             send_part(k, c).wait_send()
         return carry
 
     lax.fori_loop(0, chunks, finish, 0)
-    for g in range(len(starts)):
-        send_x(g).wait_send()
     for j in range(stages + 1):
         send_small(j).wait_send()
 
 
-def dense_gradients(pairs, small, experts):
+def over_dp(array):
+    return lax.ppermute(array, "dp", [(0, 1), (1, 0)])
+
+
+def both_halves(x):
+    half = x.shape[1] // 2
+    dp = lax.axis_index("dp")
+    own = lax.dynamic_slice_in_dim(x, dp * half, half, 1)
+    other = lax.dynamic_slice_in_dim(x, (1 - dp) * half, half, 1)
+    return own, other
+
+
+def dense_gradients(xt, own, peer, small, experts):
     chunk = 512
-    rows, width = pairs[0][0].shape
-    xt = jnp.stack([jnp.transpose(x) for x, _ in pairs])
-    dy = jnp.concatenate([y for _, y in pairs], axis=1)
-    chunks = dy.shape[1] // chunk
-    dy = jnp.transpose(dy.reshape(rows, chunks, chunk), (1, 0, 2))
-    starts, at = [], 0
-    for _, y in pairs:
-        starts.append(at)
-        at += y.shape[1] // chunk
+    half_rows = xt.shape[1]
+    chunks = sum(y.shape[1] for y in own) // chunk
     stages = experts.bit_length() - 1
-    own = width // (2 * experts)
+    keep = half_rows // experts
     vmem = pl.BlockSpec(memory_space=pltpu.VMEM)
     dma = pltpu.SemaphoreType.DMA
-    scratch = [
-        pltpu.VMEM((len(pairs), width // 2, rows), BF16),
-        pltpu.VMEM(dy.shape, BF16),
-        pltpu.VMEM((stages + 1, *small.shape), F32),
-    ]
-    scratch += [
-        pltpu.VMEM((chunks, experts >> (k + 1), 2, own, chunk), BF16) for k in range(stages)
-    ]
-    scratch += [pltpu.VMEM((chunks, experts >> (k + 1), own, chunk), BF16) for k in range(stages)]
-    scratch += [
-        dma((len(pairs),)),
-        dma((len(pairs),)),
-        dma((chunks,)),
-        dma((chunks,)),
-        dma((stages + 1,)),
-        dma((stages + 1,)),
-        dma((stages, chunks)),
-        dma((stages, chunks)),
-    ]
+    blocks = [(experts // 4, 2, 2)] + [(experts >> (k + 1), 2) for k in range(1, stages)]
+    scratch = [pltpu.VMEM((stages + 1, *small.shape), F32)]
+    scratch += [pltpu.VMEM((chunks, *b, keep, chunk), BF16) for b in blocks]
+    halved = [(experts // 4, 2)] + [(experts >> (k + 1),) for k in range(1, stages)]
+    scratch += [pltpu.VMEM((chunks, *b, keep, chunk), BF16) for b in halved]
+    scratch += [dma((stages + 1,)), dma((stages + 1,)), dma((stages, chunks)), dma((stages, chunks))]
     out, sums = pl.pallas_call(
-        functools.partial(dense_kernel, tuple(starts), stages, 4),
-        in_specs=[vmem] * 3,
+        functools.partial(dense_kernel, stages, chunk),
+        in_specs=[vmem] * 8,
         out_specs=[vmem] * 2,
         out_shape=[
-            jax.ShapeDtypeStruct((chunks, own, chunk), F32),
+            jax.ShapeDtypeStruct((chunks, keep, chunk), F32),
             jax.ShapeDtypeStruct((stages + 1, *small.shape), F32),
         ],
         scratch_shapes=scratch,
@@ -687,13 +685,50 @@
             collective_id=0, has_side_effects=True, vmem_limit_bytes=56 << 20
         ),
         name="dense_gradients",
-    )(xt, dy, small)
-    results = []
-    for (_, y), first in zip(pairs, starts):
+    )(xt, *own, *peer, small)
+    results, at = [], 0
+    for y in own:
         count = y.shape[1] // chunk
-        part = jnp.transpose(out[first : first + count], (1, 0, 2))
-        results.append(part.reshape(own, count * chunk))
+        part = jnp.transpose(out[at : at + count], (1, 0, 2))
+        results.append(part.reshape(keep, count * chunk))
+        at += count
     return results, sums[stages]
+
+
+def product_kernel(x_ref, y_ref, out_ref):
+    out_ref[...] = dot(x_ref[...], y_ref[...].reshape(y_ref.shape[-2:]), TN).reshape(out_ref.shape)
+
+
+def expert_gradients(rows, mixed, hidden, grads):
+    total, width = rows.shape
+    span = hidden.shape[1]
+    tile = 256
+    params = pltpu.CompilerParams(vmem_limit_bytes=40 << 20)
+    din = pl.pallas_call(
+        product_kernel,
+        grid=(2, width // tile),
+        in_specs=[
+            pl.BlockSpec((total, tile), lambda g, i: (0, i)),
+            pl.BlockSpec((1, total, span), lambda g, i: (g, 0, 0)),
+        ],
+        out_specs=pl.BlockSpec((1, tile, span), lambda g, i: (g, i, 0)),
+        out_shape=jax.ShapeDtypeStruct((2, width, span), F32),
+        compiler_params=params,
+        name="expert_in_gradient",
+    )(rows, mixed)
+    ddown = pl.pallas_call(
+        product_kernel,
+        grid=(pl.cdiv(span, tile),),
+        in_specs=[
+            pl.BlockSpec((total, tile), lambda i: (0, i)),
+            pl.BlockSpec((total, width), lambda i: (0, 0)),
+        ],
+        out_specs=pl.BlockSpec((tile, width), lambda i: (i, 0)),
+        out_shape=jax.ShapeDtypeStruct((span, width), F32),
+        compiler_params=params,
+        name="expert_out_gradient",
+    )(hidden, grads)
+    return din, ddown
 
 
 def body(
@@ -864,8 +899,8 @@
 
     dbranch = grad_first.astype(BF16)
     dmixed = dot(dbranch, wout, NT).astype(BF16)
-    dq, dkv, diag = attend_back(self_info, bias, qkv, qkv, (0, 1, 2), dmixed, length, width)
-    dnormed = dot(dq, wqkv[:, :width], NT) + dot(dkv, wqkv[:, width:], NT)
+    dqkv_rows, diag = attend_back(self_info, bias, qkv, qkv, (0, 1, 2), dmixed, length, width)
+    dnormed = dot(dqkv_rows, wqkv, NT)
     dvalues, dgain_self = norm_back(values, scale0, gain[0], dnormed)
     d_tokens = (grad_first + dvalues).astype(BF16)
     dtable = lax.dot_general(
@@ -873,16 +908,17 @@
         preferred_element_type=F32,
     ).reshape(-1)
 
-    left = jnp.where(decoder, low_c, low_m)
-    right = jnp.where(decoder, dquery, dmemory[:, :width])
-    left_out = jnp.where(decoder, mixed_c, low_m)
-    right_out = jnp.where(decoder, dbranch_c, dmemory[:, width:])
-    pairs = [
-        (low0, jnp.concatenate([dq, dkv], axis=1)),
-        (mixed0, dbranch),
-        (left, right),
-        (left_out, right_out),
-    ]
+    cross_grad = jnp.where(decoder, jnp.concatenate([dquery, dbranch_c], axis=1), dmemory)
+    owns, others = zip(
+        *map(
+            both_halves,
+            (low0, mixed0, jnp.where(decoder, low_c, low_m), jnp.where(decoder, mixed_c, low_m)),
+        )
+    )
+    lefts = jnp.concatenate([jnp.stack(owns), over_dp(jnp.stack(others))], axis=1)
+    xt = jnp.transpose(lefts, (0, 2, 1))
+    own_grads = (dqkv_rows, dbranch, cross_grad)
+    peer_grads = tuple(map(over_dp, own_grads))
     extra = jnp.concatenate([dtable, tallies, jnp.zeros((width - dtable.shape[0] - tallies.shape[0],), F32)])
     small = jnp.concatenate(
         [
@@ -894,7 +930,7 @@
         ]
     )
     small = jnp.pad(small, ((0, -small.shape[0] % 8), (0, 0)))
-    (dqkv, dout, dcross_a, dcross_b), small = dense_gradients(pairs, small, experts)
+    (dqkv, dout, dcross), small = dense_gradients(xt, own_grads, peer_grads, small, experts)
     place = lax.axis_index("dp") * experts + lax.axis_index("expert")
     own = width // (2 * experts)
     mine = lax.dynamic_slice_in_dim(small[: experts + 3], place * own, own, 1)
@@ -903,18 +939,19 @@
     d_table = lax.dynamic_slice_in_dim(tail, place * own_table, own_table)
     counts = lax.dynamic_slice_in_dim(tail, dtable.shape[0] + place, 1).astype(jnp.int32)
 
-    flat = all_rows.reshape(-1, width)
     ff_half = hidden.shape[-1]
-    din = jnp.einsum(
-        "rd,grf->gdf", flat, mixed_grads.reshape(2, -1, ff_half), preferred_element_type=F32
-    )
-    ddown = dot(hidden.reshape(-1, ff_half), all_grad.reshape(-1, width), TN)
+    din, ddown = expert_gradients(
+        all_rows.reshape(-1, width),
+        mixed_grads.reshape(2, -1, ff_half),
+        hidden.reshape(-1, ff_half),
+        all_grad.reshape(-1, width),
+    )
     return (
         outputs.reshape(1, seqs, length, width),
         d_tokens.reshape(1, seqs, length, width),
         dqkv[None],
         dout[None],
-        jnp.concatenate([dcross_a, dcross_b], axis=1)[None],
+        dcross[None],
         jnp.transpose(mine[:experts])[None],
         mine[experts:][None],
         d_table[None],

time: 534 us -> 470 us (0.88)
  local copies, waits for them, and re-layouts: 74 us -> 43 us
  matrix products: 83.9 us -> 56.7 us
  waiting for transfers between devices: 83 us -> 59.6 us
  Pallas kernels: 251 us -> 265 us
    ppermute x1, waiting for transfers between devices: 83 us -> 59.6 us  [body(): dmemory = lax.ppermute(dmemory, names, back_pairs)]
    unnamed x129 -> x111, local copies, waits for them, and re-layouts: 30.2 us -> 11.9 us
    another operation x0 -> x10, local copies, waits for them, and re-layouts: none -> 13.7 us  [the longest x6 7.15 us: body(): jnp.stack(owns)]
    pallas_call x1 -> x3, Pallas kernels: 76.7 us -> 89.9 us  [the longest x1 71.8 us: dense_gradients(): pl.pallas_call(functools.partial(dense_kernel, stages, chunk), in_specs=[...]
    dot_general x1 -> x0, matrix products: 13.3 us -> none  [body(): jnp.einsum('rd,grf->gdf', flat, mixed_grads.reshape(2, -1, ff_half), pref...]
    dot_general x24 -> x22, matrix products: 64.3 us -> 52 us  [dot(): return lax.dot_general(a, b, dims, preferred_element_type=F32)]
    pallas_call x4 -> x0, local copies, waits for them, and re-layouts: 8.39 us -> none  [the longest x2 4.3 us: attend_back(): pl.pallas_call(functools.partial(attend_back_kernel, bias is not None), g...]
    pallas_call x4, Pallas kernels: 108 us -> 117 us  [expert_call(): pl.pallas_call(functools.partial(kernel, turn, group_of(experts, block),...]
  transfers between devices with their start and end apart: 2 -> 6, of which waited for: 1 -> 1; matrix products, arithmetic and copies ran while one was open for 3% -> 10% of each run, Pallas kernels for 0% -> 8%
where the time goes in v4:
time: 470 us; the launch traced here: 462 us
  Pallas kernels  265 us (56%)
  waiting for transfers between devices  59.6 us (13%)
  matrix products  56.7 us (12%)
  local copies, waits for them, and re-layouts  43 us (9%)
  other arithmetic  28.5 us (6%)
  starting transfers between devices  7.73 us (2%)
    pallas_call x4, Pallas kernels, expert_call(): pl.pallas_call(functools.partial(kernel, turn, group_of(experts, block),...  117 us
    pallas_call x1, Pallas kernels, dense_gradients(): pl.pallas_call(functools.partial(dense_kernel, stages, chunk), in_specs=[...  71.8 us
    ppermute x1, waiting for transfers between devices, body(): dmemory = lax.ppermute(dmemory, names, back_pairs)  59.6 us
    dot_general x22, matrix products, dot(): return lax.dot_general(a, b, dims, preferred_element_type=F32)  52 us
    pallas_call x2, Pallas kernels, attend_back(): pl.pallas_call(functools.partial(attend_back_kernel, bias is not None), g...  33.2 us
    pallas_call x2, Pallas kernels, attend(): pl.pallas_call(functools.partial(attend_kernel, bias is not None), grid=(...  24.8 us
    unnamed x111, local copies, waits for them, and re-layouts  11.9 us
    pallas_call x1, Pallas kernels, expert_gradients(): pl.pallas_call(product_kernel, grid=(2, width // tile), in_specs=[pl.Bloc...  11.6 us
  transfers between devices with their start and end apart: 6, of which 1 were waited for; matrix products, arithmetic and copies ran while one was open for 10% of the time, Pallas kernels for 8%

profile of v4, /device:TPU:0, one launch (start us, length us, event | category | flops | bytes accessed | tf_op | source)
XLA Modules:
  0.0 461.7 jit_solution(4462104912523545138)
XLA Ops:
  12.8 5.7 %fusion.4.refs_1_.refs_2_.refs_3_ = bf16[256,3072]{1,0:T(8,128)(2,1)} fusion(bf16[256,1024]{1,0:T(8,128)(2,1)S(1)} %bitcast.237, bf16[1,1024,3072]{2,1,0:T(8,128)(2,1)} %param.21), kind=kOutput, calls=%fused_computation.4 | convolution fusion | flops 1611399168 | bytes 8388608 | tf_op jit(solution)/shard_map/dot_general | solution.py:24
  18.5 12.4 %attend.2 = bf16[256,1024]{1,0:T(8,128)(2,1)} custom-call(s32[3]{0:T(128)} %pad_add_fusion.info, f32[16,256]{1,0:T(8,128)} %convolution_bitcast_fusion.1.refs_0_, bf16[256,3072]{1,0:T(8,128)(2,1)} %fusion.4.refs_1_.refs_2_.refs_3_, bf16[256,3072]{1,0:T(8,128)(2,1)} %fusion.4.refs_1_.refs_2_.refs_3_, bf16[256,3072]{1,0:T(8,128)(2,1)} %fusion.4.refs_1_.refs_2_.refs_3_), custom_call_target="tpu_custom_call" | custom-call | tf_op jit(solution)/shard_map/attend/pallas_call | solution.py:129
  35.4 44.2 %moe_forward.2 = (bf16[8,80,1024]{2,1,0:T(8,128)(2,1)}, bf16[8,80,1024]{2,1,0:T(8,128)(2,1)}) custom-call(bf16[8,80,1024]{2,1,0:T(8,128)(2,1)} %bitcast.228, bf16[2,1024,2816]{2,1,0:T(8,128)(2,1)} %bitcast.214, bf16[2816,1024]{1,0:T(8,128)(2,1)} %bitcast.218), custom_call_target="tpu_custom_call" | custom-call | tf_op jit(solution)/shard_map/moe_forward/pallas_call | solution.py:467
  79.6 2.5 multiply_reduce_fusion.3
  87.1 2.4 collective-permute-start
  97.7 3.2 fusion.30.refs_0_
  100.9 12.3 %attend.3 = bf16[256,1024]{1,0:T(8,128)(2,1)} custom-call(s32[3]{0:T(128)} %pad_add_fusion.1.info, bf16[256,1024]{1,0:T(8,128)(2,1)} %fusion.30.refs_0_, bf16[256,2048]{1,0:T(8,128)(2,1)} %collective-permute-done.refs_1_.refs_2_, bf16[256,2048]{1,0:T(8,128)(2,1)} %collective-permute-done.refs_1_.refs_2_), custom_call_target="tpu_custom_call" | custom-call | tf_op jit(solution)/shard_map/attend/pallas_call | solution.py:129
  113.2 2.8 multiply_reduce_fusion.13
  120.1 4.1 multiply_reduce_fusion.1
  126.3 9.7 %moe_backward.2 = (bf16[8,80,1024]{2,1,0:T(8,128)(2,1)}, bf16[2,2,640,1408]{3,2,1,0:T(8,128)(2,1)}, bf16[2,640,1408]{2,1,0:T(8,128)(2,1)}, bf16[2,8,80,1024]{3,2,1,0:T(8,128)(2,1)}, bf16[2,8,80,1024]{3,2,1,0:T(8,128)(2,1)}) custom-call(bf16[8,80,1024]{2,1,0:T(8,128)(2,1)} %bitcast.233, bf16[8,80,1024]{2,1,0:T(8,128)(2,1)} %get-tuple-element.34.refs_1_, ...), custom_call_target="tpu_custom_call" | custom-call | tf_op jit(solution)/shard_map/moe_backward/pallas_call | solution.py:467
  142.3 15.3 %attend_back.2 = (bf16[256,1024]{1,0:T(8,128)(2,1)}, bf16[256,2048]{1,0:T(8,128)(2,1)}) custom-call(s32[3]{0:T(128)} %pad_add_fusion.1.info, bf16[256,1024]{1,0:T(8,128)(2,1)} %fusion.30.refs_0_, bf16[256,2048]{1,0:T(8,128)(2,1)} %collective-permute-done.refs_1_.refs_2_, bf16[256,2048]{1,0:T(8,128)(2,1)} %collective-permute-done.refs_1_.refs_2_, ...), custom_call_target="tpu_custom_call" | custom-call | tf_op jit(solution)/shard_map/attend_back/pallas_call | solution.py:153
  171.7 59.6 %collective-permute-done.1 = bf16[256,2048]{1,0:T(8,128)(2,1)} collective-permute-done((bf16[256,2048]{1,0:T(8,128)(2,1)}, bf16[256,2048]{1,0:T(8,128)(2,1)}, u32[]{:S(2)}, u32[]{:S(2)}) %collective-permute-start.1) | collective-permute-done | bytes 1048608 | tf_op jit(solution)/shard_map/ppermute | solution.py:885
  231.3 3.8 fusion.90
  235.2 2.7 multiply_reduce_fusion.5
  241.7 61.1 %moe_backward.3 = (bf16[8,80,1024]{2,1,0:T(8,128)(2,1)}, bf16[2,2,640,1408]{3,2,1,0:T(8,128)(2,1)}, bf16[2,640,1408]{2,1,0:T(8,128)(2,1)}, bf16[2,8,80,1024]{3,2,1,0:T(8,128)(2,1)}, bf16[2,8,80,1024]{3,2,1,0:T(8,128)(2,1)}) custom-call(bf16[8,80,1024]{2,1,0:T(8,128)(2,1)} %bitcast.232, ...), custom_call_target="tpu_custom_call", output_to_operand_aliasing={{0}: (4, {}), {1}: (5, {}), {2}: (6, {}), {3}: (7, {}), {4}... | custom-call | tf_op jit(solution)/shard_map/moe_backward/pallas_call | solution.py:467
  308.9 2.7 fusion.36.refs_4_
  311.6 2.6 maximum_select_fusion.refs_3_
  316.2 17.9 %attend_back.3 = (bf16[256,3072]{1,0:T(8,128)(2,1)}, f32[16,256]{1,0:T(8,128)}) custom-call(s32[3]{0:T(128)} %pad_add_fusion.info, f32[16,256]{1,0:T(8,128)} %convolution_bitcast_fusion.1.refs_0_, bf16[256,3072]{1,0:T(8,128)(2,1)} %fusion.4.refs_1_.refs_2_.refs_3_, bf16[256,3072]{1,0:T(8,128)(2,1)} %fusion.4.refs_1_.refs_2_.refs_3_, ...), custom_call_target="tpu_custom_call" | custom-call | tf_op jit(solution)/shard_map/attend_back/pallas_call | solution.py:153
  335.3 6.2 %multiply_reduce_fusion.7 = (f32[1024]{0:T(1024)S(1)}, f32[256]{0:T(256)S(1)}, bf16[256,1024]{1,0:T(8,128)(2,1)S(1)}, f32[256,1024]{1,0:T(8,128)}) fusion(bf16[1,2,128,1024]{3,2,1,0:T(8,128)(2,1)} %param.17, f32[256]{0:T(256)S(1)} %copy-done.44, f32[1024]{0:T(1024)S(1)} %bitcast.260, bf16[256,3072]{1,0:T(8,128)(2,1)} %get-tuple-element.43.refs_1_, ...), kind=kOutput, calls=%fused_computation.55 | convolution fusion | flops 1612970752 | bytes 9971712 | tf_op jit(solution)/shard_map/dot_general | solution.py:24
  350.1 3.0 copy-done.1
  354.9 11.6 %expert_in_gradient.1 = f32[2,1024,1408]{2,1,0:T(8,128)} custom-call(bf16[1280,1024]{1,0:T(8,128)(2,1)S(1)} %bitcast.213, bf16[2,1280,1408]{2,1,0:T(8,128)(2,1)S(1)} %bitcast.210), custom_call_target="tpu_custom_call" | custom-call | tf_op jit(solution)/shard_map/expert_in_gradient/pallas_call | solution.py:707
  366.5 6.5 %expert_out_gradient.1 = f32[1408,1024]{1,0:T(8,128)} custom-call(bf16[1280,1408]{1,0:T(8,128)(2,1)S(1)} %bitcast.211, bf16[1280,1024]{1,0:T(8,128)(2,1)S(1)} %bitcast.212), custom_call_target="tpu_custom_call" | custom-call | tf_op jit(solution)/shard_map/expert_out_gradient/pallas_call | solution.py:719
  374.2 2.7 maximum_bitcast_fusion.refs_0_
  377.0 71.8 %dense_gradients.1 = (f32[12,64,512]{2,1,0:T(8,128)}, f32[4,16,1024]{2,1,0:T(8,128)}) custom-call(bf16[4,512,512]{2,1,0:T(8,128)(2,1)} %maximum_bitcast_fusion.refs_0_, bf16[256,3072]{1,0:T(8,128)(2,1)} %get-tuple-element.43.refs_1_, bf16[256,1024]{1,0:T(8,128)(2,1)} %get-tuple-element.113.refs_2_, bf16[256,2048]{1,0:T(8,128)(2,1)} %maximum_select_fusion.refs_3_, ...), custom_call_target="tpu_custom_call" | custom-call | tf_op jit(solution)/shard_map/dense_gradients/pallas_call | solution.py:675
  (225 shorter events, 93.3 us)
Async XLA Ops:
  0.6 30.3 %copy-start = (bf16[1,1024,1024]{2,1,0:T(8,128)(2,1)S(1)}, bf16[1,1024,1024]{2,1,0:T(8,128)(2,1)}, u32[]{:S(2)}) copy-start(bf16[1,1024,1024]{2,1,0:T(8,128)(2,1)} %param.22) | copy-start | bytes 6291460
  33.0 64.7 %copy-start.5 = (f32[256,1024]{1,0:T(8,128)}, f32[256,1024]{1,0:T(8,128)S(1)}, u32[]{:S(2)}) copy-start(f32[256,1024]{1,0:T(8,128)S(1)} %get-tuple-element.137) | copy-start | bytes 3145732
  87.1 10.0 %copy-start.49 = (s32[2,2]{1,0:T(2,128)S(1)}, s32[2,2]{1,0:T(2,128)}, u32[]{:S(2)}) copy-start(s32[2,2]{1,0:T(2,128)} %param.19) | copy-start | bytes 52
  87.1 13.7 %collective-permute-start = (bf16[256,2048]{1,0:T(8,128)(2,1)}, bf16[256,2048]{1,0:T(8,128)(2,1)}, u32[]{:S(2)}, u32[]{:S(2)}) collective-permute-start(bf16[256,2048]{1,0:T(8,128)(2,1)} %convolution_convert_fusion), channel_id=1, source_target_pairs={{0,16},{1,17},{2,18},{3,19},{4,20},{5,21},{6,22},{7,23},{8,24},{9,... | collective-permute-start | bytes 3145736 | tf_op jit(solution)/shard_map/ppermute | solution.py:840
  142.3 22.0 %copy-start.35 = (f32[2,256]{1,0:T(2,128)S(1)}, f32[2,256]{1,0:T(2,128)}, u32[]{:S(2)}) copy-start(f32[2,256]{1,0:T(2,128)} %copy-done.34) | copy-start | bytes 6148
  157.6 73.7 %collective-permute-start.1 = (bf16[256,2048]{1,0:T(8,128)(2,1)}, bf16[256,2048]{1,0:T(8,128)(2,1)}, u32[]{:S(2)}, u32[]{:S(2)}) collective-permute-start(bf16[256,2048]{1,0:T(8,128)(2,1)} %get-tuple-element.37), channel_id=1, source_target_pairs={{16,0},{17,1},{18,2},{19,3},{20,4},{21,5},{22,6},{23,7},{24,8},{25... | collective-permute-start | bytes 3145736 | tf_op jit(solution)/shard_map/ppermute | solution.py:885
  171.7 63.4 %copy-start.6 = (f32[256,1024]{1,0:T(8,128)S(1)}, f32[256,1024]{1,0:T(8,128)}, u32[]{:S(2)}) copy-start(f32[256,1024]{1,0:T(8,128)} %copy-done.5) | copy-start | bytes 3145732
  171.7 63.4 %copy-start.9 = (f32[256,1024]{1,0:T(8,128)S(1)}, f32[256,1024]{1,0:T(8,128)}, u32[]{:S(2)}) copy-start(f32[256,1024]{1,0:T(8,128)} %copy-done.8) | copy-start | bytes 3145732
  171.7 63.4 %copy-start.31 = (bf16[256,1024]{1,0:T(8,128)(2,1)S(1)}, bf16[256,1024]{1,0:T(8,128)(2,1)}, u32[]{:S(2)}) copy-start(bf16[256,1024]{1,0:T(8,128)(2,1)} %get-tuple-element.36) | copy-start | bytes 1572868
  171.7 63.4 %copy-start.43 = (f32[256]{0:T(256)S(1)}, f32[256]{0:T(256)}, u32[]{:S(2)}) copy-start(f32[256]{0:T(256)} %copy-done.42) | copy-start | bytes 3076
  171.7 63.4 %copy-start.53 = (bf16[1,1024,2048]{2,1,0:T(8,128)(2,1)S(1)}, bf16[1,1024,2048]{2,1,0:T(8,128)(2,1)}, u32[]{:S(2)}) copy-start(bf16[1,1024,2048]{2,1,0:T(8,128)(2,1)} %param.23) | copy-start | bytes 12582916
  311.6 65.4 %collective-permute-start.4 = (bf16[256,1024]{1,0:T(8,128)(2,1)}, bf16[256,1024]{1,0:T(8,128)(2,1)}, u32[]{:S(2)}, u32[]{:S(2)}) collective-permute-start(bf16[256,1024]{1,0:T(8,128)(2,1)} %get-tuple-element.113.refs_2_), channel_id=1, source_target_pairs={{0,8},{8,0},{1,9},{9,1},{2,10},{10,2},{3,11},{11,3},{4,12},{12,4},... | collective-permute-start | bytes 1572872 | tf_op jit(solution)/shard_map/ppermute | solution.py:650
  314.2 20.0 %copy-start.48 = (s32[256]{0:T(256)S(1)}, s32[256]{0:T(256)}, u32[]{:S(2)}) copy-start(s32[256]{0:T(256)} %broadcast_select_fusion.3) | copy-start | bytes 3076
  314.2 21.1 %copy-start.44 = (f32[256]{0:T(256)S(1)}, f32[256]{0:T(256)}, u32[]{:S(2)}) copy-start(f32[256]{0:T(256)} %get-tuple-element.134) | copy-start | bytes 3076
  314.2 62.8 %collective-permute-start.5 = (bf16[256,2048]{1,0:T(8,128)(2,1)}, bf16[256,2048]{1,0:T(8,128)(2,1)}, u32[]{:S(2)}, u32[]{:S(2)}) collective-permute-start(bf16[256,2048]{1,0:T(8,128)(2,1)} %maximum_select_fusion.refs_3_), channel_id=1, source_target_pairs={{0,8},{8,0},{1,9},{9,1},{2,10},{10,2},{3,11},{11,3},{4,12},{12,4},... | collective-permute-start | bytes 3145736 | tf_op jit(solution)/shard_map/ppermute | solution.py:650
  335.2 41.7 %collective-permute-start.3 = (bf16[256,3072]{1,0:T(8,128)(2,1)}, bf16[256,3072]{1,0:T(8,128)(2,1)}, u32[]{:S(2)}, u32[]{:S(2)}) collective-permute-start(bf16[256,3072]{1,0:T(8,128)(2,1)} %get-tuple-element.43.refs_1_), channel_id=1, source_target_pairs={{0,8},{8,0},{1,9},{9,1},{2,10},{10,2},{3,11},{11,3},{4,12},{12,4},... | collective-permute-start | bytes 4718600 | tf_op jit(solution)/shard_map/ppermute | solution.py:650
  341.5 6.9 %copy-start.45 = (f32[1024]{0:T(1024)S(1)}, f32[1024]{0:T(1024)}, u32[]{:S(2)}) copy-start(f32[1024]{0:T(1024)} %get-tuple-element.133) | copy-start | bytes 12292
  341.5 6.9 %copy-start.47 = (f32[8]{0:T(128)S(1)}, f32[8]{0:T(128)}, u32[]{:S(2)}) copy-start(f32[8]{0:T(128)} %copy-done.46) | copy-start | bytes 100
  341.5 6.9 %copy-start.50 = (f32[8]{0:T(128)S(1)}, f32[8]{0:T(128)}, u32[]{:S(2)}) copy-start(f32[8]{0:T(128)} %sub.98) | copy-start | bytes 100
  346.4 27.8 %collective-permute-start.2 = (bf16[4,256,512]{1,2,0:T(8,128)(2,1)}, bf16[4,256,512]{1,2,0:T(8,128)(2,1)}, u32[]{:S(2)}, u32[]{:S(2)}) collective-permute-start(bf16[4,256,512]{1,2,0:T(8,128)(2,1)} %pad_maximum_fusion), channel_id=1, source_target_pairs={{0,8},{8,0},{1,9},{9,1},{2,10},{10,2},{3,11},{11,3},{4,12},{12,4},... | collective-permute-start | bytes 3145736 | tf_op jit(solution)/shard_map/ppermute | solution.py:650
  354.9 11.6 %copy-start.2 = (bf16[2,640,1408]{2,1,0:T(8,128)(2,1)S(1)}, bf16[2,640,1408]{2,1,0:T(8,128)(2,1)}, u32[]{:S(2)}) copy-start(bf16[2,640,1408]{2,1,0:T(8,128)(2,1)} %get-tuple-element.49) | copy-start | bytes 10813444
  354.9 11.6 %copy-start.3 = (bf16[2,8,80,1024]{3,2,1,0:T(8,128)(2,1)S(1)}, bf16[2,8,80,1024]{3,2,1,0:T(8,128)(2,1)}, u32[]{:S(2)}) copy-start(bf16[2,8,80,1024]{3,2,1,0:T(8,128)(2,1)} %get-tuple-element.50) | copy-start | bytes 7864324
  366.5 6.6 %copy-start.20 = (f32[256,1024]{1,0:T(8,128)S(1)}, f32[256,1024]{1,0:T(8,128)}, u32[]{:S(2)}) copy-start(f32[256,1024]{1,0:T(8,128)} %get-tuple-element.114) | copy-start | bytes 3145732
  366.5 6.6 %copy-start.28 = (f32[256,1024]{1,0:T(8,128)S(1)}, f32[256,1024]{1,0:T(8,128)}, u32[]{:S(2)}) copy-start(f32[256,1024]{1,0:T(8,128)} %get-tuple-element.150) | copy-start | bytes 3145732
  (36 other events, 91.3 us)
